TPU v7x, 128 devices: a whole 4x4x4 slice. The times are simulated.
128 devices in a mesh: context: 8 (over z_lo, y), expert: 16 (over z_hi, x, core).
Axes of the slice: x: 4, y: 4, z: 4 (z_hi: 2, z_lo: 2; z = z_hi * 2 + z_lo), core: 2. Of those that a mesh axis runs over, the one named last changes fastest.
Arguments:
- queries: bfloat16 [2, 1024, 4096], P(None, 'context', 'expert'), may hold values from -5 to 5
- keys: bfloat16 [2, 1024, 512], P(None, 'context'), may hold values from -5 to 5
- values: bfloat16 [2, 1024, 512], P(None, 'context'), may hold values from -8 to 8
- out_proj: bfloat16 [4096, 4096], P('expert'), may hold values from -0.09375 to 0.09375
- residual: bfloat16 [2, 1024, 4096], P(None, ('context', 'expert')), may hold values from -9 to 9
- norm_gain: float32 [4096], replicated, may hold values from 0.25 to 1.75
- w_in: bfloat16 [128, 4096, 1536], P(('context', 'expert')), may hold values from -0.09375 to 0.09375
- w_out: bfloat16 [128, 768, 4096], P(('context', 'expert')), may hold values from -0.15625 to 0.15625
- expert_ids: int32 [2, 1024, 8], P(None, ('context', 'expert')), may hold values from 0 to 63, as said below
- gate_weights: float32 [2, 1024, 8], P(None, ('context', 'expert')), may hold values from 0.02 to 0.25
Outputs:
- out: bfloat16 [2, 1024, 4096], P(None, ('context', 'expert'))
Inputs may be any that keep to these rules, and one draw needn't show every extreme that they name: `expert_ids`: each row names 8 different experts. In each micro-batch the 8 rows of one device (aligned blocks along the sequence) name no expert more than 2 times, and one expert is named exactly 2 times in every such block.
All inputs are finite; a program needn't handle non-finite values.
Results may differ from a plain program's by a relative error of at most 0.02.
Values may be sent and summed in bfloat16 or wider, within the bound.
No kernel may reach another device: no remote copies, remote signals or barrier semaphores. Data moves between devices by JAX's collectives and lax.ppermute only.
A program may use at most 128 MiB of HBM per device.

v0:
```python
import jax
import jax.numpy as jnp
from jax import lax
from jax.sharding import PartitionSpec as P

QH = 32
KVH = 4
HD = 128
BLOCK = 64


masked_score = -1e30


def folded_positions(first_row, row_count, context_size):
    stored = first_row + jnp.arange(row_count, dtype=jnp.int32)
    block_index = stored // BLOCK
    block_order = jnp.where(
        block_index % 2 == 0, block_index // 2, 2 * context_size - 1 - block_index // 2
    )
    return block_order * BLOCK + stored % BLOCK


def attention_step(query_heads, query_position, context_size, fold_state, key_values, first_row):
    running_max, running_sum, weighted = fold_state
    key_piece, value_piece = key_values
    key_position = folded_positions(first_row, key_piece.shape[1], context_size)
    allowed = (key_position[None, :] <= query_position[:, None])[None, None]
    scores = jnp.einsum(
        "mhqd,mkd->mhqk", query_heads, key_piece, preferred_element_type=jnp.float32
    ) * HD ** (-0.5)
    scores = jnp.where(allowed, scores, masked_score)
    new_max = jnp.maximum(running_max, jnp.max(scores, axis=-1))
    weights = jnp.where(allowed, jnp.exp(scores - new_max[..., None]), 0.0)
    running_sum = jnp.sum(weights, axis=-1)
    weighted = jnp.einsum(
        "mhqk,mkd->mhqd",
        weights.astype(jnp.bfloat16),
        value_piece,
        preferred_element_type=jnp.float32,
    )
    return (new_max, running_sum, weighted)


def empty_state(batch_count, heads_here, row_count):
    state_shape = (batch_count, heads_here, row_count)
    return (
        jnp.full(state_shape, masked_score, jnp.float32),
        jnp.zeros(state_shape, jnp.float32),
        jnp.zeros(state_shape + (HD,), jnp.float32),
    )


def normalize_heads(fold_state):
    running_max, running_sum, weighted = fold_state
    result = weighted / running_sum[..., None]
    batch_count, heads_here, row_count, head_size = result.shape
    return (
        result.transpose(0, 2, 1, 3)
        .reshape(batch_count, row_count, heads_here * head_size)
        .astype(jnp.bfloat16)
    )


def expert_rows(slot_rows, w_in, w_out):
    total_rows = slot_rows.shape[0] * slot_rows.shape[1]
    flattened = slot_rows.reshape(total_rows, slot_rows.shape[2])
    mixed = jnp.dot(flattened, w_in[0], preferred_element_type=jnp.float32)
    half_width = w_out.shape[1]
    hidden = (jax.nn.silu(mixed[:, :half_width]) * mixed[:, half_width:]).astype(jnp.bfloat16)
    partial_value = jnp.dot(hidden, w_out[0], preferred_element_type=jnp.float32).astype(
        jnp.bfloat16
    )
    return lax.optimization_barrier(partial_value).reshape(slot_rows.shape)


def expert_layer(attended, out_proj, residual_rows, norm_gain, w_in, w_out, id_rows, gate_rows):
    context_size = lax.axis_size("context")
    expert_size = lax.axis_size("expert")
    projected = lax.psum_scatter(
        jnp.dot(attended, out_proj, preferred_element_type=jnp.float32).astype(jnp.bfloat16),
        "expert",
        scatter_dimension=0,
        tiled=True,
    ).astype(jnp.float32)
    residual_sum = residual_rows.astype(jnp.float32) + projected
    scale_rows = lax.rsqrt(jnp.mean(residual_sum * residual_sum, axis=-1, keepdims=True) + 1e-06)
    normed = (residual_sum * scale_rows * norm_gain).astype(jnp.bfloat16)
    tokens, top_count = id_rows.shape
    model_width = normed.shape[1]
    device_count = context_size * expert_size
    experts_total = device_count // 2
    capacity = 2 * top_count * tokens // experts_total
    flattened = id_rows.reshape(-1)
    onehot = (flattened[:, None] == jnp.arange(experts_total, dtype=jnp.int32)[None, :]).astype(
        jnp.int32
    )
    slot_index = jnp.sum((jnp.cumsum(onehot, axis=0) - onehot) * onehot, axis=1)
    target = flattened * capacity + slot_index
    placing = (
        target.reshape(tokens, top_count)[None, :, :]
        == jnp.arange(experts_total * capacity, dtype=jnp.int32)[:, None, None]
    )
    placing = jnp.any(placing, axis=-1).astype(jnp.bfloat16)
    slot_rows = jnp.dot(placing, normed, preferred_element_type=jnp.float32).astype(jnp.bfloat16)
    grouped = slot_rows.reshape(context_size // 2, 1, expert_size, capacity, model_width)
    outgoing = jnp.broadcast_to(
        grouped, (context_size // 2, 2, expert_size, capacity, model_width)
    ).reshape(device_count, capacity, model_width)
    returned = lax.all_to_all(
        expert_rows(
            lax.all_to_all(
                outgoing, ("context", "expert"), split_axis=0, concat_axis=0, tiled=True
            ),
            w_in,
            w_out,
        ),
        ("context", "expert"),
        split_axis=0,
        concat_axis=0,
        tiled=True,
    )
    halves = returned.reshape(context_size // 2, 2, expert_size, capacity, model_width).astype(
        jnp.float32
    )
    expert_out = (
        (halves[:, 0] + halves[:, 1])
        .astype(jnp.bfloat16)
        .reshape(experts_total * capacity, model_width)
    )
    picked = expert_out[target].reshape(tokens, top_count, model_width).astype(jnp.float32)
    mixed_out = jnp.sum(picked * gate_rows[:, :, None], axis=1)
    return (residual_sum + mixed_out).astype(jnp.bfloat16)


def local(
    queries, keys, values, out_proj, residual, norm_gain, w_in, w_out, expert_ids, gate_weights
):
    batch_count = queries.shape[0]
    row_count = queries.shape[1]
    context_size = lax.axis_size("context")
    heads_here = QH // lax.axis_size("expert")
    kv_head = lax.axis_index("expert") * heads_here // (QH // KVH)
    key_columns = lax.dynamic_slice_in_dim(keys, kv_head * HD, HD, 2)
    value_columns = lax.dynamic_slice_in_dim(values, kv_head * HD, HD, 2)
    query_position = folded_positions(
        lax.axis_index("context") * row_count, row_count, context_size
    )
    query_heads = queries.reshape(batch_count, row_count, heads_here, HD).transpose(0, 2, 1, 3)
    results = []
    for batch_index in range(batch_count):
        fold_state = attention_step(
            query_heads[batch_index : batch_index + 1],
            query_position,
            context_size,
            empty_state(1, heads_here, row_count),
            (
                lax.all_gather(
                    key_columns[batch_index : batch_index + 1], "context", axis=1, tiled=True
                ),
                lax.all_gather(
                    value_columns[batch_index : batch_index + 1], "context", axis=1, tiled=True
                ),
            ),
            jnp.int32(0),
        )
        attended = normalize_heads(fold_state)[0]
        results.append(
            expert_layer(
                attended,
                out_proj,
                residual[batch_index],
                norm_gain,
                w_in,
                w_out,
                expert_ids[batch_index],
                gate_weights[batch_index],
            )
        )
    return jnp.stack(results)


def solution(mesh):
    placed = (
        P(None, "context", "expert"),
        P(None, "context", None),
        P(None, "context", None),
        P("expert", None),
        P(None, ("context", "expert"), None),
        P(),
        P(("context", "expert"), None, None),
        P(("context", "expert"), None, None),
        P(None, ("context", "expert"), None),
        P(None, ("context", "expert"), None),
    )
    return jax.shard_map(
        local,
        mesh=mesh,
        in_specs=placed,
        out_specs=P(None, ("context", "expert"), None),
        check_vma=False,
    )
```

profile of v0, /device:TPU:1, one launch (start us, length us, event | category | flops | bytes accessed | tf_op | source)
XLA Modules:
  0.0 409.7 jit_solution(578721511591974643)
XLA Ops:
  7.5 23.9 %all_gather.14 = bf16[1,1024,128]{2,1,0:T(8,128)(2,1)S(1)} all-gather(bf16[1,128,128]{2,1,0:T(8,128)(2,1)S(1)} %get-tuple-element.12), channel_id=1, replica_groups=mesh['context'=8,'expert'=16] {'context'}, dimensions={1}, use_global_device_ids=true | all-gather | bytes 294912 | tf_op jit(solution)/shard_map/all_gather | solution.py:158
  34.1 22.0 %all_gather.12 = bf16[1,1024,128]{2,1,0:T(8,128)(2,1)S(1)} all-gather(bf16[1,128,128]{2,1,0:T(8,128)(2,1)S(1)} %get-tuple-element.11), channel_id=1, replica_groups=mesh['context'=8,'expert'=16] {'context'}, dimensions={1}, use_global_device_ids=true | all-gather | bytes 294912 | tf_op jit(solution)/shard_map/all_gather | solution.py:158
  57.4 20.2 %all_gather.15 = bf16[1,1024,128]{1,2,0:T(8,128)(2,1)S(1)} all-gather(bf16[1,128,128]{1,2,0:T(8,128)(2,1)S(1)} %copy.42), channel_id=1, replica_groups=mesh['context'=8,'expert'=16] {'context'}, dimensions={1}, use_global_device_ids=true | all-gather | bytes 294912 | tf_op jit(solution)/shard_map/all_gather | solution.py:161
  81.3 19.5 %all_gather.13 = bf16[1,1024,128]{1,2,0:T(8,128)(2,1)S(1)} all-gather(bf16[1,128,128]{1,2,0:T(8,128)(2,1)S(1)} %copy.39), channel_id=1, replica_groups=mesh['context'=8,'expert'=16] {'context'}, dimensions={1}, use_global_device_ids=true | all-gather | bytes 294912 | tf_op jit(solution)/shard_map/all_gather | solution.py:161
  103.8 59.5 %reduce-scatter.5.cloned.1.call-done = bf16[8,4096]{1,0:T(8,128)(2,1)} async-done(((bf16[128,4096]{1,0:T(8,128)(2,1)}), bf16[8,4096]{1,0:T(8,128)(2,1)}) %reduce-scatter.5.cloned.1.call-update) | async-done | bytes 65552 | tf_op jit(solution)/shard_map/reduce_scatter | solution.py:80
  163.3 70.1 %reduce-scatter.3.cloned.1.call-done = bf16[8,4096]{1,0:T(8,128)(2,1)} async-done(((bf16[128,4096]{1,0:T(8,128)(2,1)}), bf16[8,4096]{1,0:T(8,128)(2,1)}) %reduce-scatter.3.cloned.1.call-update) | async-done | bytes 65552 | tf_op jit(solution)/shard_map/reduce_scatter | solution.py:80
  236.6 3.9 broadcast_in_dim.66
  240.4 9.2 %all-to-all-start.2 = ((bf16[128,2,4096]{2,1,0:T(2,128)(2,1)}), bf16[128,2,4096]{2,1,0:T(2,128)(2,1)S(1)}, u32[]{:S(2)}, u32[]{:S(2)}) async-start(bf16[128,2,4096]{2,1,0:T(2,128)(2,1)} %bitcast.149), calls=%async_computation.4 | async-start | bytes 4194304 | tf_op jit(solution)/shard_map/all_to_all | solution.py:112
  252.9 27.0 %all-to-all-done.2 = bf16[128,2,4096]{2,1,0:T(2,128)(2,1)S(1)} async-done(((bf16[128,2,4096]{2,1,0:T(2,128)(2,1)}), bf16[128,2,4096]{2,1,0:T(2,128)(2,1)S(1)}, u32[]{:S(2)}, u32[]{:S(2)}) %all-to-all-start.2) | async-done | bytes 2097184 | tf_op jit(solution)/shard_map/all_to_all | solution.py:112
  279.9 3.8 broadcast_in_dim.64
  283.7 5.7 %all-to-all-start = ((bf16[128,2,4096]{2,1,0:T(2,128)(2,1)}), bf16[128,2,4096]{2,1,0:T(2,128)(2,1)}, u32[]{:S(2)}, u32[]{:S(2)}) async-start(bf16[128,2,4096]{2,1,0:T(2,128)(2,1)} %bitcast.150), calls=%async_computation.1 | async-start | bytes 4194304 | tf_op jit(solution)/shard_map/all_to_all | solution.py:112
  291.7 7.0 %fusion = f32[256,1536]{1,0:T(8,128)S(1)} fusion(bf16[256,4096]{1,0:T(8,128)(2,1)} %reshape.364, bf16[1,4096,1536]{2,1,0:T(8,128)(2,1)} %param.16), kind=kOutput, calls=%fused_computation.2 | convolution fusion | flops 3221225472 | bytes 16252928 | tf_op jit(solution)/shard_map/dot_general | solution.py:68
  298.7 4.6 %fusion.11 = bf16[256,4096]{1,0:T(8,128)(2,1)S(1)} fusion(bf16[1,768,4096]{2,1,0:T(8,128)(2,1)} %param.17, f32[256,1536]{1,0:T(8,128)S(1)} %fusion), kind=kOutput, calls=%fused_computation.11 | convolution fusion | flops 1612840960 | bytes 9961472 | tf_op jit(solution)/shard_map/dot_general | solution.py:71
  303.3 2.7 reshape.365
  306.0 13.5 %all-to-all-done = bf16[128,2,4096]{2,1,0:T(2,128)(2,1)} async-done(((bf16[128,2,4096]{2,1,0:T(2,128)(2,1)}), bf16[128,2,4096]{2,1,0:T(2,128)(2,1)}, u32[]{:S(2)}, u32[]{:S(2)}) %all-to-all-start) | async-done | bytes 2097184 | tf_op jit(solution)/shard_map/all_to_all | solution.py:112
  319.5 4.7 %all-to-all-start.3 = ((bf16[128,2,4096]{2,1,0:T(2,128)(2,1)}), bf16[128,2,4096]{2,1,0:T(2,128)(2,1)S(1)}, u32[]{:S(2)}, u32[]{:S(2)}) async-start(bf16[128,2,4096]{2,1,0:T(2,128)(2,1)} %reshape.365), calls=%async_computation.5 | async-start | bytes 4194304 | tf_op jit(solution)/shard_map/all_to_all | solution.py:110
  324.1 4.1 %reshape.358 = bf16[256,4096]{1,0:T(8,128)(2,1)} reshape(bf16[128,2,4096]{2,1,0:T(2,128)(2,1)} %all-to-all-done) | data formatting | bytes 4194304 | tf_op jit(solution)/shard_map/reshape | solution.py:67
  328.3 7.0 %fusion.2 = f32[256,1536]{1,0:T(8,128)S(1)} fusion(bf16[256,4096]{1,0:T(8,128)(2,1)} %reshape.358, bf16[1,4096,1536]{2,1,0:T(8,128)(2,1)} %param.16), kind=kOutput, calls=%fused_computation.4 | convolution fusion | flops 3221225472 | bytes 16252928 | tf_op jit(solution)/shard_map/dot_general | solution.py:68
  335.3 6.0 %fusion.8 = bf16[256,4096]{1,0:T(8,128)(2,1)} fusion(bf16[1,768,4096]{2,1,0:T(8,128)(2,1)} %param.17, f32[256,1536]{1,0:T(8,128)S(1)} %fusion.2), kind=kOutput, calls=%fused_computation.10 | convolution fusion | flops 1612840960 | bytes 9961472 | tf_op jit(solution)/shard_map/dot_general | solution.py:71
  341.3 4.4 %reshape.359 = bf16[128,2,4096]{2,1,0:T(2,128)(2,1)} reshape(bf16[256,4096]{1,0:T(8,128)(2,1)} %fusion.8) | data formatting | bytes 4194304 | tf_op jit(solution)/shard_map/reshape | solution.py:74
  345.7 8.9 %all-to-all-done.3 = bf16[128,2,4096]{2,1,0:T(2,128)(2,1)S(1)} async-done(((bf16[128,2,4096]{2,1,0:T(2,128)(2,1)}), bf16[128,2,4096]{2,1,0:T(2,128)(2,1)S(1)}, u32[]{:S(2)}, u32[]{:S(2)}) %all-to-all-start.3) | async-done | bytes 2097184 | tf_op jit(solution)/shard_map/all_to_all | solution.py:110
  354.6 5.7 %all-to-all-start.1 = ((bf16[128,2,4096]{2,1,0:T(2,128)(2,1)}), bf16[128,2,4096]{2,1,0:T(2,128)(2,1)}, u32[]{:S(2)}, u32[]{:S(2)}) async-start(bf16[128,2,4096]{2,1,0:T(2,128)(2,1)} %reshape.359), calls=%async_computation.2 | async-start | bytes 4194304 | tf_op jit(solution)/shard_map/all_to_all | solution.py:110
  364.2 26.1 %all-to-all-done.1 = bf16[128,2,4096]{2,1,0:T(2,128)(2,1)} async-done(((bf16[128,2,4096]{2,1,0:T(2,128)(2,1)}), bf16[128,2,4096]{2,1,0:T(2,128)(2,1)}, u32[]{:S(2)}, u32[]{:S(2)}) %all-to-all-start.1) | async-done | bytes 2097184 | tf_op jit(solution)/shard_map/all_to_all | solution.py:110
  390.4 3.6 convert.6
  (78 shorter events, 32.9 us)
Async XLA Ops:
  6.5 73.1 %copy-start = (bf16[256,4096]{1,0:T(8,128)(2,1)S(1)}, bf16[256,4096]{1,0:T(8,128)(2,1)}, u32[]{:S(2)}) copy-start(bf16[256,4096]{1,0:T(8,128)(2,1)} %param.13) | copy-start | bytes 6291460
  6.5 156.8 %reduce-scatter.5.cloned.1.call-start = ((), (), s32[]{:S(2)}) async-start(), calls=%async_computation.7 | async-start | bytes 1114112 | tf_op jit(solution)/shard_map/reduce_scatter | solution.py:80
  57.4 21.8 %copy-start.2 = (f32[2,128,1024]{1,2,0:T(8,128)S(1)}, f32[2,128,1024]{1,2,0:T(8,128)}, u32[]{:S(2)}) copy-start(f32[2,128,1024]{1,2,0:T(8,128)} %get-tuple-element.26) | copy-start | bytes 3145732
  81.1 152.3 %reduce-scatter.3.cloned.1.call-start = ((), (), s32[]{:S(2)}) async-start(), calls=%async_computation.6 | async-start | bytes 1114112 | tf_op jit(solution)/shard_map/reduce_scatter | solution.py:80
  101.1 1.6 copy-start.7
  101.1 132.3 %copy-start.3 = (bf16[2,8,4096]{2,1,0:T(8,128)(2,1)S(1)}, bf16[2,8,4096]{2,1,0:T(8,128)(2,1)}, u32[]{:S(2)}) copy-start(bf16[2,8,4096]{2,1,0:T(8,128)(2,1)} %param.14) | copy-start | bytes 393220
  101.1 133.4 %copy-start.6 = (f32[4096]{0:T(1024)S(1)}, f32[4096]{0:T(1024)}, u32[]{:S(2)}) copy-start(f32[4096]{0:T(1024)} %param.15) | copy-start | bytes 49156
  240.4 9.3 %copy-start.5 = (bf16[8,4096]{1,0:T(8,128)(2,1)S(1)}, bf16[8,4096]{1,0:T(8,128)(2,1)}, u32[]{:S(2)}) copy-start(bf16[8,4096]{1,0:T(8,128)(2,1)} %reduce-scatter.3.cloned.1.call-done) | copy-start | bytes 196612
  240.4 39.5 %all-to-all-start.2 = ((bf16[128,2,4096]{2,1,0:T(2,128)(2,1)}), bf16[128,2,4096]{2,1,0:T(2,128)(2,1)S(1)}, u32[]{:S(2)}, u32[]{:S(2)}) async-start(bf16[128,2,4096]{2,1,0:T(2,128)(2,1)} %bitcast.149), calls=%async_computation.4 | async-start | bytes 4194304 | tf_op jit(solution)/shard_map/all_to_all | solution.py:112
  283.7 35.8 %all-to-all-start = ((bf16[128,2,4096]{2,1,0:T(2,128)(2,1)}), bf16[128,2,4096]{2,1,0:T(2,128)(2,1)}, u32[]{:S(2)}, u32[]{:S(2)}) async-start(bf16[128,2,4096]{2,1,0:T(2,128)(2,1)} %bitcast.150), calls=%async_computation.1 | async-start | bytes 4194304 | tf_op jit(solution)/shard_map/all_to_all | solution.py:112
  319.5 35.1 %all-to-all-start.3 = ((bf16[128,2,4096]{2,1,0:T(2,128)(2,1)}), bf16[128,2,4096]{2,1,0:T(2,128)(2,1)S(1)}, u32[]{:S(2)}, u32[]{:S(2)}) async-start(bf16[128,2,4096]{2,1,0:T(2,128)(2,1)} %reshape.365), calls=%async_computation.5 | async-start | bytes 4194304 | tf_op jit(solution)/shard_map/all_to_all | solution.py:110
  345.7 14.8 %copy-start.8 = (f32[2,8,8]{2,1,0:T(8,128)S(1)}, f32[2,8,8]{2,1,0:T(8,128)}, u32[]{:S(2)}) copy-start(f32[2,8,8]{2,1,0:T(8,128)} %param.19) | copy-start | bytes 1540
  354.6 35.8 %all-to-all-start.1 = ((bf16[128,2,4096]{2,1,0:T(2,128)(2,1)}), bf16[128,2,4096]{2,1,0:T(2,128)(2,1)}, u32[]{:S(2)}, u32[]{:S(2)}) async-start(bf16[128,2,4096]{2,1,0:T(2,128)(2,1)} %reshape.359), calls=%async_computation.2 | async-start | bytes 4194304 | tf_op jit(solution)/shard_map/all_to_all | solution.py:110
  397.3 5.5 %copy-start.1 = (bf16[256,4096]{1,0:T(8,128)(2,1)S(1)}, bf16[256,4096]{1,0:T(8,128)(2,1)}, u32[]{:S(2)}) copy-start(bf16[256,4096]{1,0:T(8,128)(2,1)} %param.13) | copy-start | bytes 6291460
  398.9 3.2 copy-start.4
Sparse Core Ops, SparseCore 0:
  81.2 82.0 reduce-scatter.4
  167.6 65.7 reduce-scatter.2
where the time goes:
time: 411 us; the launch traced here: 410 us
  waiting for transfers between devices  205 us (50%)
  blocking collectives  85.6 us (21%)
  matrix products  32.8 us (8%)
  local copies, waits for them, and re-layouts  31.4 us (8%)
  starting transfers between devices  25.3 us (6%)
  other arithmetic  15.7 us (4%)
  between operations  13.8 us (3%)
    reduce_scatter x2, waiting for transfers between devices, expert_layer(): lax.psum_scatter(jnp.dot(attended, out_proj, preferred_element_type=jnp.f...  130 us
    all_gather x2, blocking collectives, local(): lax.all_gather(key_columns[batch_index:batch_index + 1], 'context', axis=...  45.9 us
    all_to_all x2, waiting for transfers between devices, expert_layer(): lax.all_to_all(outgoing, ('context', 'expert'), split_axis=0, concat_axis...  40.4 us
    all_gather x2, blocking collectives, local(): lax.all_gather(value_columns[batch_index:batch_index + 1], 'context', axi...  39.7 us
    all_to_all x2, waiting for transfers between devices, expert_layer(): lax.all_to_all(expert_rows(lax.all_to_all(outgoing, ('context', 'expert')...  35 us
    all_to_all x2, starting transfers between devices, expert_layer(): lax.all_to_all(outgoing, ('context', 'expert'), split_axis=0, concat_axis...  14.9 us
    dot_general x2, matrix products, expert_rows(): mixed = jnp.dot(flattened, w_in[0], preferred_element_type=jnp.float32)  14 us
    dot_general x2, matrix products, expert_rows(): jnp.dot(hidden, w_out[0], preferred_element_type=jnp.float32)  10.6 us
  transfers between devices with their start and end apart: 6, of which 6 were waited for; matrix products, arithmetic and copies ran while one was open for 12% of the time, Pallas kernels for 0%

commit v1 on v0

v1 whole, which is shorter than its diff:
```python
import jax
import jax.numpy as jnp
from jax import lax
from jax.sharding import Mesh, PartitionSpec as P

QH = 32
KVH = 4
HD = 128
BLOCK = 64
masked_score = -1e30

CONTEXT = ("zl", "y")
COLUMN = ("zh", "x")
CHIPS = ("zl", "y", "zh", "x")
SWAP = [(0, 1), (1, 0)]


def swap_cores(value):
    return lax.ppermute(value, "core", SWAP)


def folded_positions(first_row, row_count, context_size):
    stored = first_row + jnp.arange(row_count, dtype=jnp.int32)
    block_index = stored // BLOCK
    block_order = jnp.where(
        block_index % 2 == 0, block_index // 2, 2 * context_size - 1 - block_index // 2
    )
    return block_order * BLOCK + stored % BLOCK


def attend(query_heads, keys, values, query_position, key_position):
    allowed = (key_position[None, :] <= query_position[:, None])[None]
    scores = jnp.einsum(
        "hqd,kd->hqk", query_heads, keys, preferred_element_type=jnp.float32
    ) * HD ** (-0.5)
    scores = jnp.where(allowed, scores, masked_score)
    largest = jnp.max(scores, axis=-1, keepdims=True)
    weights = jnp.exp(scores - largest)
    total = jnp.sum(weights, axis=-1, keepdims=True)
    weighted = jnp.einsum(
        "hqk,kd->qhd", weights.astype(jnp.bfloat16), values, preferred_element_type=jnp.float32
    )
    return (weighted / total.transpose(1, 0, 2)).astype(jnp.bfloat16)


def local(
    queries, keys, values, out_proj, residual, norm_gain, w_in, w_out, expert_ids, gate_weights
):
    batch_count, row_count, feature_count = queries.shape
    token_rows, top_count = expert_ids.shape[1:]
    model_width = out_proj.shape[1]
    context_size = lax.axis_size(CONTEXT)
    column_size = lax.axis_size(COLUMN)
    chip_count = context_size * column_size
    core = lax.axis_index("core")
    heads_here = feature_count // HD
    chip_rows = 2 * token_rows

    def of_batch(value, index):
        return lax.dynamic_index_in_dim(value, index, 0, keepdims=False)

    other_queries = swap_cores(of_batch(queries, 1 - core))
    other_proj = swap_cores(out_proj)
    other_residual = swap_cores(of_batch(residual, 1 - core))
    other_ids = swap_cores(expert_ids)
    other_gates = swap_cores(gate_weights)

    def in_core_order(own, other, axis):
        stacked = jnp.stack([own, other], axis=axis)
        flipped = jnp.stack([other, own], axis=axis)
        return jnp.where(core == 0, stacked, flipped)

    kv_head = lax.axis_index(COLUMN) * 2 * heads_here // (QH // KVH)
    pair = jnp.stack([of_batch(keys, core), of_batch(values, core)])
    pair = lax.dynamic_slice_in_dim(pair, kv_head * HD, HD, 2)
    gathered = lax.all_to_all(
        jnp.broadcast_to(pair[None], (context_size,) + pair.shape), CONTEXT, 0, 0
    )
    all_keys = gathered[:, 0].reshape(context_size * row_count, HD)
    all_values = gathered[:, 1].reshape(context_size * row_count, HD)
    query_rows = jnp.concatenate([of_batch(queries, core), other_queries], axis=1)
    query_heads = query_rows.reshape(row_count, 2 * heads_here, HD).transpose(1, 0, 2)
    attended = attend(
        query_heads,
        all_keys,
        all_values,
        folded_positions(lax.axis_index(CONTEXT) * row_count, row_count, context_size),
        folded_positions(0, context_size * row_count, context_size),
    ).reshape(row_count, 2 * feature_count)
    projected = jnp.dot(
        attended,
        jnp.concatenate([out_proj, other_proj], axis=0),
        preferred_element_type=jnp.float32,
    ).astype(jnp.bfloat16)
    pieces = lax.all_to_all(
        projected.reshape(column_size, chip_rows, model_width), COLUMN, 0, 0
    )
    residual_rows = in_core_order(of_batch(residual, core), other_residual, 0)
    residual_sum = residual_rows.reshape(chip_rows, model_width).astype(jnp.float32) + jnp.sum(
        pieces.astype(jnp.float32), axis=0
    )
    scale_rows = lax.rsqrt(jnp.mean(residual_sum * residual_sum, axis=-1, keepdims=True) + 1e-06)
    normed = (residual_sum * scale_rows * norm_gain).astype(jnp.bfloat16)
    tokens = batch_count * chip_rows
    all_normed = in_core_order(normed, swap_cores(normed), 0).reshape(tokens, model_width)

    ids = in_core_order(expert_ids, other_ids, 1)
    gates = in_core_order(gate_weights, other_gates, 1).reshape(tokens, top_count)
    experts_total = chip_count
    onehot = (
        ids.reshape(batch_count * 2, token_rows * top_count)[:, :, None]
        == jnp.arange(experts_total, dtype=jnp.int32)
    ).astype(jnp.int32)
    slot_index = jnp.sum((jnp.cumsum(onehot, axis=1) - onehot) * onehot, axis=2)
    flat = ids.reshape(batch_count * 2, token_rows * top_count)
    block_index = jnp.arange(batch_count * 2, dtype=jnp.int32)[:, None]
    slots = batch_count * 2 * 2
    target = jnp.where(
        flat % 2 == core, (flat // 2) * slots + block_index * 2 + slot_index, -1
    ).reshape(tokens, top_count)
    slot_rows = experts_total // 2 * slots
    matches = target[None] == jnp.arange(slot_rows, dtype=jnp.int32)[:, None, None]
    gate_matrix = jnp.sum(jnp.where(matches, gates[None], 0.0), axis=2)
    placing = jnp.any(matches, axis=2).astype(jnp.bfloat16)

    def both_halves(matrix):
        grouped = matrix.reshape(context_size // 2, 1, slot_rows // (context_size // 2), tokens)
        return jnp.broadcast_to(
            grouped, (grouped.shape[0], 2, grouped.shape[2], tokens)
        ).reshape(2 * slot_rows, tokens)

    outgoing = jnp.dot(
        both_halves(placing), all_normed, preferred_element_type=jnp.float32
    ).astype(jnp.bfloat16)
    received = lax.all_to_all(
        outgoing.reshape(chip_count, slots, model_width), CHIPS, 0, 0
    ).reshape(chip_count * slots, model_width)
    mixed = jnp.dot(received, w_in[0], preferred_element_type=jnp.float32)
    half_width = w_out.shape[1]
    hidden = (jax.nn.silu(mixed[:, :half_width]) * mixed[:, half_width:]).astype(jnp.bfloat16)
    partial_value = jnp.dot(hidden, w_out[0], preferred_element_type=jnp.float32).astype(
        jnp.bfloat16
    )
    returned = lax.all_to_all(
        partial_value.reshape(chip_count, slots, model_width), CHIPS, 0, 0
    ).reshape(chip_count * slots, model_width)
    gate_high = gate_matrix.astype(jnp.bfloat16)
    gate_low = (gate_matrix - gate_high.astype(jnp.float32)).astype(jnp.bfloat16)
    both = jnp.concatenate([both_halves(gate_high), both_halves(gate_low)], axis=1)
    summed = lax.dot_general(
        both, returned, (((0,), (0,)), ((), ())), preferred_element_type=jnp.float32
    )
    mixed_out = (summed[:tokens] + summed[tokens:]).reshape(
        batch_count, 2, token_rows, model_width
    )
    own_sum = jnp.where(
        (jnp.arange(batch_count) == core)[:, None, None, None],
        residual_sum.reshape(1, 2, token_rows, model_width),
        0.0,
    )
    total = mixed_out + own_sum
    kept = lax.dynamic_index_in_dim(total, core, 1, keepdims=False)
    sent = lax.dynamic_index_in_dim(total, 1 - core, 1, keepdims=False)
    return (kept + swap_cores(sent)).astype(jnp.bfloat16)


def solution(mesh):
    chips = Mesh(mesh.devices.reshape(2, 4, 2, 4, 2), ("zl", "y", "zh", "x", "core"))
    expert = ("zh", "x", "core")
    every = CONTEXT + expert
    placed = (
        P(None, CONTEXT, expert),
        P(None, CONTEXT, None),
        P(None, CONTEXT, None),
        P(expert, None),
        P(None, every, None),
        P(),
        P(every, None, None),
        P(every, None, None),
        P(None, every, None),
        P(None, every, None),
    )
    return jax.shard_map(
        local,
        mesh=chips,
        in_specs=placed,
        out_specs=P(None, every, None),
        check_vma=False,
    )
```

time: 411 us -> 191 us (0.46)
  waiting for transfers between devices: 205 us -> 74.9 us
  blocking collectives: 85.6 us -> 54.6 us
  local copies, waits for them, and re-layouts: 31.4 us -> 4.46 us
  between operations: 13.8 us -> 0.32 us
  other arithmetic: 15.7 us -> 3.07 us
  matrix products: 32.8 us -> 21.8 us
  starting transfers between devices: 25.3 us -> 30.3 us
    reduce_scatter x2 -> x0, waiting for transfers between devices: 130 us -> none  [expert_layer(): lax.psum_scatter(jnp.dot(attended, out_proj, preferred_element_type=jnp.f...]
    all_gather x4 -> x0, blocking collectives: 85.6 us -> none  [the longest x2 45.9 us: local(): lax.all_gather(key_columns[batch_index:batch_index + 1], 'context', axis=...]
    all_to_all x0 -> x1, blocking collectives: none -> 54.6 us  [local(): lax.all_to_all(outgoing.reshape(chip_count, slots, model_width), CHIPS, 0...]
    reshape x5 -> x0, local copies, waits for them, and re-layouts: 13.6 us -> none  [the longest x2 7.06 us: expert_rows(): return lax.optimization_barrier(partial_value).reshape(slot_rows.shape)]
    dot_general x12 -> x7, matrix products: 32.8 us -> 21.8 us  [the longest x1 9.35 us: local(): mixed = jnp.dot(received, w_in[0], preferred_element_type=jnp.float32)]
    broadcast_in_dim x4, local copies, waits for them, and re-layouts: 10.1 us -> 0.94 us  [the longest x1 0.89 us: local(): jnp.broadcast_to(pair[None], (context_size,) + pair.shape)]
    ppermute x0 -> x7, starting transfers between devices: none -> 8.67 us  [swap_cores(): return lax.ppermute(value, 'core', SWAP)]
    convert_element_type x6, other arithmetic: 8.19 us -> 1 us  [the longest x1 0.68 us: local(): return (kept + swap_cores(sent)).astype(jnp.bfloat16)]
  transfers between devices with their start and end apart: 6 -> 10, of which waited for: 6 -> 8; matrix products, arithmetic and copies ran while one was open for 12% -> 4% of each run, Pallas kernels for 0% -> 0%
where the time goes in v1:
time: 191 us; the launch traced here: 189 us
  waiting for transfers between devices  74.9 us (39%)
  blocking collectives  54.6 us (29%)
  starting transfers between devices  30.3 us (16%)
  matrix products  21.8 us (11%)
  local copies, waits for them, and re-layouts  4.46 us (2%)
  other arithmetic  3.07 us (2%)
    all_to_all x1, blocking collectives, local(): lax.all_to_all(outgoing.reshape(chip_count, slots, model_width), CHIPS, 0...  54.6 us
    all_to_all x1, waiting for transfers between devices, local(): lax.all_to_all(partial_value.reshape(chip_count, slots, model_width), CHI...  48.2 us
    all_to_all x1, waiting for transfers between devices, local(): lax.all_to_all(projected.reshape(column_size, chip_rows, model_width), CO...  13.7 us
    dot_general x1, matrix products, local(): mixed = jnp.dot(received, w_in[0], preferred_element_type=jnp.float32)  9.35 us
    all_to_all x1, starting transfers between devices, local(): lax.all_to_all(partial_value.reshape(chip_count, slots, model_width), CHI...  8.82 us
    all_to_all x1, waiting for transfers between devices, local(): lax.all_to_all(jnp.broadcast_to(pair[None], (context_size,) + pair.shape)...  8.68 us
    ppermute x7, starting transfers between devices, swap_cores(): return lax.ppermute(value, 'core', SWAP)  8.67 us
    all_to_all x1, starting transfers between devices, local(): lax.all_to_all(projected.reshape(column_size, chip_rows, model_width), CO...  7.17 us
  transfers between devices with their start and end apart: 10, of which 8 were waited for; matrix products, arithmetic and copies ran while one was open for 4% of the time, Pallas kernels for 0%

profile of v1, /device:TPU:1, one launch (start us, length us, event | category | flops | bytes accessed | tf_op | source)
XLA Modules:
  0.0 189.4 jit_solution(3554464585488929888)
XLA Ops:
  0.0 1.4 collective-permute-start.4
  1.4 1.0 constant_dynamic-slice_fusion.2
  2.4 0.9 broadcast_in_dim.85
  3.3 5.6 %all-to-all-start = ((bf16[8,2,128,128]{3,2,1,0:T(8,128)(2,1)}), bf16[8,2,128,128]{3,2,1,0:T(8,128)(2,1)S(1)}, u32[]{:S(2)}, u32[]{:S(2)}) async-start(bf16[8,2,128,128]{3,2,1,0:T(8,128)(2,1)} %broadcast_in_dim.85), calls=%async_computation | async-start | bytes 1048576 | tf_op jit(solution)/shard_map/all_to_all | solution.py:76
  10.6 8.7 %all-to-all-done = bf16[8,2,128,128]{3,2,1,0:T(8,128)(2,1)S(1)} async-done(((bf16[8,2,128,128]{3,2,1,0:T(8,128)(2,1)}), bf16[8,2,128,128]{3,2,1,0:T(8,128)(2,1)S(1)}, u32[]{:S(2)}, u32[]{:S(2)}) %all-to-all-start) | async-done | bytes 524320 | tf_op jit(solution)/shard_map/all_to_all | solution.py:76
  21.2 0.9 copy-done.5
  22.1 1.7 convolution_convert_fusion.1
  23.8 7.2 %all-to-all-start.1 = ((bf16[8,16,4096]{2,1,0:T(8,128)(2,1)}), bf16[8,16,4096]{2,1,0:T(8,128)(2,1)S(1)}, u32[]{:S(2)}, u32[]{:S(2)}) async-start(bf16[8,16,4096]{2,1,0:T(8,128)(2,1)} %bitcast.25), calls=%async_computation.1 | async-start | bytes 2097152 | tf_op jit(solution)/shard_map/all_to_all | solution.py:95
  31.0 1.1 collective-permute-start.2
  32.4 0.9 collective-permute-done
  34.6 13.7 %all-to-all-done.1 = bf16[8,16,4096]{2,1,0:T(8,128)(2,1)S(1)} async-done(((bf16[8,16,4096]{2,1,0:T(8,128)(2,1)}), bf16[8,16,4096]{2,1,0:T(8,128)(2,1)S(1)}, u32[]{:S(2)}, u32[]{:S(2)}) %all-to-all-start.1) | async-done | bytes 1048608 | tf_op jit(solution)/shard_map/all_to_all | solution.py:95
  48.7 0.9 collective-permute-start.5
  49.8 0.9 collective-permute-done.5
  50.7 1.2 fusion.7
  51.9 54.6 %all_to_all.20 = bf16[64,8,4096]{2,1,0:T(8,128)(2,1)S(1)} all-to-all(bf16[64,8,4096]{2,1,0:T(8,128)(2,1)S(1)} %fusion.7), channel_id=1, replica_groups=mesh['zl'=2,'y'=4,'zh'=2,'x'=4,'core'=2] {'zl','y','zh','x'}, dimensions={0} | all-to-all | bytes 8388608 | tf_op jit(solution)/shard_map/all_to_all | solution.py:135
  106.5 9.3 %fusion = f32[512,1536]{1,0:T(8,128)S(1)} fusion(bf16[1,4096,1536]{2,1,0:T(8,128)(2,1)} %param.16, bf16[64,8,4096]{2,1,0:T(8,128)(2,1)S(1)} %all_to_all.20), kind=kOutput, calls=%fused_computation | convolution fusion | flops 6442450944 | bytes 19922944 | tf_op jit(solution)/shard_map/dot_general | solution.py:138
  115.9 5.1 %fusion.8 = bf16[64,8,4096]{2,1,0:T(8,128)(2,1)} fusion(bf16[1,768,4096]{2,1,0:T(8,128)(2,1)S(1)} %bitcast.125, f32[512,1536]{1,0:T(8,128)S(1)} %fusion), kind=kOutput, calls=%fused_computation.7 | convolution fusion | flops 3225681920 | bytes 13631488 | tf_op jit(solution)/shard_map/dot_general | solution.py:141
  121.0 8.8 %all-to-all-start.3 = ((bf16[64,8,4096]{2,1,0:T(8,128)(2,1)}), bf16[64,8,4096]{2,1,0:T(8,128)(2,1)}, u32[]{:S(2)}, u32[]{:S(2)}) async-start(bf16[64,8,4096]{2,1,0:T(8,128)(2,1)} %fusion.8), calls=%async_computation.3 | async-start | bytes 8388608 | tf_op jit(solution)/shard_map/all_to_all | solution.py:144
  129.8 2.0 %collective-permute-start.1 = (f32[2,8,8]{2,1,0:T(8,128)S(1)}, f32[2,8,8]{2,1,0:T(8,128)S(1)}, u32[]{:S(2)}, u32[]{:S(2)}) collective-permute-start(f32[2,8,8]{2,1,0:T(8,128)S(1)} %copy-done.4), channel_id=1, source_target_pairs={{0,1},{1,0},{2,3},{3,2},{4,5},{5,4},{6,7},{7,6},{8,9},{9,8},{10,11... | collective-permute-start | bytes 1544 | tf_op jit(solution)/shard_map/ppermute | solution.py:19
  131.8 0.8 collective-permute-done.1
  133.2 48.2 %all-to-all-done.3 = bf16[64,8,4096]{2,1,0:T(8,128)(2,1)} async-done(((bf16[64,8,4096]{2,1,0:T(8,128)(2,1)}), bf16[64,8,4096]{2,1,0:T(8,128)(2,1)}, u32[]{:S(2)}, u32[]{:S(2)}) %all-to-all-start.3) | async-done | bytes 4194336 | tf_op jit(solution)/shard_map/all_to_all | solution.py:144
  181.5 3.1 %fusion.14 = f32[64,4096]{1,0:T(8,128)S(1)} fusion(bf16[64,8,4096]{2,1,0:T(8,128)(2,1)} %all-to-all-done.3, bf16[512,32]{1,0:T(8,128)(2,1)S(1)} %bitcast.110, bf16[512,32]{1,0:T(8,128)(2,1)S(1)} %bitcast.109), kind=kOutput, calls=%fused_computation.12 | convolution fusion | flops 268566528 | bytes 5308416 | tf_op jit(solution)/shard_map/dot_general | solution.py:150
  184.9 2.7 %collective-permute-start.6 = (f32[2,8,4096]{2,1,0:T(8,128)S(1)}, f32[2,8,4096]{2,1,0:T(8,128)S(1)}, u32[]{:S(2)}, u32[]{:S(2)}) collective-permute-start(f32[2,8,4096]{2,1,0:T(8,128)S(1)} %dynamic-slice_bitcast_fusion), channel_id=1, source_target_pairs={{0,1},{1,0},{2,3},{3,2},{4,5},{5,4},{6,7},{7,6},{8,9},{9,8},{10,11... | collective-permute-start | bytes 786440 | tf_op jit(solution)/shard_map/ppermute | solution.py:19
  187.6 1.2 collective-permute-done.6
  (75 shorter events, 7.1 us)
Async XLA Ops:
  0.0 9.0 %copy-start = (bf16[2,128,256]{2,1,0:T(8,128)(2,1)S(1)}, bf16[2,128,256]{2,1,0:T(8,128)(2,1)}, u32[]{:S(2)}) copy-start(bf16[2,128,256]{2,1,0:T(8,128)(2,1)} %param.10) | copy-start | bytes 393220
  0.0 21.2 %collective-permute-start.4 = (bf16[256,4096]{1,0:T(8,128)(2,1)}, bf16[256,4096]{1,0:T(8,128)(2,1)S(1)}, u32[]{:S(2)}, u32[]{:S(2)}) collective-permute-start(bf16[256,4096]{1,0:T(8,128)(2,1)} %param.13), channel_id=1, source_target_pairs={{0,1},{1,0},{2,3},{3,2},{4,5},{5,4},{6,7},{7,6},{8,9},{9,8},{10,11... | collective-permute-start | bytes 6291464 | tf_op jit(solution)/shard_map/ppermute | solution.py:19
  3.3 15.9 %all-to-all-start = ((bf16[8,2,128,128]{3,2,1,0:T(8,128)(2,1)}), bf16[8,2,128,128]{3,2,1,0:T(8,128)(2,1)S(1)}, u32[]{:S(2)}, u32[]{:S(2)}) async-start(bf16[8,2,128,128]{3,2,1,0:T(8,128)(2,1)} %broadcast_in_dim.85), calls=%async_computation | async-start | bytes 1048576 | tf_op jit(solution)/shard_map/all_to_all | solution.py:76
  9.1 1.3 collective-permute-start.3
  20.5 1.6 copy-start.5
  23.8 7.2 %copy-start.1 = (bf16[2,8,4096]{2,1,0:T(8,128)(2,1)S(1)}, bf16[2,8,4096]{2,1,0:T(8,128)(2,1)}, u32[]{:S(2)}) copy-start(bf16[2,8,4096]{2,1,0:T(8,128)(2,1)} %param.14) | copy-start | bytes 393220
  23.8 8.3 %copy-start.3 = (s32[2,8,8]{2,1,0:T(8,128)S(1)}, s32[2,8,8]{2,1,0:T(8,128)}, u32[]{:S(2)}) copy-start(s32[2,8,8]{2,1,0:T(8,128)} %param.18) | copy-start | bytes 1540
  23.8 24.8 %copy-start.2 = (f32[4096]{0:T(1024)S(1)}, f32[4096]{0:T(1024)}, u32[]{:S(2)}) copy-start(f32[4096]{0:T(1024)} %param.15) | copy-start | bytes 49156
  23.8 24.5 %all-to-all-start.1 = ((bf16[8,16,4096]{2,1,0:T(8,128)(2,1)}), bf16[8,16,4096]{2,1,0:T(8,128)(2,1)S(1)}, u32[]{:S(2)}, u32[]{:S(2)}) async-start(bf16[8,16,4096]{2,1,0:T(8,128)(2,1)} %bitcast.25), calls=%async_computation.1 | async-start | bytes 2097152 | tf_op jit(solution)/shard_map/all_to_all | solution.py:95
  31.0 17.4 %collective-permute-start.2 = (bf16[8,4096]{1,0:T(8,128)(2,1)S(1)}, bf16[8,4096]{1,0:T(8,128)(2,1)S(1)}, u32[]{:S(2)}, u32[]{:S(2)}) collective-permute-start(bf16[8,4096]{1,0:T(8,128)(2,1)S(1)} %get-tuple-element.9), channel_id=1, source_target_pairs={{0,1},{1,0},{2,3},{3,2},{4,5},{5,4},{6,7},{7,6},{8,9},{9,8},{10,11... | collective-permute-start | bytes 196616 | tf_op jit(solution)/shard_map/ppermute | solution.py:19
  32.1 1.2 collective-permute-start
  48.7 1.9 %collective-permute-start.5 = (bf16[16,4096]{1,0:T(8,128)(2,1)S(1)}, bf16[16,4096]{1,0:T(8,128)(2,1)S(1)}, u32[]{:S(2)}, u32[]{:S(2)}) collective-permute-start(bf16[16,4096]{1,0:T(8,128)(2,1)S(1)} %multiply_convert_fusion), channel_id=1, source_target_pairs={{0,1},{1,0},{2,3},{3,2},{4,5},{5,4},{6,7},{7,6},{8,9},{9,8},{10,11... | collective-permute-start | bytes 393224 | tf_op jit(solution)/shard_map/ppermute | solution.py:19
  51.9 63.9 %slice-start = ((s8[6291456]{0:T(1024)(128)(4,1)}), s8[4194304]{0:T(1024)(128)(4,1)S(1)}, s32[]{:S(2)}) async-start(s8[6291456]{0:T(1024)(128)(4,1)} %bitcast.124), calls=%async_computation.4 | async-start | bytes 8388608
  106.5 9.4 %slice-start.1 = ((s8[6291456]{0:T(1024)(128)(4,1)}), s8[2097152]{0:T(1024)(128)(4,1)S(1)}, s32[]{:S(2)}) async-start(s8[6291456]{0:T(1024)(128)(4,1)} %bitcast.124), calls=%async_computation.5 | async-start | bytes 4194304
  121.0 8.8 %copy-start.4 = (f32[2,8,8]{2,1,0:T(8,128)S(1)}, f32[2,8,8]{2,1,0:T(8,128)}, u32[]{:S(2)}) copy-start(f32[2,8,8]{2,1,0:T(8,128)} %param.19) | copy-start | bytes 1540
  121.0 60.5 %all-to-all-start.3 = ((bf16[64,8,4096]{2,1,0:T(8,128)(2,1)}), bf16[64,8,4096]{2,1,0:T(8,128)(2,1)}, u32[]{:S(2)}, u32[]{:S(2)}) async-start(bf16[64,8,4096]{2,1,0:T(8,128)(2,1)} %fusion.8), calls=%async_computation.3 | async-start | bytes 8388608 | tf_op jit(solution)/shard_map/all_to_all | solution.py:144
  129.8 2.9 %collective-permute-start.1 = (f32[2,8,8]{2,1,0:T(8,128)S(1)}, f32[2,8,8]{2,1,0:T(8,128)S(1)}, u32[]{:S(2)}, u32[]{:S(2)}) collective-permute-start(f32[2,8,8]{2,1,0:T(8,128)S(1)} %copy-done.4), channel_id=1, source_target_pairs={{0,1},{1,0},{2,3},{3,2},{4,5},{5,4},{6,7},{7,6},{8,9},{9,8},{10,11... | collective-permute-start | bytes 1544 | tf_op jit(solution)/shard_map/ppermute | solution.py:19
  184.9 3.8 %collective-permute-start.6 = (f32[2,8,4096]{2,1,0:T(8,128)S(1)}, f32[2,8,4096]{2,1,0:T(8,128)S(1)}, u32[]{:S(2)}, u32[]{:S(2)}) collective-permute-start(f32[2,8,4096]{2,1,0:T(8,128)S(1)} %dynamic-slice_bitcast_fusion), channel_id=1, source_target_pairs={{0,1},{1,0},{2,3},{3,2},{4,5},{5,4},{6,7},{7,6},{8,9},{9,8},{10,11... | collective-permute-start | bytes 786440 | tf_op jit(solution)/shard_map/ppermute | solution.py:19

commit v2 on v1

--- a/solution.py
+++ b/solution.py
@@ -1,6 +1,10 @@
+import functools
+
 import jax
 import jax.numpy as jnp
 from jax import lax
+from jax.experimental import pallas as pl
+from jax.experimental.pallas import tpu as pltpu
 from jax.sharding import Mesh, PartitionSpec as P
 
 QH = 32
@@ -19,28 +23,185 @@
     return lax.ppermute(value, "core", SWAP)
 
 
-def folded_positions(first_row, row_count, context_size):
-    stored = first_row + jnp.arange(row_count, dtype=jnp.int32)
-    block_index = stored // BLOCK
-    block_order = jnp.where(
-        block_index % 2 == 0, block_index // 2, 2 * context_size - 1 - block_index // 2
-    )
-    return block_order * BLOCK + stored % BLOCK
-
-
-def attend(query_heads, keys, values, query_position, key_position):
-    allowed = (key_position[None, :] <= query_position[:, None])[None]
-    scores = jnp.einsum(
-        "hqd,kd->hqk", query_heads, keys, preferred_element_type=jnp.float32
-    ) * HD ** (-0.5)
-    scores = jnp.where(allowed, scores, masked_score)
-    largest = jnp.max(scores, axis=-1, keepdims=True)
-    weights = jnp.exp(scores - largest)
-    total = jnp.sum(weights, axis=-1, keepdims=True)
-    weighted = jnp.einsum(
-        "hqk,kd->qhd", weights.astype(jnp.bfloat16), values, preferred_element_type=jnp.float32
-    )
-    return (weighted / total.transpose(1, 0, 2)).astype(jnp.bfloat16)
+def folded(rows, piece, context_size):
+    block_order = jnp.where(rows < BLOCK, piece, 2 * context_size - 1 - piece)
+    return block_order * BLOCK + rows % BLOCK
+
+
+def attention_kernel(
+    index_ref, own_ref, other_ref, kv_ref, proj_ref, other_proj_ref, out_ref, proj, sems
+):
+    context_size, _, row_count, _ = kv_ref.shape
+    feature_count = own_ref.shape[1]
+    copies = [
+        pltpu.make_async_copy(source, proj.at[pl.ds(part * feature_count, feature_count)], sems.at[part])
+        for part, source in enumerate((proj_ref, other_proj_ref))
+    ]
+    for copy in copies:
+        copy.start()
+    key_count = context_size * row_count
+    keys = kv_ref[:, 0].reshape(key_count, HD)
+    values = kv_ref[:, 1].reshape(key_count, HD)
+    query_rows = lax.broadcasted_iota(jnp.int32, (row_count, key_count), 0)
+    key_rows = lax.broadcasted_iota(jnp.int32, (row_count, key_count), 1)
+    allowed = folded(key_rows % row_count, key_rows // row_count, context_size) <= folded(
+        query_rows, index_ref[0], context_size
+    )
+    heads = []
+    for source in (own_ref, other_ref):
+        for head in range(feature_count // HD):
+            query = source[:, head * HD : (head + 1) * HD]
+            scores = lax.dot_general(
+                query, keys, (((1,), (1,)), ((), ())), preferred_element_type=jnp.float32
+            ) * HD ** (-0.5)
+            scores = jnp.where(allowed, scores, masked_score)
+            weights = jnp.exp(scores - jnp.max(scores, axis=-1, keepdims=True))
+            total = jnp.sum(weights, axis=-1, keepdims=True)
+            weighted = jnp.dot(
+                weights.astype(jnp.bfloat16), values, preferred_element_type=jnp.float32
+            )
+            heads.append((weighted / total).astype(jnp.bfloat16))
+    attended = jnp.concatenate(heads, axis=1)
+    for copy in copies:
+        copy.wait()
+    out_ref[...] = jnp.dot(attended, proj[...], preferred_element_type=jnp.float32).astype(
+        jnp.bfloat16
+    )
+
+
+def attend(context_index, own, other, gathered, out_proj, other_proj):
+    row_count, feature_count = own.shape
+    model_width = out_proj.shape[1]
+    whole = pl.BlockSpec(memory_space=pltpu.VMEM)
+    apart = pl.BlockSpec(memory_space=pl.ANY)
+    return pl.pallas_call(
+        attention_kernel,
+        in_specs=[pl.BlockSpec(memory_space=pltpu.SMEM), whole, whole, whole, apart, apart],
+        out_specs=whole,
+        out_shape=jax.ShapeDtypeStruct((row_count, model_width), jnp.bfloat16),
+        scratch_shapes=[
+            pltpu.VMEM((2 * feature_count, model_width), jnp.bfloat16),
+            pltpu.SemaphoreType.DMA((2,)),
+        ],
+        compiler_params=pltpu.CompilerParams(vmem_limit_bytes=48 * 2**20),
+    )(context_index, own, other, gathered, out_proj, other_proj)
+
+
+def starts(sizes):
+    return [sum(sizes[:part]) for part in range(len(sizes))]
+
+
+def expert_kernel(
+    rows_ref, w_in_ref, w_out_ref, out_ref,
+    rows, w_in, w_out, mixed, hidden, result, row_sems, in_sems, out_sem, result_sems,
+    *, depths, widths,
+):
+    half_width = w_out_ref.shape[0]
+    pieces = list(zip(starts(depths), depths))
+    row_copies = [
+        pltpu.make_async_copy(
+            rows_ref.at[:, pl.ds(first, size)], rows.at[:, pl.ds(first, size)], row_sems.at[part]
+        )
+        for part, (first, size) in enumerate(pieces)
+    ]
+    in_copies = [
+        pltpu.make_async_copy(
+            w_in_ref.at[pl.ds(first, size)], w_in.at[pl.ds(first, size)], in_sems.at[part]
+        )
+        for part, (first, size) in enumerate(pieces)
+    ]
+    out_copy = pltpu.make_async_copy(w_out_ref, w_out, out_sem)
+    for part in range(len(pieces)):
+        row_copies[part].start()
+        in_copies[part].start()
+    out_copy.start()
+    for part, (first, size) in enumerate(pieces):
+        row_copies[part].wait()
+        in_copies[part].wait()
+        product = jnp.dot(
+            rows[:, first : first + size],
+            w_in[first : first + size, :],
+            preferred_element_type=jnp.float32,
+        )
+        if part == 0:
+            mixed[...] = product
+        elif part < len(pieces) - 1:
+            mixed[...] += product
+        else:
+            total = mixed[...] + product
+            gate = total[:, :half_width]
+            hidden[...] = (gate / (1.0 + jnp.exp(-gate)) * total[:, half_width:]).astype(
+                jnp.bfloat16
+            )
+    out_copy.wait()
+    result_copies = []
+    for part, (first, size) in enumerate(zip(starts(widths), widths)):
+        columns = pl.ds(first, size)
+        result[:, columns] = jnp.dot(
+            hidden[...], w_out[:, columns], preferred_element_type=jnp.float32
+        ).astype(jnp.bfloat16)
+        copy = pltpu.make_async_copy(
+            result.at[:, columns], out_ref.at[:, columns], result_sems.at[part]
+        )
+        copy.start()
+        result_copies.append(copy)
+    for copy in result_copies:
+        copy.wait()
+
+
+def expert_rows(rows, w_in, w_out):
+    row_count, model_width = rows.shape
+    half_width = w_out.shape[0]
+    depths = tuple(model_width * part // 16 for part in (2, 4, 5, 5))
+    widths = (model_width // 8,) * 8
+    apart = pl.BlockSpec(memory_space=pl.ANY)
+    return pl.pallas_call(
+        functools.partial(expert_kernel, depths=depths, widths=widths),
+        in_specs=[apart, apart, apart],
+        out_specs=apart,
+        out_shape=jax.ShapeDtypeStruct((row_count, model_width), jnp.bfloat16),
+        scratch_shapes=[
+            pltpu.VMEM((row_count, model_width), jnp.bfloat16),
+            pltpu.VMEM((model_width, 2 * half_width), jnp.bfloat16),
+            pltpu.VMEM((half_width, model_width), jnp.bfloat16),
+            pltpu.VMEM((row_count, 2 * half_width), jnp.float32),
+            pltpu.VMEM((row_count, half_width), jnp.bfloat16),
+            pltpu.VMEM((row_count, model_width), jnp.bfloat16),
+            pltpu.SemaphoreType.DMA((len(depths),)),
+            pltpu.SemaphoreType.DMA((len(depths),)),
+            pltpu.SemaphoreType.DMA,
+            pltpu.SemaphoreType.DMA((len(widths),)),
+        ],
+        compiler_params=pltpu.CompilerParams(vmem_limit_bytes=52 * 2**20),
+    )(rows, w_in, w_out)
+
+
+def combine_kernel(gates_ref, returned_ref, base_ref, kept_ref, sent_ref):
+    token_count = base_ref.shape[0]
+    summed = jnp.dot(gates_ref[...], returned_ref[...], preferred_element_type=jnp.float32)
+    total = summed[:token_count] + summed[token_count:] + base_ref[...]
+    kept_ref[...] = total[: token_count // 2]
+    sent_ref[...] = total[token_count // 2 :]
+
+
+def combine(gates, returned, base):
+    slot_count, model_width = returned.shape
+    token_count = base.shape[0]
+    width = model_width // 4
+    half = jax.ShapeDtypeStruct((token_count // 2, model_width), jnp.float32)
+    columns = lambda rows: pl.BlockSpec((rows, width), lambda step: (0, step))
+    return pl.pallas_call(
+        combine_kernel,
+        grid=(model_width // width,),
+        in_specs=[
+            pl.BlockSpec(gates.shape, lambda step: (0, 0)),
+            columns(slot_count),
+            columns(token_count),
+        ],
+        out_specs=[columns(token_count // 2), columns(token_count // 2)],
+        out_shape=[half, half],
+        compiler_params=pltpu.CompilerParams(vmem_limit_bytes=32 * 2**20),
+    )(gates, returned, base)
 
 
 def local(
@@ -76,22 +237,14 @@
     gathered = lax.all_to_all(
         jnp.broadcast_to(pair[None], (context_size,) + pair.shape), CONTEXT, 0, 0
     )
-    all_keys = gathered[:, 0].reshape(context_size * row_count, HD)
-    all_values = gathered[:, 1].reshape(context_size * row_count, HD)
-    query_rows = jnp.concatenate([of_batch(queries, core), other_queries], axis=1)
-    query_heads = query_rows.reshape(row_count, 2 * heads_here, HD).transpose(1, 0, 2)
-    attended = attend(
-        query_heads,
-        all_keys,
-        all_values,
-        folded_positions(lax.axis_index(CONTEXT) * row_count, row_count, context_size),
-        folded_positions(0, context_size * row_count, context_size),
-    ).reshape(row_count, 2 * feature_count)
-    projected = jnp.dot(
-        attended,
-        jnp.concatenate([out_proj, other_proj], axis=0),
-        preferred_element_type=jnp.float32,
-    ).astype(jnp.bfloat16)
+    projected = attend(
+        lax.axis_index(CONTEXT).astype(jnp.int32).reshape(1),
+        of_batch(queries, core),
+        other_queries,
+        gathered,
+        out_proj,
+        other_proj,
+    )
     pieces = lax.all_to_all(
         projected.reshape(column_size, chip_rows, model_width), COLUMN, 0, 0
     )
@@ -135,33 +288,32 @@
     received = lax.all_to_all(
         outgoing.reshape(chip_count, slots, model_width), CHIPS, 0, 0
     ).reshape(chip_count * slots, model_width)
-    mixed = jnp.dot(received, w_in[0], preferred_element_type=jnp.float32)
-    half_width = w_out.shape[1]
-    hidden = (jax.nn.silu(mixed[:, :half_width]) * mixed[:, half_width:]).astype(jnp.bfloat16)
-    partial_value = jnp.dot(hidden, w_out[0], preferred_element_type=jnp.float32).astype(
-        jnp.bfloat16
-    )
+    partial_value = expert_rows(received, w_in[0], w_out[0])
     returned = lax.all_to_all(
         partial_value.reshape(chip_count, slots, model_width), CHIPS, 0, 0
     ).reshape(chip_count * slots, model_width)
-    gate_high = gate_matrix.astype(jnp.bfloat16)
-    gate_low = (gate_matrix - gate_high.astype(jnp.float32)).astype(jnp.bfloat16)
-    both = jnp.concatenate([both_halves(gate_high), both_halves(gate_low)], axis=1)
-    summed = lax.dot_general(
-        both, returned, (((0,), (0,)), ((), ())), preferred_element_type=jnp.float32
-    )
-    mixed_out = (summed[:tokens] + summed[tokens:]).reshape(
-        batch_count, 2, token_rows, model_width
-    )
+    def kept_first(value):
+        grouped = value.reshape((batch_count, 2, token_rows) + value.shape[1:])
+        ordered = jnp.stack(
+            [
+                lax.dynamic_index_in_dim(grouped, core, 1, keepdims=False),
+                lax.dynamic_index_in_dim(grouped, 1 - core, 1, keepdims=False),
+            ]
+        )
+        return ordered.reshape(value.shape)
+
+    gate_rows = kept_first(both_halves(gate_matrix).T)
+    gate_high = gate_rows.astype(jnp.bfloat16)
+    gate_low = (gate_rows - gate_high.astype(jnp.float32)).astype(jnp.bfloat16)
     own_sum = jnp.where(
-        (jnp.arange(batch_count) == core)[:, None, None, None],
-        residual_sum.reshape(1, 2, token_rows, model_width),
-        0.0,
-    )
-    total = mixed_out + own_sum
-    kept = lax.dynamic_index_in_dim(total, core, 1, keepdims=False)
-    sent = lax.dynamic_index_in_dim(total, 1 - core, 1, keepdims=False)
-    return (kept + swap_cores(sent)).astype(jnp.bfloat16)
+        (jnp.arange(batch_count) == core)[:, None, None], residual_sum[None], 0.0
+    ).reshape(tokens, model_width)
+    kept, sent = combine(
+        jnp.concatenate([gate_high, gate_low]), returned, kept_first(own_sum)
+    )
+    return (
+        (kept + swap_cores(sent)).astype(jnp.bfloat16).reshape(batch_count, token_rows, model_width)
+    )
 
 
 def solution(mesh):

time: 191 us -> 192 us (level)
  Pallas kernels: 0 us -> 21.7 us
  matrix products: 21.8 us -> 1.22 us
  starting transfers between devices: 30.3 us -> 27.9 us
    pallas_call x0 -> x3, Pallas kernels: none -> 21.7 us  [the longest x1 13.4 us: expert_rows(): pl.pallas_call(functools.partial(expert_kernel, depths=depths, widths=wid...]
    dot_general x6 -> x0, matrix products: 20.6 us -> none  [the longest x1 9.35 us: local(): mixed = jnp.dot(received, w_in[0], preferred_element_type=jnp.float32)]
  transfers between devices with their start and end apart: 10 -> 10, of which waited for: 8 -> 8; matrix products, arithmetic and copies ran while one was open for 4% -> 3% of each run, Pallas kernels for 0% -> 0%
where the time goes in v2:
time: 192 us; the launch traced here: 189 us
  waiting for transfers between devices  75.6 us (39%)
  blocking collectives  55.7 us (29%)
  starting transfers between devices  27.9 us (15%)
  Pallas kernels  21.7 us (11%)
  local copies, waits for them, and re-layouts  3.99 us (2%)
  other arithmetic  2.28 us (1%)
    all_to_all x1, blocking collectives, local(): lax.all_to_all(outgoing.reshape(chip_count, slots, model_width), CHIPS, 0...  55.7 us
    all_to_all x1, waiting for transfers between devices, local(): lax.all_to_all(partial_value.reshape(chip_count, slots, model_width), CHI...  49.4 us
    all_to_all x1, waiting for transfers between devices, local(): lax.all_to_all(projected.reshape(column_size, chip_rows, model_width), CO...  13.7 us
    pallas_call x1, Pallas kernels, expert_rows(): pl.pallas_call(functools.partial(expert_kernel, depths=depths, widths=wid...  13.4 us
    all_to_all x1, waiting for transfers between devices, local(): lax.all_to_all(jnp.broadcast_to(pair[None], (context_size,) + pair.shape)...  7.89 us
    all_to_all x1, starting transfers between devices, local(): lax.all_to_all(partial_value.reshape(chip_count, slots, model_width), CHI...  7.83 us
    ppermute x7, starting transfers between devices, swap_cores(): return lax.ppermute(value, 'core', SWAP)  7.34 us
    all_to_all x1, starting transfers between devices, local(): lax.all_to_all(projected.reshape(column_size, chip_rows, model_width), CO...  7.05 us
  transfers between devices with their start and end apart: 10, of which 8 were waited for; matrix products, arithmetic and copies ran while one was open for 3% of the time, Pallas kernels for 0%

profile of v2, /device:TPU:1, one launch (start us, length us, event | category | flops | bytes accessed | tf_op | source)
XLA Modules:
  0.0 188.6 jit_solution(708369360444934131)
XLA Ops:
  0.0 1.4 collective-permute-start.4
  1.4 1.0 constant_dynamic-slice_fusion
  2.4 0.9 broadcast_in_dim.64
  3.3 5.6 %all-to-all-start = ((bf16[8,2,128,128]{3,2,1,0:T(8,128)(2,1)}), bf16[8,2,128,128]{3,2,1,0:T(8,128)(2,1)S(1)}, u32[]{:S(2)}, u32[]{:S(2)}) async-start(bf16[8,2,128,128]{3,2,1,0:T(8,128)(2,1)} %broadcast_in_dim.64), calls=%async_computation | async-start | bytes 1048576 | tf_op jit(solution)/shard_map/all_to_all | solution.py:237
  9.0 0.9 dynamic-slice_bitcast_fusion.2
  10.4 0.9 collective-permute-done.3.other_ref
  11.3 7.9 %all-to-all-done.kv_ref = bf16[8,2,128,128]{3,2,1,0:T(8,128)(2,1)S(1)} async-done(((bf16[8,2,128,128]{3,2,1,0:T(8,128)(2,1)}), bf16[8,2,128,128]{3,2,1,0:T(8,128)(2,1)S(1)}, u32[]{:S(2)}, u32[]{:S(2)}) %all-to-all-start) | async-done | bytes 524320 | tf_op jit(solution)/shard_map/all_to_all | solution.py:237
  19.2 4.8 %shard_map.100 = bf16[128,4096]{1,0:T(8,128)(2,1)} custom-call(s32[1]{0:T(128)} %bitcast.16.index_ref, bf16[128,256]{1,0:T(8,128)(2,1)S(1)} %get-tuple-element.16.own_ref, bf16[128,256]{1,0:T(8,128)(2,1)S(1)} %collective-permute-done.3.other_ref, bf16[8,2,128,128]{3,2,1,0:T(8,128)(2,1)S(1)} %all-to-all-done.kv_ref, bf16[256,4096]{1,0:T(8,128)(2,1)S(1)} %copy-done, ...), custom_call_target="tpu_custom_call" | custom-call | tf_op jit(solution)/shard_map/pallas_call | solution.py:77
  24.1 7.0 %all-to-all-start.1 = ((bf16[8,16,4096]{2,1,0:T(8,128)(2,1)}), bf16[8,16,4096]{2,1,0:T(8,128)(2,1)S(1)}, u32[]{:S(2)}, u32[]{:S(2)}) async-start(bf16[8,16,4096]{2,1,0:T(8,128)(2,1)} %bitcast.19), calls=%async_computation.1 | async-start | bytes 2097152 | tf_op jit(solution)/shard_map/all_to_all | solution.py:248
  31.1 1.1 collective-permute-start.2
  32.5 0.9 collective-permute-done
  34.7 13.7 %all-to-all-done.1 = bf16[8,16,4096]{2,1,0:T(8,128)(2,1)S(1)} async-done(((bf16[8,16,4096]{2,1,0:T(8,128)(2,1)}), bf16[8,16,4096]{2,1,0:T(8,128)(2,1)S(1)}, u32[]{:S(2)}, u32[]{:S(2)}) %all-to-all-start.1) | async-done | bytes 1048608 | tf_op jit(solution)/shard_map/all_to_all | solution.py:248
  48.9 0.9 collective-permute-start.5
  49.9 0.9 collective-permute-done.5
  50.8 1.2 fusion
  52.1 55.7 %all_to_all.20 = bf16[64,8,4096]{2,1,0:T(8,128)(2,1)} all-to-all(bf16[64,8,4096]{2,1,0:T(8,128)(2,1)S(1)} %fusion), channel_id=1, replica_groups=mesh['zl'=2,'y'=4,'zh'=2,'x'=4,'core'=2] {'zl','y','zh','x'}, dimensions={0} | all-to-all | bytes 8388608 | tf_op jit(solution)/shard_map/all_to_all | solution.py:288
  107.7 13.4 %shard_map.101 = bf16[512,4096]{1,0:T(8,128)(2,1)} custom-call(bf16[512,4096]{1,0:T(8,128)(2,1)} %bitcast.79, bf16[4096,1536]{1,0:T(8,128)(2,1)} %bitcast.80, bf16[768,4096]{1,0:T(8,128)(2,1)} %bitcast.81), custom_call_target="tpu_custom_call" | custom-call | tf_op jit(solution)/shard_map/pallas_call | solution.py:158
  121.1 7.8 %all-to-all-start.3 = ((bf16[64,8,4096]{2,1,0:T(8,128)(2,1)}), bf16[64,8,4096]{2,1,0:T(8,128)(2,1)}, u32[]{:S(2)}, u32[]{:S(2)}) async-start(bf16[64,8,4096]{2,1,0:T(8,128)(2,1)} %bitcast.78), calls=%async_computation.3 | async-start | bytes 8388608 | tf_op jit(solution)/shard_map/all_to_all | solution.py:292
  129.0 1.5 collective-permute-start.1
  130.5 0.8 collective-permute-done.1
  132.2 49.4 %all-to-all-done.3 = bf16[64,8,4096]{2,1,0:T(8,128)(2,1)} async-done(((bf16[64,8,4096]{2,1,0:T(8,128)(2,1)}), bf16[64,8,4096]{2,1,0:T(8,128)(2,1)}, u32[]{:S(2)}, u32[]{:S(2)}) %all-to-all-start.3) | async-done | bytes 4194336 | tf_op jit(solution)/shard_map/all_to_all | solution.py:292
  181.6 3.5 %shard_map.102 = (f32[16,4096]{1,0:T(8,128)S(1)}, f32[16,4096]{1,0:T(8,128)S(1)}) custom-call(bf16[64,512]{1,0:T(8,128)(2,1)S(1)} %pad_maximum_fusion.2.gates_ref, bf16[512,4096]{1,0:T(8,128)(2,1)} %bitcast.29.returned_ref, f32[32,4096]{1,0:T(8,128)S(1)} %bitcast.77), custom_call_target="tpu_custom_call" | custom-call | tf_op jit(solution)/shard_map/pallas_call | solution.py:193
  185.1 1.7 collective-permute-start.6
  186.8 1.2 collective-permute-done.6
  (57 shorter events, 4.1 us)
Async XLA Ops:
  0.0 19.2 %copy-start = (bf16[256,4096]{1,0:T(8,128)(2,1)S(1)}, bf16[256,4096]{1,0:T(8,128)(2,1)}, u32[]{:S(2)}) copy-start(bf16[256,4096]{1,0:T(8,128)(2,1)} %proj_ref.1) | copy-start | bytes 6291460
  0.0 19.2 %collective-permute-start.4 = (bf16[256,4096]{1,0:T(8,128)(2,1)}, bf16[256,4096]{1,0:T(8,128)(2,1)}, u32[]{:S(2)}, u32[]{:S(2)}) collective-permute-start(bf16[256,4096]{1,0:T(8,128)(2,1)} %proj_ref.1), channel_id=1, source_target_pairs={{0,1},{1,0},{2,3},{3,2},{4,5},{5,4},{6,7},{7,6},{8,9},{9,8},{10,11... | collective-permute-start | bytes 6291464 | tf_op jit(solution)/shard_map/ppermute | solution.py:23
  3.3 15.9 %all-to-all-start = ((bf16[8,2,128,128]{3,2,1,0:T(8,128)(2,1)}), bf16[8,2,128,128]{3,2,1,0:T(8,128)(2,1)S(1)}, u32[]{:S(2)}, u32[]{:S(2)}) async-start(bf16[8,2,128,128]{3,2,1,0:T(8,128)(2,1)} %broadcast_in_dim.64), calls=%async_computation | async-start | bytes 1048576 | tf_op jit(solution)/shard_map/all_to_all | solution.py:237
  9.0 22.1 %copy-start.1 = (bf16[2,8,4096]{2,1,0:T(8,128)(2,1)S(1)}, bf16[2,8,4096]{2,1,0:T(8,128)(2,1)}, u32[]{:S(2)}) copy-start(bf16[2,8,4096]{2,1,0:T(8,128)(2,1)} %param.14) | copy-start | bytes 393220
  9.9 22.4 %copy-start.3 = (s32[2,8,8]{2,1,0:T(8,128)S(1)}, s32[2,8,8]{2,1,0:T(8,128)}, u32[]{:S(2)}) copy-start(s32[2,8,8]{2,1,0:T(8,128)} %param.18) | copy-start | bytes 1540
  9.9 1.4 collective-permute-start.3
  19.2 29.5 %copy-start.2 = (f32[4096]{0:T(1024)S(1)}, f32[4096]{0:T(1024)}, u32[]{:S(2)}) copy-start(f32[4096]{0:T(1024)} %param.15) | copy-start | bytes 49156
  24.1 24.4 %all-to-all-start.1 = ((bf16[8,16,4096]{2,1,0:T(8,128)(2,1)}), bf16[8,16,4096]{2,1,0:T(8,128)(2,1)S(1)}, u32[]{:S(2)}, u32[]{:S(2)}) async-start(bf16[8,16,4096]{2,1,0:T(8,128)(2,1)} %bitcast.19), calls=%async_computation.1 | async-start | bytes 2097152 | tf_op jit(solution)/shard_map/all_to_all | solution.py:248
  31.1 17.4 %collective-permute-start.2 = (bf16[8,4096]{1,0:T(8,128)(2,1)S(1)}, bf16[8,4096]{1,0:T(8,128)(2,1)S(1)}, u32[]{:S(2)}, u32[]{:S(2)}) collective-permute-start(bf16[8,4096]{1,0:T(8,128)(2,1)S(1)} %get-tuple-element.13), channel_id=1, source_target_pairs={{0,1},{1,0},{2,3},{3,2},{4,5},{5,4},{6,7},{7,6},{8,9},{9,8},{10,11... | collective-permute-start | bytes 196616 | tf_op jit(solution)/shard_map/ppermute | solution.py:23
  32.3 1.2 collective-permute-start
  48.9 1.9 %collective-permute-start.5 = (bf16[16,4096]{1,0:T(8,128)(2,1)S(1)}, bf16[16,4096]{1,0:T(8,128)(2,1)S(1)}, u32[]{:S(2)}, u32[]{:S(2)}) collective-permute-start(bf16[16,4096]{1,0:T(8,128)(2,1)S(1)} %multiply_convert_fusion), channel_id=1, source_target_pairs={{0,1},{1,0},{2,3},{3,2},{4,5},{5,4},{6,7},{7,6},{8,9},{9,8},{10,11... | collective-permute-start | bytes 393224 | tf_op jit(solution)/shard_map/ppermute | solution.py:23
  121.1 7.9 %copy-start.4 = (f32[2,8,8]{2,1,0:T(8,128)S(1)}, f32[2,8,8]{2,1,0:T(8,128)}, u32[]{:S(2)}) copy-start(f32[2,8,8]{2,1,0:T(8,128)} %param.19) | copy-start | bytes 1540
  121.1 60.4 %all-to-all-start.3 = ((bf16[64,8,4096]{2,1,0:T(8,128)(2,1)}), bf16[64,8,4096]{2,1,0:T(8,128)(2,1)}, u32[]{:S(2)}, u32[]{:S(2)}) async-start(bf16[64,8,4096]{2,1,0:T(8,128)(2,1)} %bitcast.78), calls=%async_computation.3 | async-start | bytes 8388608 | tf_op jit(solution)/shard_map/all_to_all | solution.py:292
  129.0 2.4 %collective-permute-start.1 = (f32[2,8,8]{2,1,0:T(8,128)S(1)}, f32[2,8,8]{2,1,0:T(8,128)S(1)}, u32[]{:S(2)}, u32[]{:S(2)}) collective-permute-start(f32[2,8,8]{2,1,0:T(8,128)S(1)} %copy-done.4), channel_id=1, source_target_pairs={{0,1},{1,0},{2,3},{3,2},{4,5},{5,4},{6,7},{7,6},{8,9},{9,8},{10,11... | collective-permute-start | bytes 1544 | tf_op jit(solution)/shard_map/ppermute | solution.py:23
  185.1 2.8 %collective-permute-start.6 = (f32[16,4096]{1,0:T(8,128)S(1)}, f32[16,4096]{1,0:T(8,128)S(1)}, u32[]{:S(2)}, u32[]{:S(2)}) collective-permute-start(f32[16,4096]{1,0:T(8,128)S(1)} %get-tuple-element.8), channel_id=1, source_target_pairs={{0,1},{1,0},{2,3},{3,2},{4,5},{5,4},{6,7},{7,6},{8,9},{9,8},{10,11... | collective-permute-start | bytes 786440 | tf_op jit(solution)/shard_map/ppermute | solution.py:23

commit v3 on v2

--- a/solution.py
+++ b/solution.py
@@ -91,19 +91,26 @@
     return [sum(sizes[:part]) for part in range(len(sizes))]
 
 
-def expert_kernel(
-    rows_ref, w_in_ref, w_out_ref, out_ref,
-    rows, w_in, w_out, mixed, hidden, result, row_sems, in_sems, out_sem, result_sems,
-    *, depths, widths,
-):
+def expert_kernel(*refs, depths, widths, part_widths):
+    row_refs = refs[: len(part_widths)]
+    w_in_ref, w_out_ref, out_ref = refs[len(part_widths) : len(part_widths) + 3]
+    rows, w_in, w_out, mixed, hidden, result, row_sems, in_sems, out_sem, result_sems = refs[
+        len(part_widths) + 3 :
+    ]
     half_width = w_out_ref.shape[0]
     pieces = list(zip(starts(depths), depths))
-    row_copies = [
-        pltpu.make_async_copy(
-            rows_ref.at[:, pl.ds(first, size)], rows.at[:, pl.ds(first, size)], row_sems.at[part]
-        )
-        for part, (first, size) in enumerate(pieces)
-    ]
+    row_copies = []
+    for part, (first, size) in enumerate(pieces):
+        holder, base = [
+            (ref, base) for ref, base in zip(row_refs, starts(part_widths)) if base <= first
+        ][-1]
+        row_copies.append(
+            pltpu.make_async_copy(
+                holder.at[:, pl.ds(first - base, size)],
+                rows.at[:, pl.ds(first, size)],
+                row_sems.at[part],
+            )
+        )
     in_copies = [
         pltpu.make_async_copy(
             w_in_ref.at[pl.ds(first, size)], w_in.at[pl.ds(first, size)], in_sems.at[part]
@@ -149,15 +156,20 @@
         copy.wait()
 
 
-def expert_rows(rows, w_in, w_out):
-    row_count, model_width = rows.shape
-    half_width = w_out.shape[0]
+def expert_rows(row_parts, w_in, w_out):
+    row_count = row_parts[0].shape[0]
+    half_width, model_width = w_out.shape
     depths = tuple(model_width * part // 16 for part in (2, 4, 5, 5))
     widths = (model_width // 8,) * 8
     apart = pl.BlockSpec(memory_space=pl.ANY)
     return pl.pallas_call(
-        functools.partial(expert_kernel, depths=depths, widths=widths),
-        in_specs=[apart, apart, apart],
+        functools.partial(
+            expert_kernel,
+            depths=depths,
+            widths=widths,
+            part_widths=tuple(part.shape[1] for part in row_parts),
+        ),
+        in_specs=[apart] * (len(row_parts) + 2),
         out_specs=apart,
         out_shape=jax.ShapeDtypeStruct((row_count, model_width), jnp.bfloat16),
         scratch_shapes=[
@@ -173,7 +185,7 @@
             pltpu.SemaphoreType.DMA((len(widths),)),
         ],
         compiler_params=pltpu.CompilerParams(vmem_limit_bytes=52 * 2**20),
-    )(rows, w_in, w_out)
+    )(*row_parts, w_in, w_out)
 
 
 def combine_kernel(gates_ref, returned_ref, base_ref, kept_ref, sent_ref):
@@ -282,16 +294,6 @@
             grouped, (grouped.shape[0], 2, grouped.shape[2], tokens)
         ).reshape(2 * slot_rows, tokens)
 
-    outgoing = jnp.dot(
-        both_halves(placing), all_normed, preferred_element_type=jnp.float32
-    ).astype(jnp.bfloat16)
-    received = lax.all_to_all(
-        outgoing.reshape(chip_count, slots, model_width), CHIPS, 0, 0
-    ).reshape(chip_count * slots, model_width)
-    partial_value = expert_rows(received, w_in[0], w_out[0])
-    returned = lax.all_to_all(
-        partial_value.reshape(chip_count, slots, model_width), CHIPS, 0, 0
-    ).reshape(chip_count * slots, model_width)
     def kept_first(value):
         grouped = value.reshape((batch_count, 2, token_rows) + value.shape[1:])
         ordered = jnp.stack(
@@ -308,8 +310,42 @@
     own_sum = jnp.where(
         (jnp.arange(batch_count) == core)[:, None, None], residual_sum[None], 0.0
     ).reshape(tokens, model_width)
-    kept, sent = combine(
-        jnp.concatenate([gate_high, gate_low]), returned, kept_first(own_sum)
+    both_gates = jnp.concatenate([gate_high, gate_low])
+    base = kept_first(own_sum)
+    first_width = model_width // 8
+
+    def exchange(rows):
+        width = rows.shape[1]
+        return lax.all_to_all(rows.reshape(chip_count, slots, width), CHIPS, 0, 0).reshape(
+            chip_count * slots, width
+        )
+
+    def dispatch(placing_rows, columns):
+        return exchange(
+            jnp.dot(placing_rows, columns, preferred_element_type=jnp.float32).astype(jnp.bfloat16)
+        )
+
+    def experts_and_back(row_parts, w_in, w_out, both_gates, base):
+        return combine(both_gates, exchange(expert_rows(row_parts, w_in, w_out)), base)
+
+    def at_once(placing_rows, all_normed, *rest):
+        return experts_and_back([dispatch(placing_rows, all_normed)], *rest)
+
+    def in_two(placing_rows, all_normed, *rest):
+        first = dispatch(placing_rows, all_normed[:, :first_width])
+        columns, first = lax.optimization_barrier((all_normed[:, first_width:], first))
+        return experts_and_back([first, dispatch(placing_rows, columns)], *rest)
+
+    kept, sent = lax.cond(
+        core == 0,
+        at_once,
+        in_two,
+        both_halves(placing),
+        all_normed,
+        w_in[0],
+        w_out[0],
+        both_gates,
+        base,
     )
     return (
         (kept + swap_cores(sent)).astype(jnp.bfloat16).reshape(batch_count, token_rows, model_width)

time: 192 us -> 190 us (0.990); the launches traced: 189 us -> 190 us
  blocking collectives: 55.7 us -> 99.6 us
  waiting for transfers between devices: 75.6 us -> 38.6 us
  starting transfers between devices: 27.9 us -> 21.1 us
    all_to_all x1 -> x2, blocking collectives: 55.7 us -> 99.6 us  [exchange(): lax.all_to_all(rows.reshape(chip_count, slots, width), CHIPS, 0, 0)]
    all_to_all x1, waiting for transfers between devices: 49.4 us -> 11.8 us  [exchange(): lax.all_to_all(rows.reshape(chip_count, slots, width), CHIPS, 0, 0)]
    ppermute x7, starting transfers between devices: 7.34 us -> 3.78 us  [swap_cores(): return lax.ppermute(value, 'core', SWAP)]
    all_to_all x1, starting transfers between devices: 7.83 us -> 4.63 us  [exchange(): lax.all_to_all(rows.reshape(chip_count, slots, width), CHIPS, 0, 0)]
    all_to_all x1, waiting for transfers between devices: 13.7 us -> 16.3 us  [local(): lax.all_to_all(projected.reshape(column_size, chip_rows, model_width), CO...]
    ppermute x7, waiting for transfers between devices: 4.69 us -> 2.16 us  [swap_cores(): return lax.ppermute(value, 'core', SWAP)]
  transfers between devices with their start and end apart: 10 -> 10, of which waited for: 8 -> 5; matrix products, arithmetic and copies ran while one was open for 3% -> 4% of each run, Pallas kernels for 0% -> 3%
where the time goes in v3:
time: 190 us
  blocking collectives  99.6 us (52%)
  waiting for transfers between devices  38.6 us (20%)
  starting transfers between devices  21.1 us (11%)
  Pallas kernels  19.8 us (10%)
  local copies, waits for them, and re-layouts  4.81 us (3%)
  other arithmetic  3.06 us (2%)
  matrix products  2.14 us (1%)
    all_to_all x2, blocking collectives, exchange(): lax.all_to_all(rows.reshape(chip_count, slots, width), CHIPS, 0, 0)  99.6 us
    all_to_all x1, waiting for transfers between devices, local(): lax.all_to_all(projected.reshape(column_size, chip_rows, model_width), CO...  16.3 us
    pallas_call x1, Pallas kernels, expert_rows(): pl.pallas_call(functools.partial(expert_kernel, depths=depths, widths=wid...  13.3 us
    all_to_all x1, waiting for transfers between devices, exchange(): lax.all_to_all(rows.reshape(chip_count, slots, width), CHIPS, 0, 0)  11.8 us
    all_to_all x1, waiting for transfers between devices, local(): lax.all_to_all(jnp.broadcast_to(pair[None], (context_size,) + pair.shape)...  8.37 us
    all_to_all x1, starting transfers between devices, local(): lax.all_to_all(projected.reshape(column_size, chip_rows, model_width), CO...  7.05 us
    all_to_all x1, starting transfers between devices, local(): lax.all_to_all(jnp.broadcast_to(pair[None], (context_size,) + pair.shape)...  5.63 us
    pallas_call x1, Pallas kernels, attend(): pl.pallas_call(attention_kernel, in_specs=[pl.BlockSpec(memory_space=pltp...  4.79 us
  transfers between devices with their start and end apart: 10, of which 5 were waited for; matrix products, arithmetic and copies ran while one was open for 4% of the time, Pallas kernels for 3%

profile of v3, /device:TPU:1, one launch (start us, length us, event | category | flops | bytes accessed | tf_op | source)
XLA Modules:
  0.0 189.6 jit_solution(473392334684176466)
XLA Ops:
  0.0 1.4 collective-permute-start.2
  1.9 0.9 dynamic-slice_bitcast_fusion.2
  3.0 0.9 dynamic-slice_bitcast_fusion.4
  4.4 1.0 constant_dynamic-slice_fusion
  5.4 0.9 broadcast_in_dim.59
  6.3 5.6 %all-to-all-start.5 = ((bf16[8,2,128,128]{3,2,1,0:T(8,128)(2,1)}), bf16[8,2,128,128]{3,2,1,0:T(8,128)(2,1)S(1)}, u32[]{:S(2)}, u32[]{:S(2)}) async-start(bf16[8,2,128,128]{3,2,1,0:T(8,128)(2,1)} %broadcast_in_dim.59), calls=%async_computation.5 | async-start | bytes 1048576 | tf_op jit(solution)/shard_map/all_to_all | solution.py:249
  12.1 0.8 add_select_fusion
  13.8 8.4 %all-to-all-done.5.kv_ref = bf16[8,2,128,128]{3,2,1,0:T(8,128)(2,1)S(1)} async-done(((bf16[8,2,128,128]{3,2,1,0:T(8,128)(2,1)}), bf16[8,2,128,128]{3,2,1,0:T(8,128)(2,1)S(1)}, u32[]{:S(2)}, u32[]{:S(2)}) %all-to-all-start.5) | async-done | bytes 524320 | tf_op jit(solution)/shard_map/all_to_all | solution.py:249
  22.2 4.8 %shard_map.100 = bf16[128,4096]{1,0:T(8,128)(2,1)} custom-call(s32[1]{0:T(128)} %bitcast.14.index_ref, bf16[128,256]{1,0:T(8,128)(2,1)S(1)} %get-tuple-element.54.own_ref, bf16[128,256]{1,0:T(8,128)(2,1)S(1)} %collective-permute-done.1.other_ref, bf16[8,2,128,128]{3,2,1,0:T(8,128)(2,1)S(1)} %all-to-all-done.5.kv_ref, bf16[256,4096]{1,0:T(8,128)(2,1)S(1)} %copy-done, ...), custom_call_target="tpu_custom_call" | custom-call | tf_op jit(solution)/shard_map/pallas_call | solution.py:77
  27.0 7.1 %all-to-all-start.6 = ((bf16[8,16,4096]{2,1,0:T(8,128)(2,1)}), bf16[8,16,4096]{2,1,0:T(8,128)(2,1)S(1)}, u32[]{:S(2)}, u32[]{:S(2)}) async-start(bf16[8,16,4096]{2,1,0:T(8,128)(2,1)} %bitcast.17), calls=%async_computation.6 | async-start | bytes 2097152 | tf_op jit(solution)/shard_map/all_to_all | solution.py:260
  35.0 16.3 %all-to-all-done.6 = bf16[8,16,4096]{2,1,0:T(8,128)(2,1)S(1)} async-done(((bf16[8,16,4096]{2,1,0:T(8,128)(2,1)}), bf16[8,16,4096]{2,1,0:T(8,128)(2,1)S(1)}, u32[]{:S(2)}, u32[]{:S(2)}) %all-to-all-start.6) | async-done | bytes 1048608 | tf_op jit(solution)/shard_map/all_to_all | solution.py:260
  51.9 0.9 collective-permute-start.3
  53.1 0.8 collective-permute-done.3
  53.9 133.4 %conditional.1 = ((f32[16,4096]{1,0:T(8,128)S(1)}, f32[16,4096]{1,0:T(8,128)S(1)})) conditional(s32[]{:T(128)} %convert_element_type.82, (bf16[32,4096]{1,0:T(8,128)(2,1)S(1)}, bf16[512,32]{1,0:T(8,128)(2,1)S(1)}, bf16[4096,1536]{1,0:T(8,128)(2,1)}, bf16[768,4096]{1,0:T(8,128)(2,1)}, bf16[64,512]{1,0:T(8,128)(2,1)S(1)}, ...), branch_computations={%region_6.7_spmd, %region_7.8_spmd} | conditional | flops 136314880 | bytes 47546436 | solution.py:339
  53.9 1.1 fusion.1
  55.0 4.6 %all-to-all-start = ((bf16[64,8,512]{2,1,0:T(8,128)(2,1)}), bf16[64,8,512]{2,1,0:T(8,128)(2,1)S(1)}, u32[]{:S(2)}, u32[]{:S(2)}) async-start(bf16[64,8,512]{2,1,0:T(8,128)(2,1)} %fusion.1), calls=%async_computation | async-start | bytes 1048576 | tf_op jit(solution)/shard_map/cond/branch_0_fun/all_to_all | solution.py:319
  59.7 11.8 %all-to-all-done = bf16[64,8,512]{2,1,0:T(8,128)(2,1)S(1)} async-done(((bf16[64,8,512]{2,1,0:T(8,128)(2,1)}), bf16[64,8,512]{2,1,0:T(8,128)(2,1)S(1)}, u32[]{:S(2)}, u32[]{:S(2)}) %all-to-all-start) | async-done | bytes 524320 | tf_op jit(solution)/shard_map/cond/branch_0_fun/all_to_all | solution.py:319
  71.4 1.1 fusion
  72.5 39.1 %all_to_all.30 = bf16[64,8,3584]{2,1,0:T(8,128)(2,1)} all-to-all(bf16[64,8,3584]{2,1,0:T(8,128)(2,1)S(1)} %fusion), channel_id=1, replica_groups=mesh['zl'=2,'y'=4,'zh'=2,'x'=4,'core'=2] {'zl','y','zh','x'}, dimensions={0} | all-to-all | bytes 7340032 | tf_op jit(solution)/shard_map/cond/branch_0_fun/all_to_all | solution.py:319
  111.6 13.3 %branch_0_fun.2 = bf16[512,4096]{1,0:T(8,128)(2,1)} custom-call(bf16[512,512]{1,0:T(8,128)(2,1)S(1)} %bitcast.92, bf16[512,3584]{1,0:T(8,128)(2,1)} %bitcast.102, bf16[4096,1536]{1,0:T(8,128)(2,1)} %get-tuple-element.34.refs_2_, bf16[768,4096]{1,0:T(8,128)(2,1)S(1)} %copy-done.1), custom_call_target="tpu_custom_call" | custom-call | tf_op jit(solution)/shard_map/cond/branch_0_fun/pallas_call | solution.py:165
  124.9 60.5 %all_to_all.31 = bf16[64,8,4096]{2,1,0:T(8,128)(2,1)S(1)} all-to-all(bf16[64,8,4096]{2,1,0:T(8,128)(2,1)} %bitcast.99), channel_id=1, replica_groups=mesh['zl'=2,'y'=4,'zh'=2,'x'=4,'core'=2] {'zl','y','zh','x'}, dimensions={0} | all-to-all | bytes 8388608 | tf_op jit(solution)/shard_map/cond/branch_0_fun/all_to_all | solution.py:319
  185.4 1.6 branch_0_fun.3
  187.6 1.4 collective-permute-done.6
  188.9 0.7 fusion.10
  (59 shorter events, 4.2 us)
Async XLA Ops:
  0.0 22.2 %copy-start = (bf16[256,4096]{1,0:T(8,128)(2,1)S(1)}, bf16[256,4096]{1,0:T(8,128)(2,1)}, u32[]{:S(2)}) copy-start(bf16[256,4096]{1,0:T(8,128)(2,1)} %proj_ref.1) | copy-start | bytes 6291460
  0.0 22.2 %collective-permute-start.2 = (bf16[256,4096]{1,0:T(8,128)(2,1)}, bf16[256,4096]{1,0:T(8,128)(2,1)}, u32[]{:S(2)}, u32[]{:S(2)}) collective-permute-start(bf16[256,4096]{1,0:T(8,128)(2,1)} %proj_ref.1), channel_id=1, source_target_pairs={{0,1},{1,0},{2,3},{3,2},{4,5},{5,4},{6,7},{7,6},{8,9},{9,8},{10,11... | collective-permute-start | bytes 6291464 | tf_op jit(solution)/shard_map/ppermute | solution.py:23
  1.4 10.7 %collective-permute-start.4 = (s32[2,8,8]{2,1,0:T(8,128)}, s32[2,8,8]{2,1,0:T(8,128)S(1)}, u32[]{:S(2)}, u32[]{:S(2)}) collective-permute-start(s32[2,8,8]{2,1,0:T(8,128)} %param.20), channel_id=1, source_target_pairs={{0,1},{1,0},{2,3},{3,2},{4,5},{5,4},{6,7},{7,6},{8,9},{9,8},{10,11... | collective-permute-start | bytes 1544 | tf_op jit(solution)/shard_map/ppermute | solution.py:23
  1.4 32.6 %collective-permute-start.5 = (f32[2,8,8]{2,1,0:T(8,128)}, f32[2,8,8]{2,1,0:T(8,128)S(1)}, u32[]{:S(2)}, u32[]{:S(2)}) collective-permute-start(f32[2,8,8]{2,1,0:T(8,128)} %param.21), channel_id=1, source_target_pairs={{0,1},{1,0},{2,3},{3,2},{4,5},{5,4},{6,7},{7,6},{8,9},{9,8},{10,11... | collective-permute-start | bytes 1544 | tf_op jit(solution)/shard_map/ppermute | solution.py:23
  2.8 11.0 %collective-permute-start.1 = (bf16[128,256]{1,0:T(8,128)(2,1)S(1)}, bf16[128,256]{1,0:T(8,128)(2,1)S(1)}, u32[]{:S(2)}, u32[]{:S(2)}) collective-permute-start(bf16[128,256]{1,0:T(8,128)(2,1)S(1)} %get-tuple-element.53), channel_id=1, source_target_pairs={{0,1},{1,0},{2,3},{3,2},{4,5},{5,4},{6,7},{7,6},{8,9},{9,8},{10,11... | collective-permute-start | bytes 196616 | tf_op jit(solution)/shard_map/ppermute | solution.py:23
  3.9 47.6 %collective-permute-start = (bf16[8,4096]{1,0:T(8,128)(2,1)S(1)}, bf16[8,4096]{1,0:T(8,128)(2,1)S(1)}, u32[]{:S(2)}, u32[]{:S(2)}) collective-permute-start(bf16[8,4096]{1,0:T(8,128)(2,1)S(1)} %get-tuple-element.51), channel_id=1, source_target_pairs={{0,1},{1,0},{2,3},{3,2},{4,5},{5,4},{6,7},{7,6},{8,9},{9,8},{10,11... | collective-permute-start | bytes 196616 | tf_op jit(solution)/shard_map/ppermute | solution.py:23
  6.3 15.9 %all-to-all-start.5 = ((bf16[8,2,128,128]{3,2,1,0:T(8,128)(2,1)}), bf16[8,2,128,128]{3,2,1,0:T(8,128)(2,1)S(1)}, u32[]{:S(2)}, u32[]{:S(2)}) async-start(bf16[8,2,128,128]{3,2,1,0:T(8,128)(2,1)} %broadcast_in_dim.59), calls=%async_computation.5 | async-start | bytes 1048576 | tf_op jit(solution)/shard_map/all_to_all | solution.py:249
  13.2 20.8 %copy-start.3 = (f32[2,8,8]{2,1,0:T(8,128)S(1)}, f32[2,8,8]{2,1,0:T(8,128)}, u32[]{:S(2)}) copy-start(f32[2,8,8]{2,1,0:T(8,128)} %param.21) | copy-start | bytes 1540
  22.2 29.5 %copy-start.2 = (f32[4096]{0:T(1024)S(1)}, f32[4096]{0:T(1024)}, u32[]{:S(2)}) copy-start(f32[4096]{0:T(1024)} %param.17) | copy-start | bytes 49156
  27.0 24.4 %all-to-all-start.6 = ((bf16[8,16,4096]{2,1,0:T(8,128)(2,1)}), bf16[8,16,4096]{2,1,0:T(8,128)(2,1)S(1)}, u32[]{:S(2)}, u32[]{:S(2)}) async-start(bf16[8,16,4096]{2,1,0:T(8,128)(2,1)} %bitcast.17), calls=%async_computation.6 | async-start | bytes 2097152 | tf_op jit(solution)/shard_map/all_to_all | solution.py:260
  51.9 1.9 %collective-permute-start.3 = (bf16[16,4096]{1,0:T(8,128)(2,1)S(1)}, bf16[16,4096]{1,0:T(8,128)(2,1)S(1)}, u32[]{:S(2)}, u32[]{:S(2)}) collective-permute-start(bf16[16,4096]{1,0:T(8,128)(2,1)S(1)} %multiply_convert_fusion), channel_id=1, source_target_pairs={{0,1},{1,0},{2,3},{3,2},{4,5},{5,4},{6,7},{7,6},{8,9},{9,8},{10,11... | collective-permute-start | bytes 393224 | tf_op jit(solution)/shard_map/ppermute | solution.py:23
  55.0 16.4 %all-to-all-start = ((bf16[64,8,512]{2,1,0:T(8,128)(2,1)}), bf16[64,8,512]{2,1,0:T(8,128)(2,1)S(1)}, u32[]{:S(2)}, u32[]{:S(2)}) async-start(bf16[64,8,512]{2,1,0:T(8,128)(2,1)} %fusion.1), calls=%async_computation | async-start | bytes 1048576 | tf_op jit(solution)/shard_map/cond/branch_0_fun/all_to_all | solution.py:319
  72.5 39.1 %copy-start.1 = (bf16[768,4096]{1,0:T(8,128)(2,1)S(1)}, bf16[768,4096]{1,0:T(8,128)(2,1)}, u32[]{:S(2)}) copy-start(bf16[768,4096]{1,0:T(8,128)(2,1)} %get-tuple-element.35.refs_3_) | copy-start | bytes 18874372 | tf_op jit(solution)/shard_map/cond
  187.3 1.6 collective-permute-start.6

commit v4 on v3

--- a/solution.py
+++ b/solution.py
@@ -1,5 +1,3 @@
-import functools
-
 import jax
 import jax.numpy as jnp
 from jax import lax
@@ -25,7 +23,7 @@
 
 def folded(rows, piece, context_size):
     block_order = jnp.where(rows < BLOCK, piece, 2 * context_size - 1 - piece)
-    return block_order * BLOCK + rows % BLOCK
+    return block_order * BLOCK + (rows & (BLOCK - 1))
 
 
 def attention_kernel(
@@ -42,25 +40,30 @@
     key_count = context_size * row_count
     keys = kv_ref[:, 0].reshape(key_count, HD)
     values = kv_ref[:, 1].reshape(key_count, HD)
-    query_rows = lax.broadcasted_iota(jnp.int32, (row_count, key_count), 0)
-    key_rows = lax.broadcasted_iota(jnp.int32, (row_count, key_count), 1)
+    query_rows = lax.broadcasted_iota(jnp.int32, (row_count, 1), 0)
+    key_rows = lax.broadcasted_iota(jnp.int32, (1, key_count), 1)
     allowed = folded(key_rows % row_count, key_rows // row_count, context_size) <= folded(
         query_rows, index_ref[0], context_size
     )
     heads = []
     for source in (own_ref, other_ref):
-        for head in range(feature_count // HD):
-            query = source[:, head * HD : (head + 1) * HD]
-            scores = lax.dot_general(
-                query, keys, (((1,), (1,)), ((), ())), preferred_element_type=jnp.float32
-            ) * HD ** (-0.5)
-            scores = jnp.where(allowed, scores, masked_score)
-            weights = jnp.exp(scores - jnp.max(scores, axis=-1, keepdims=True))
-            total = jnp.sum(weights, axis=-1, keepdims=True)
-            weighted = jnp.dot(
-                weights.astype(jnp.bfloat16), values, preferred_element_type=jnp.float32
-            )
-            heads.append((weighted / total).astype(jnp.bfloat16))
+        head_count = feature_count // HD
+        query = jnp.concatenate(
+            [source[:, head * HD : (head + 1) * HD] for head in range(head_count)], axis=0
+        )
+        scores = lax.dot_general(
+            query, keys, (((1,), (1,)), ((), ())), preferred_element_type=jnp.float32
+        ) * HD ** (-0.5)
+        scores = jnp.where(
+            allowed[None], scores.reshape(head_count, row_count, key_count), masked_score
+        ).reshape(head_count * row_count, key_count)
+        weights = jnp.exp(scores - jnp.max(scores, axis=-1, keepdims=True))
+        total = jnp.sum(weights, axis=-1, keepdims=True)
+        weighted = jnp.dot(
+            weights.astype(jnp.bfloat16), values, preferred_element_type=jnp.float32
+        )
+        rows = (weighted / total).astype(jnp.bfloat16)
+        heads += [rows[head * row_count : (head + 1) * row_count] for head in range(head_count)]
     attended = jnp.concatenate(heads, axis=1)
     for copy in copies:
         copy.wait()
@@ -87,105 +90,15 @@
     )(context_index, own, other, gathered, out_proj, other_proj)
 
 
-def starts(sizes):
-    return [sum(sizes[:part]) for part in range(len(sizes))]
-
-
-def expert_kernel(*refs, depths, widths, part_widths):
-    row_refs = refs[: len(part_widths)]
-    w_in_ref, w_out_ref, out_ref = refs[len(part_widths) : len(part_widths) + 3]
-    rows, w_in, w_out, mixed, hidden, result, row_sems, in_sems, out_sem, result_sems = refs[
-        len(part_widths) + 3 :
-    ]
-    half_width = w_out_ref.shape[0]
-    pieces = list(zip(starts(depths), depths))
-    row_copies = []
-    for part, (first, size) in enumerate(pieces):
-        holder, base = [
-            (ref, base) for ref, base in zip(row_refs, starts(part_widths)) if base <= first
-        ][-1]
-        row_copies.append(
-            pltpu.make_async_copy(
-                holder.at[:, pl.ds(first - base, size)],
-                rows.at[:, pl.ds(first, size)],
-                row_sems.at[part],
-            )
-        )
-    in_copies = [
-        pltpu.make_async_copy(
-            w_in_ref.at[pl.ds(first, size)], w_in.at[pl.ds(first, size)], in_sems.at[part]
-        )
-        for part, (first, size) in enumerate(pieces)
-    ]
-    out_copy = pltpu.make_async_copy(w_out_ref, w_out, out_sem)
-    for part in range(len(pieces)):
-        row_copies[part].start()
-        in_copies[part].start()
-    out_copy.start()
-    for part, (first, size) in enumerate(pieces):
-        row_copies[part].wait()
-        in_copies[part].wait()
-        product = jnp.dot(
-            rows[:, first : first + size],
-            w_in[first : first + size, :],
-            preferred_element_type=jnp.float32,
-        )
-        if part == 0:
-            mixed[...] = product
-        elif part < len(pieces) - 1:
-            mixed[...] += product
-        else:
-            total = mixed[...] + product
-            gate = total[:, :half_width]
-            hidden[...] = (gate / (1.0 + jnp.exp(-gate)) * total[:, half_width:]).astype(
-                jnp.bfloat16
-            )
-    out_copy.wait()
-    result_copies = []
-    for part, (first, size) in enumerate(zip(starts(widths), widths)):
-        columns = pl.ds(first, size)
-        result[:, columns] = jnp.dot(
-            hidden[...], w_out[:, columns], preferred_element_type=jnp.float32
-        ).astype(jnp.bfloat16)
-        copy = pltpu.make_async_copy(
-            result.at[:, columns], out_ref.at[:, columns], result_sems.at[part]
-        )
-        copy.start()
-        result_copies.append(copy)
-    for copy in result_copies:
-        copy.wait()
-
-
-def expert_rows(row_parts, w_in, w_out):
-    row_count = row_parts[0].shape[0]
+def expert_rows(rows, w_in, w_out, started=None):
     half_width, model_width = w_out.shape
-    depths = tuple(model_width * part // 16 for part in (2, 4, 5, 5))
-    widths = (model_width // 8,) * 8
-    apart = pl.BlockSpec(memory_space=pl.ANY)
-    return pl.pallas_call(
-        functools.partial(
-            expert_kernel,
-            depths=depths,
-            widths=widths,
-            part_widths=tuple(part.shape[1] for part in row_parts),
-        ),
-        in_specs=[apart] * (len(row_parts) + 2),
-        out_specs=apart,
-        out_shape=jax.ShapeDtypeStruct((row_count, model_width), jnp.bfloat16),
-        scratch_shapes=[
-            pltpu.VMEM((row_count, model_width), jnp.bfloat16),
-            pltpu.VMEM((model_width, 2 * half_width), jnp.bfloat16),
-            pltpu.VMEM((half_width, model_width), jnp.bfloat16),
-            pltpu.VMEM((row_count, 2 * half_width), jnp.float32),
-            pltpu.VMEM((row_count, half_width), jnp.bfloat16),
-            pltpu.VMEM((row_count, model_width), jnp.bfloat16),
-            pltpu.SemaphoreType.DMA((len(depths),)),
-            pltpu.SemaphoreType.DMA((len(depths),)),
-            pltpu.SemaphoreType.DMA,
-            pltpu.SemaphoreType.DMA((len(widths),)),
-        ],
-        compiler_params=pltpu.CompilerParams(vmem_limit_bytes=52 * 2**20),
-    )(*row_parts, w_in, w_out)
+    mixed = jnp.dot(
+        rows, w_in[model_width - rows.shape[1] :], preferred_element_type=jnp.float32
+    )
+    if started is not None:
+        mixed = mixed + started
+    hidden = (jax.nn.silu(mixed[:, :half_width]) * mixed[:, half_width:]).astype(jnp.bfloat16)
+    return jnp.dot(hidden, w_out, preferred_element_type=jnp.float32).astype(jnp.bfloat16)
 
 
 def combine_kernel(gates_ref, returned_ref, base_ref, kept_ref, sent_ref):
@@ -232,9 +145,17 @@
     def of_batch(value, index):
         return lax.dynamic_index_in_dim(value, index, 0, keepdims=False)
 
-    other_queries = swap_cores(of_batch(queries, 1 - core))
+    kv_head = lax.axis_index(COLUMN) * 2 * heads_here // (QH // KVH)
+    pair = jnp.stack([of_batch(keys, core), of_batch(values, core)])
+    pair = lax.dynamic_slice_in_dim(pair, kv_head * HD, HD, 2)
+    spread = jnp.broadcast_to(pair[None], (context_size,) + pair.shape)
+    spread, queries, out_proj, residual, expert_ids, gate_weights = lax.optimization_barrier(
+        (spread, queries, out_proj, residual, expert_ids, gate_weights)
+    )
+    gathered = lax.all_to_all(spread, CONTEXT, 0, 0)
+    other_queries = of_batch(swap_cores(queries), core)
     other_proj = swap_cores(out_proj)
-    other_residual = swap_cores(of_batch(residual, 1 - core))
+    other_residual = of_batch(swap_cores(residual), core)
     other_ids = swap_cores(expert_ids)
     other_gates = swap_cores(gate_weights)
 
@@ -243,12 +164,6 @@
         flipped = jnp.stack([other, own], axis=axis)
         return jnp.where(core == 0, stacked, flipped)
 
-    kv_head = lax.axis_index(COLUMN) * 2 * heads_here // (QH // KVH)
-    pair = jnp.stack([of_batch(keys, core), of_batch(values, core)])
-    pair = lax.dynamic_slice_in_dim(pair, kv_head * HD, HD, 2)
-    gathered = lax.all_to_all(
-        jnp.broadcast_to(pair[None], (context_size,) + pair.shape), CONTEXT, 0, 0
-    )
     projected = attend(
         lax.axis_index(CONTEXT).astype(jnp.int32).reshape(1),
         of_batch(queries, core),
@@ -312,7 +227,7 @@
     ).reshape(tokens, model_width)
     both_gates = jnp.concatenate([gate_high, gate_low])
     base = kept_first(own_sum)
-    first_width = model_width // 8
+    first_width = 1024
 
     def exchange(rows):
         width = rows.shape[1]
@@ -320,21 +235,24 @@
             chip_count * slots, width
         )
 
-    def dispatch(placing_rows, columns):
-        return exchange(
-            jnp.dot(placing_rows, columns, preferred_element_type=jnp.float32).astype(jnp.bfloat16)
-        )
-
-    def experts_and_back(row_parts, w_in, w_out, both_gates, base):
-        return combine(both_gates, exchange(expert_rows(row_parts, w_in, w_out)), base)
-
-    def at_once(placing_rows, all_normed, *rest):
-        return experts_and_back([dispatch(placing_rows, all_normed)], *rest)
-
-    def in_two(placing_rows, all_normed, *rest):
-        first = dispatch(placing_rows, all_normed[:, :first_width])
-        columns, first = lax.optimization_barrier((all_normed[:, first_width:], first))
-        return experts_and_back([first, dispatch(placing_rows, columns)], *rest)
+    def place(placing_rows, columns):
+        return jnp.dot(placing_rows, columns, preferred_element_type=jnp.float32).astype(
+            jnp.bfloat16
+        )
+
+    def at_once(placing_rows, all_normed, w_in, w_out, both_gates, base):
+        partial_value = expert_rows(exchange(place(placing_rows, all_normed)), w_in, w_out)
+        return combine(both_gates, exchange(partial_value), base)
+
+    def in_two(placing_rows, all_normed, w_in, w_out, both_gates, base):
+        first = exchange(place(placing_rows, all_normed[:, :first_width]))
+        started = jnp.dot(first, w_in[:first_width], preferred_element_type=jnp.float32)
+        outgoing, started = lax.optimization_barrier(
+            (place(placing_rows, all_normed[:, first_width:]), started)
+        )
+        second = exchange(outgoing)
+        partial_value = expert_rows(second, w_in, w_out, started)
+        return combine(both_gates, exchange(partial_value), base)
 
     kept, sent = lax.cond(
         core == 0,

time: 190 us -> 167 us (0.88)
  blocking collectives: 99.6 us -> 69.2 us
  matrix products: 2.14 us -> 18.9 us
  Pallas kernels: 19.8 us -> 5.92 us
    all_to_all x2, blocking collectives: 99.6 us -> 69.2 us  [exchange(): lax.all_to_all(rows.reshape(chip_count, slots, width), CHIPS, 0, 0)]
    dot_general x2 -> x5, matrix products: 2.14 us -> 18.9 us  [the longest x1 7.06 us: expert_rows(): jnp.dot(rows, w_in[model_width - rows.shape[1]:], preferred_element_type=...]
    pallas_call x1 -> x0, Pallas kernels: 13.3 us -> none  [expert_rows(): pl.pallas_call(functools.partial(expert_kernel, depths=depths, widths=wid...]
    all_to_all x1, waiting for transfers between devices: 11.8 us -> 17.6 us  [exchange(): lax.all_to_all(rows.reshape(chip_count, slots, width), CHIPS, 0, 0)]
    all_to_all x1, waiting for transfers between devices: 8.37 us -> 5.06 us  [local(): gathered = lax.all_to_all(spread, CONTEXT, 0, 0)]
  transfers between devices with their start and end apart: 10 -> 10, of which waited for: 5 -> 4; matrix products, arithmetic and copies ran while one was open for 4% -> 4% of each run, Pallas kernels for 3% -> 3%
where the time goes in v4:
time: 167 us; the launch traced here: 166 us
  blocking collectives  69.2 us (41%)
  waiting for transfers between devices  40.5 us (24%)
  starting transfers between devices  21.7 us (13%)
  matrix products  18.9 us (11%)
  Pallas kernels  5.92 us (4%)
  local copies, waits for them, and re-layouts  4.9 us (3%)
  other arithmetic  4.5 us (3%)
    all_to_all x2, blocking collectives, exchange(): lax.all_to_all(rows.reshape(chip_count, slots, width), CHIPS, 0, 0)  69.2 us
    all_to_all x1, waiting for transfers between devices, exchange(): lax.all_to_all(rows.reshape(chip_count, slots, width), CHIPS, 0, 0)  17.6 us
    all_to_all x1, waiting for transfers between devices, local(): lax.all_to_all(projected.reshape(column_size, chip_rows, model_width), CO...  16.3 us
    dot_general x1, matrix products, expert_rows(): jnp.dot(rows, w_in[model_width - rows.shape[1]:], preferred_element_type=...  7.06 us
    all_to_all x1, starting transfers between devices, local(): lax.all_to_all(projected.reshape(column_size, chip_rows, model_width), CO...  7.05 us
    dot_general x1, matrix products, in_two(): jnp.dot(first, w_in[:first_width], preferred_element_type=jnp.float32)  5.8 us
    all_to_all x1, starting transfers between devices, local(): gathered = lax.all_to_all(spread, CONTEXT, 0, 0)  5.63 us
    all_to_all x1, starting transfers between devices, exchange(): lax.all_to_all(rows.reshape(chip_count, slots, width), CHIPS, 0, 0)  5.51 us
  transfers between devices with their start and end apart: 10, of which 4 were waited for; matrix products, arithmetic and copies ran while one was open for 4% of the time, Pallas kernels for 3%

profile of v4, /device:TPU:1, one launch (start us, length us, event | category | flops | bytes accessed | tf_op | source)
XLA Modules:
  0.0 166.1 jit_solution(17612703532105605489)
XLA Ops:
  0.0 1.1 constant_dynamic-slice_fusion.2
  1.2 0.9 broadcast_in_dim.59
  2.1 1.4 collective-permute-start.2
  3.5 5.6 %all-to-all-start.5 = ((bf16[8,2,128,128]{3,2,1,0:T(8,128)(2,1)}), bf16[8,2,128,128]{3,2,1,0:T(8,128)(2,1)S(1)}, u32[]{:S(2)}, u32[]{:S(2)}) async-start(bf16[8,2,128,128]{3,2,1,0:T(8,128)(2,1)} %broadcast_in_dim.59), calls=%async_computation.5 | async-start | bytes 1048576 | tf_op jit(solution)/shard_map/all_to_all | solution.py:155
  10.1 0.8 dynamic-slice_bitcast_fusion.3.own_ref
  11.0 0.8 constant_dynamic-slice_fusion.1
  14.3 5.1 %all-to-all-done.5.kv_ref = bf16[8,2,128,128]{3,2,1,0:T(8,128)(2,1)S(1)} async-done(((bf16[8,2,128,128]{3,2,1,0:T(8,128)(2,1)}), bf16[8,2,128,128]{3,2,1,0:T(8,128)(2,1)S(1)}, u32[]{:S(2)}, u32[]{:S(2)}) %all-to-all-start.5) | async-done | bytes 524320 | tf_op jit(solution)/shard_map/all_to_all | solution.py:155
  19.4 4.3 %shard_map.100 = bf16[128,4096]{1,0:T(8,128)(2,1)} custom-call(s32[1]{0:T(128)} %bitcast.11.index_ref, bf16[128,256]{1,0:T(8,128)(2,1)S(1)} %dynamic-slice_bitcast_fusion.3.own_ref, bf16[128,256]{1,0:T(8,128)(2,1)S(1)} %dynamic-slice_bitcast_fusion.2.other_ref, bf16[8,2,128,128]{3,2,1,0:T(8,128)(2,1)S(1)} %all-to-all-done.5.kv_ref, ...), custom_call_target="tpu_custom_call" | custom-call | tf_op jit(solution)/shard_map/pallas_call | solution.py:80
  23.7 7.0 %all-to-all-start.6 = ((bf16[8,16,4096]{2,1,0:T(8,128)(2,1)}), bf16[8,16,4096]{2,1,0:T(8,128)(2,1)S(1)}, u32[]{:S(2)}, u32[]{:S(2)}) async-start(bf16[8,16,4096]{2,1,0:T(8,128)(2,1)} %bitcast.14), calls=%async_computation.6 | async-start | bytes 2097152 | tf_op jit(solution)/shard_map/all_to_all | solution.py:175
  31.7 16.3 %all-to-all-done.6 = bf16[8,16,4096]{2,1,0:T(8,128)(2,1)S(1)} async-done(((bf16[8,16,4096]{2,1,0:T(8,128)(2,1)}), bf16[8,16,4096]{2,1,0:T(8,128)(2,1)S(1)}, u32[]{:S(2)}, u32[]{:S(2)}) %all-to-all-start.6) | async-done | bytes 1048608 | tf_op jit(solution)/shard_map/all_to_all | solution.py:175
  48.6 0.9 collective-permute-start.3
  49.7 0.8 pad_maximum_fusion
  50.6 113.2 %conditional.1 = ((f32[16,4096]{1,0:T(8,128)S(1)}, f32[16,4096]{1,0:T(8,128)S(1)})) conditional(s32[]{:T(128)} %convert_element_type.91, (bf16[32,4096]{1,0:T(8,128)(2,1)S(1)}, bf16[512,32]{1,0:T(8,128)(2,1)S(1)}, bf16[4096,1536]{1,0:T(8,128)(2,1)}, bf16[768,4096]{1,0:T(8,128)(2,1)}, bf16[64,512]{1,0:T(8,128)(2,1)}, ...), branch_computations={%region_6.7_spmd, %region_7.8_spmd} | conditional | flops 9805234176 | bytes 133955760 | solution.py:257
  50.7 1.4 fusion.10
  52.1 5.5 %all-to-all-start = ((bf16[64,8,1024]{2,1,0:T(8,128)(2,1)}), bf16[64,8,1024]{2,1,0:T(8,128)(2,1)}, u32[]{:S(2)}, u32[]{:S(2)}) async-start(bf16[64,8,1024]{2,1,0:T(8,128)(2,1)} %fusion.10), calls=%async_computation | async-start | bytes 2097152 | tf_op jit(solution)/shard_map/cond/branch_0_fun/all_to_all | solution.py:234
  57.6 1.0 convolution_convert_fusion.1
  58.5 17.6 %all-to-all-done = bf16[64,8,1024]{2,1,0:T(8,128)(2,1)} async-done(((bf16[64,8,1024]{2,1,0:T(8,128)(2,1)}), bf16[64,8,1024]{2,1,0:T(8,128)(2,1)}, u32[]{:S(2)}, u32[]{:S(2)}) %all-to-all-start) | async-done | bytes 1048608 | tf_op jit(solution)/shard_map/cond/branch_0_fun/all_to_all | solution.py:234
  76.1 5.8 %fusion.7 = f32[512,1536]{1,0:T(8,128)} fusion(bf16[4096,1536]{1,0:T(8,128)(2,1)} %get-tuple-element.32, bf16[64,8,1024]{2,1,0:T(8,128)(2,1)} %all-to-all-done), kind=kOutput, calls=%fused_computation.7 | convolution fusion | flops 1610612736 | bytes 7340032 | tf_op jit(solution)/shard_map/cond/branch_0_fun/dot_general | solution.py:249
  81.9 32.2 %all_to_all.30 = bf16[64,8,3072]{2,1,0:T(8,128)(2,1)S(1)} all-to-all(bf16[64,8,3072]{2,1,0:T(8,128)(2,1)S(1)} %bitcast.96), channel_id=1, replica_groups=mesh['zl'=2,'y'=4,'zh'=2,'x'=4,'core'=2] {'zl','y','zh','x'}, dimensions={0} | all-to-all | bytes 6291456 | tf_op jit(solution)/shard_map/cond/branch_0_fun/all_to_all | solution.py:234
  114.1 7.1 %fusion.3 = f32[512,1536]{1,0:T(8,128)S(1)} fusion(f32[512,1536]{1,0:T(8,128)} %fusion.7, bf16[4096,1536]{1,0:T(8,128)(2,1)S(1)} %copy-done.7, bf16[64,8,3072]{2,1,0:T(8,128)(2,1)S(1)} %all_to_all.30), kind=kOutput, calls=%fused_computation.5 | convolution fusion | flops 4832624640 | bytes 18874368 | tf_op jit(solution)/shard_map/cond/branch_0_fun/dot_general | solution.py:95
  121.2 3.7 %fusion.2 = bf16[64,8,4096]{2,1,0:T(8,128)(2,1)S(1)} fusion(bf16[768,4096]{1,0:T(8,128)(2,1)S(1)} %bitcast.116, f32[512,1536]{1,0:T(8,128)S(1)} %fusion.3), kind=kOutput, calls=%fused_computation.3 | convolution fusion | flops 3225681920 | bytes 13631488 | tf_op jit(solution)/shard_map/cond/branch_0_fun/dot_general | solution.py:101
  125.0 37.0 %all_to_all.31 = bf16[64,8,4096]{2,1,0:T(8,128)(2,1)S(1)} all-to-all(bf16[64,8,4096]{2,1,0:T(8,128)(2,1)S(1)} %fusion.2), channel_id=1, replica_groups=mesh['zl'=2,'y'=4,'zh'=2,'x'=4,'core'=2] {'zl','y','zh','x'}, dimensions={0} | all-to-all | bytes 8388608 | tf_op jit(solution)/shard_map/cond/branch_0_fun/all_to_all | solution.py:234
  162.0 1.6 branch_0_fun.1
  163.9 1.5 collective-permute-done.6
  (71 shorter events, 6.0 us)
Async XLA Ops:
  0.0 13.7 %copy-start.6 = (f32[2,8,8]{2,1,0:T(8,128)S(1)}, f32[2,8,8]{2,1,0:T(8,128)}, u32[]{:S(2)}) copy-start(f32[2,8,8]{2,1,0:T(8,128)} %param.21) | copy-start | bytes 1540
  0.0 19.4 %copy-start = (bf16[256,4096]{1,0:T(8,128)(2,1)S(1)}, bf16[256,4096]{1,0:T(8,128)(2,1)}, u32[]{:S(2)}) copy-start(bf16[256,4096]{1,0:T(8,128)(2,1)} %proj_ref) | copy-start | bytes 6291460
  2.1 17.3 %collective-permute-start.2 = (bf16[256,4096]{1,0:T(8,128)(2,1)}, bf16[256,4096]{1,0:T(8,128)(2,1)}, u32[]{:S(2)}, u32[]{:S(2)}) collective-permute-start(bf16[256,4096]{1,0:T(8,128)(2,1)} %proj_ref), channel_id=1, source_target_pairs={{0,1},{1,0},{2,3},{3,2},{4,5},{5,4},{6,7},{7,6},{8,9},{9,8},{10,11... | collective-permute-start | bytes 6291464 | tf_op jit(solution)/shard_map/ppermute | solution.py:21
  3.5 15.9 %all-to-all-start.5 = ((bf16[8,2,128,128]{3,2,1,0:T(8,128)(2,1)}), bf16[8,2,128,128]{3,2,1,0:T(8,128)(2,1)S(1)}, u32[]{:S(2)}, u32[]{:S(2)}) async-start(bf16[8,2,128,128]{3,2,1,0:T(8,128)(2,1)} %broadcast_in_dim.59), calls=%async_computation.5 | async-start | bytes 1048576 | tf_op jit(solution)/shard_map/all_to_all | solution.py:155
  9.1 2.9 %collective-permute-start.4 = (s32[2,8,8]{2,1,0:T(8,128)}, s32[2,8,8]{2,1,0:T(8,128)S(1)}, u32[]{:S(2)}, u32[]{:S(2)}) collective-permute-start(s32[2,8,8]{2,1,0:T(8,128)} %param.20), channel_id=1, source_target_pairs={{0,1},{1,0},{2,3},{3,2},{4,5},{5,4},{6,7},{7,6},{8,9},{9,8},{10,11... | collective-permute-start | bytes 1544 | tf_op jit(solution)/shard_map/ppermute | solution.py:21
  9.4 4.3 %collective-permute-start.5 = (f32[2,8,8]{2,1,0:T(8,128)}, f32[2,8,8]{2,1,0:T(8,128)S(1)}, u32[]{:S(2)}, u32[]{:S(2)}) collective-permute-start(f32[2,8,8]{2,1,0:T(8,128)} %param.21), channel_id=1, source_target_pairs={{0,1},{1,0},{2,3},{3,2},{4,5},{5,4},{6,7},{7,6},{8,9},{9,8},{10,11... | collective-permute-start | bytes 1544 | tf_op jit(solution)/shard_map/ppermute | solution.py:21
  9.6 22.1 %collective-permute-start = (bf16[2,8,4096]{2,1,0:T(8,128)(2,1)}, bf16[2,8,4096]{2,1,0:T(8,128)(2,1)S(1)}, u32[]{:S(2)}, u32[]{:S(2)}) collective-permute-start(bf16[2,8,4096]{2,1,0:T(8,128)(2,1)} %param.16), channel_id=1, source_target_pairs={{0,1},{1,0},{2,3},{3,2},{4,5},{5,4},{6,7},{7,6},{8,9},{9,8},{10,11... | collective-permute-start | bytes 393224 | tf_op jit(solution)/shard_map/ppermute | solution.py:21
  9.9 4.4 %collective-permute-start.1 = (bf16[2,128,256]{2,1,0:T(8,128)(2,1)}, bf16[2,128,256]{2,1,0:T(8,128)(2,1)S(1)}, u32[]{:S(2)}, u32[]{:S(2)}) collective-permute-start(bf16[2,128,256]{2,1,0:T(8,128)(2,1)} %param.12), channel_id=1, source_target_pairs={{0,1},{1,0},{2,3},{3,2},{4,5},{5,4},{6,7},{7,6},{8,9},{9,8},{10,11... | collective-permute-start | bytes 393224 | tf_op jit(solution)/shard_map/ppermute | solution.py:21
  23.7 24.7 %copy-start.5 = (f32[4096]{0:T(1024)S(1)}, f32[4096]{0:T(1024)}, u32[]{:S(2)}) copy-start(f32[4096]{0:T(1024)} %param.17) | copy-start | bytes 49156
  23.7 24.4 %all-to-all-start.6 = ((bf16[8,16,4096]{2,1,0:T(8,128)(2,1)}), bf16[8,16,4096]{2,1,0:T(8,128)(2,1)S(1)}, u32[]{:S(2)}, u32[]{:S(2)}) async-start(bf16[8,16,4096]{2,1,0:T(8,128)(2,1)} %bitcast.14), calls=%async_computation.6 | async-start | bytes 2097152 | tf_op jit(solution)/shard_map/all_to_all | solution.py:175
  48.6 1.9 %collective-permute-start.3 = (bf16[16,4096]{1,0:T(8,128)(2,1)S(1)}, bf16[16,4096]{1,0:T(8,128)(2,1)S(1)}, u32[]{:S(2)}, u32[]{:S(2)}) collective-permute-start(bf16[16,4096]{1,0:T(8,128)(2,1)S(1)} %multiply_convert_fusion), channel_id=1, source_target_pairs={{0,1},{1,0},{2,3},{3,2},{4,5},{5,4},{6,7},{7,6},{8,9},{9,8},{10,11... | collective-permute-start | bytes 393224 | tf_op jit(solution)/shard_map/ppermute | solution.py:21
  52.1 24.1 %all-to-all-start = ((bf16[64,8,1024]{2,1,0:T(8,128)(2,1)}), bf16[64,8,1024]{2,1,0:T(8,128)(2,1)}, u32[]{:S(2)}, u32[]{:S(2)}) async-start(bf16[64,8,1024]{2,1,0:T(8,128)(2,1)} %fusion.10), calls=%async_computation | async-start | bytes 2097152 | tf_op jit(solution)/shard_map/cond/branch_0_fun/all_to_all | solution.py:234
  76.1 38.0 %copy-start.7 = (bf16[4096,1536]{1,0:T(8,128)(2,1)S(1)}, bf16[4096,1536]{1,0:T(8,128)(2,1)}, u32[]{:S(2)}) copy-start(bf16[4096,1536]{1,0:T(8,128)(2,1)} %get-tuple-element.32) | copy-start | bytes 37748740 | tf_op jit(solution)/shard_map/cond
  81.9 39.3 %slice-start = ((s8[6291456]{0:T(1024)(128)(4,1)}), s8[4194304]{0:T(1024)(128)(4,1)S(1)}, s32[]{:S(2)}) async-start(s8[6291456]{0:T(1024)(128)(4,1)} %bitcast.115), calls=%async_computation.7 | async-start | bytes 8388608 | tf_op jit(solution)/shard_map/cond
  114.1 7.1 %slice-start.1 = ((s8[6291456]{0:T(1024)(128)(4,1)}), s8[2097152]{0:T(1024)(128)(4,1)S(1)}, s32[]{:S(2)}) async-start(s8[6291456]{0:T(1024)(128)(4,1)} %bitcast.115), calls=%async_computation.8 | async-start | bytes 4194304 | tf_op jit(solution)/shard_map/cond
  124.9 37.0 %copy-start.1 = (f32[32,4096]{1,0:T(8,128)S(1)}, f32[32,4096]{1,0:T(8,128)}, u32[]{:S(2)}) copy-start(f32[32,4096]{1,0:T(8,128)} %get-tuple-element.36.base_ref) | copy-start | bytes 1572868 | tf_op jit(solution)/shard_map/cond
  125.0 37.0 %copy-start.3 = (bf16[64,512]{1,0:T(8,128)(2,1)S(1)}, bf16[64,512]{1,0:T(8,128)(2,1)}, u32[]{:S(2)}) copy-start(bf16[64,512]{1,0:T(8,128)(2,1)} %get-tuple-element.29.gates_ref) | copy-start | bytes 196612 | tf_op jit(solution)/shard_map/cond
  163.8 1.6 collective-permute-start.6

commit v5 on v4

--- a/solution.py
+++ b/solution.py
@@ -106,14 +106,14 @@
     summed = jnp.dot(gates_ref[...], returned_ref[...], preferred_element_type=jnp.float32)
     total = summed[:token_count] + summed[token_count:] + base_ref[...]
     kept_ref[...] = total[: token_count // 2]
-    sent_ref[...] = total[token_count // 2 :]
+    sent_ref[...] = total[token_count // 2 :].astype(sent_ref.dtype)
 
 
 def combine(gates, returned, base):
     slot_count, model_width = returned.shape
     token_count = base.shape[0]
     width = model_width // 4
-    half = jax.ShapeDtypeStruct((token_count // 2, model_width), jnp.float32)
+    half = (token_count // 2, model_width)
     columns = lambda rows: pl.BlockSpec((rows, width), lambda step: (0, step))
     return pl.pallas_call(
         combine_kernel,
@@ -124,7 +124,10 @@
             columns(token_count),
         ],
         out_specs=[columns(token_count // 2), columns(token_count // 2)],
-        out_shape=[half, half],
+        out_shape=[
+            jax.ShapeDtypeStruct(half, jnp.float32),
+            jax.ShapeDtypeStruct(half, jnp.bfloat16),
+        ],
         compiler_params=pltpu.CompilerParams(vmem_limit_bytes=32 * 2**20),
     )(gates, returned, base)
 
@@ -146,8 +149,12 @@
         return lax.dynamic_index_in_dim(value, index, 0, keepdims=False)
 
     kv_head = lax.axis_index(COLUMN) * 2 * heads_here // (QH // KVH)
-    pair = jnp.stack([of_batch(keys, core), of_batch(values, core)])
-    pair = lax.dynamic_slice_in_dim(pair, kv_head * HD, HD, 2)
+    pair = jnp.concatenate(
+        [
+            lax.dynamic_slice(value, (core, 0, kv_head * HD), (1, row_count, HD))
+            for value in (keys, values)
+        ]
+    )
     spread = jnp.broadcast_to(pair[None], (context_size,) + pair.shape)
     spread, queries, out_proj, residual, expert_ids, gate_weights = lax.optimization_barrier(
         (spread, queries, out_proj, residual, expert_ids, gate_weights)
@@ -227,7 +234,7 @@
     ).reshape(tokens, model_width)
     both_gates = jnp.concatenate([gate_high, gate_low])
     base = kept_first(own_sum)
-    first_width = 1024
+    first_width = model_width // 4
 
     def exchange(rows):
         width = rows.shape[1]
@@ -266,7 +273,7 @@
         base,
     )
     return (
-        (kept + swap_cores(sent)).astype(jnp.bfloat16).reshape(batch_count, token_rows, model_width)
+        (kept + swap_cores(sent).astype(jnp.float32)).astype(jnp.bfloat16).reshape(batch_count, token_rows, model_width)
     )
 
 

time: 167 us -> 166 us (level)
  transfers between devices with their start and end apart: 10 -> 10, of which waited for: 4 -> 4; matrix products, arithmetic and copies ran while one was open for 4% -> 5% of each run, Pallas kernels for 3% -> 3%
where the time goes in v5:
time: 166 us
  blocking collectives  69.2 us (42%)
  waiting for transfers between devices  39.6 us (24%)
  starting transfers between devices  21.7 us (13%)
  matrix products  18.9 us (11%)
  Pallas kernels  5.89 us (4%)
  other arithmetic  5.24 us (3%)
  local copies, waits for them, and re-layouts  4.7 us (3%)
    all_to_all x2, blocking collectives, exchange(): lax.all_to_all(rows.reshape(chip_count, slots, width), CHIPS, 0, 0)  69.2 us
    all_to_all x1, waiting for transfers between devices, exchange(): lax.all_to_all(rows.reshape(chip_count, slots, width), CHIPS, 0, 0)  17.6 us
    all_to_all x1, waiting for transfers between devices, local(): lax.all_to_all(projected.reshape(column_size, chip_rows, model_width), CO...  16.3 us
    dot_general x1, matrix products, expert_rows(): jnp.dot(rows, w_in[model_width - rows.shape[1]:], preferred_element_type=...  7.06 us
    all_to_all x1, starting transfers between devices, local(): lax.all_to_all(projected.reshape(column_size, chip_rows, model_width), CO...  7.05 us
    dot_general x1, matrix products, in_two(): jnp.dot(first, w_in[:first_width], preferred_element_type=jnp.float32)  5.79 us
    all_to_all x1, starting transfers between devices, local(): gathered = lax.all_to_all(spread, CONTEXT, 0, 0)  5.63 us
    all_to_all x1, starting transfers between devices, exchange(): lax.all_to_all(rows.reshape(chip_count, slots, width), CHIPS, 0, 0)  5.52 us
  transfers between devices with their start and end apart: 10, of which 4 were waited for; matrix products, arithmetic and copies ran while one was open for 5% of the time, Pallas kernels for 3%

profile of v5, /device:TPU:1, one launch (start us, length us, event | category | flops | bytes accessed | tf_op | source)
XLA Modules:
  0.0 165.7 jit_solution(15836286685341478045)
XLA Ops:
  0.0 0.9 constant_dynamic-slice_fusion.2
  0.9 0.9 broadcast_in_dim.59
  1.8 1.4 collective-permute-start.2
  3.3 5.6 %all-to-all-start.5 = ((bf16[8,2,128,128]{3,2,1,0:T(8,128)(2,1)}), bf16[8,2,128,128]{3,2,1,0:T(8,128)(2,1)S(1)}, u32[]{:S(2)}, u32[]{:S(2)}) async-start(bf16[8,2,128,128]{3,2,1,0:T(8,128)(2,1)} %broadcast_in_dim.59), calls=%async_computation.5 | async-start | bytes 1048576 | tf_op jit(solution)/shard_map/all_to_all | solution.py:162
  9.9 0.8 dynamic-slice_bitcast_fusion.3.own_ref
  10.8 0.8 constant_dynamic-slice_fusion.1
  14.9 4.3 %all-to-all-done.5.kv_ref = bf16[8,2,128,128]{3,2,1,0:T(8,128)(2,1)S(1)} async-done(((bf16[8,2,128,128]{3,2,1,0:T(8,128)(2,1)}), bf16[8,2,128,128]{3,2,1,0:T(8,128)(2,1)S(1)}, u32[]{:S(2)}, u32[]{:S(2)}) %all-to-all-start.5) | async-done | bytes 524320 | tf_op jit(solution)/shard_map/all_to_all | solution.py:162
  19.2 4.3 %shard_map.100 = bf16[128,4096]{1,0:T(8,128)(2,1)} custom-call(s32[1]{0:T(128)} %bitcast.11.index_ref, bf16[128,256]{1,0:T(8,128)(2,1)S(1)} %dynamic-slice_bitcast_fusion.3.own_ref, bf16[128,256]{1,0:T(8,128)(2,1)S(1)} %dynamic-slice_bitcast_fusion.2.other_ref, bf16[8,2,128,128]{3,2,1,0:T(8,128)(2,1)S(1)} %all-to-all-done.5.kv_ref, ...), custom_call_target="tpu_custom_call" | custom-call | tf_op jit(solution)/shard_map/pallas_call | solution.py:80
  23.5 7.1 %all-to-all-start.6 = ((bf16[8,16,4096]{2,1,0:T(8,128)(2,1)}), bf16[8,16,4096]{2,1,0:T(8,128)(2,1)S(1)}, u32[]{:S(2)}, u32[]{:S(2)}) async-start(bf16[8,16,4096]{2,1,0:T(8,128)(2,1)} %bitcast.14), calls=%async_computation.6 | async-start | bytes 2097152 | tf_op jit(solution)/shard_map/all_to_all | solution.py:182
  31.5 16.3 %all-to-all-done.6 = bf16[8,16,4096]{2,1,0:T(8,128)(2,1)S(1)} async-done(((bf16[8,16,4096]{2,1,0:T(8,128)(2,1)}), bf16[8,16,4096]{2,1,0:T(8,128)(2,1)S(1)}, u32[]{:S(2)}, u32[]{:S(2)}) %all-to-all-start.6) | async-done | bytes 1048608 | tf_op jit(solution)/shard_map/all_to_all | solution.py:182
  48.4 0.9 collective-permute-start.3
  49.5 0.8 pad_maximum_fusion
  50.4 113.2 %conditional.1 = ((f32[16,4096]{1,0:T(8,128)S(1)}, bf16[16,4096]{1,0:T(8,128)(2,1)S(1)})) conditional(s32[]{:T(128)} %convert_element_type.94, (bf16[32,4096]{1,0:T(8,128)(2,1)S(1)}, bf16[512,32]{1,0:T(8,128)(2,1)S(1)}, bf16[4096,1536]{1,0:T(8,128)(2,1)}, bf16[768,4096]{1,0:T(8,128)(2,1)}, bf16[64,512]{1,0:T(8,128)(2,1)}, ...), branch_computations={%region_6.7_spmd, %region_7.8_spmd} | conditional | flops 9805234176 | bytes 133955760 | solution.py:264
  50.4 1.4 fusion.10
  51.8 5.5 %all-to-all-start = ((bf16[64,8,1024]{2,1,0:T(8,128)(2,1)}), bf16[64,8,1024]{2,1,0:T(8,128)(2,1)}, u32[]{:S(2)}, u32[]{:S(2)}) async-start(bf16[64,8,1024]{2,1,0:T(8,128)(2,1)} %fusion.10), calls=%async_computation | async-start | bytes 2097152 | tf_op jit(solution)/shard_map/cond/branch_0_fun/all_to_all | solution.py:241
  57.3 0.9 convolution_convert_fusion.1
  58.3 17.6 %all-to-all-done = bf16[64,8,1024]{2,1,0:T(8,128)(2,1)} async-done(((bf16[64,8,1024]{2,1,0:T(8,128)(2,1)}), bf16[64,8,1024]{2,1,0:T(8,128)(2,1)}, u32[]{:S(2)}, u32[]{:S(2)}) %all-to-all-start) | async-done | bytes 1048608 | tf_op jit(solution)/shard_map/cond/branch_0_fun/all_to_all | solution.py:241
  75.9 5.8 %fusion.7 = f32[512,1536]{1,0:T(8,128)} fusion(bf16[4096,1536]{1,0:T(8,128)(2,1)} %get-tuple-element.32, bf16[64,8,1024]{2,1,0:T(8,128)(2,1)} %all-to-all-done), kind=kOutput, calls=%fused_computation.7 | convolution fusion | flops 1610612736 | bytes 7340032 | tf_op jit(solution)/shard_map/cond/branch_0_fun/dot_general | solution.py:256
  81.7 32.2 %all_to_all.30 = bf16[64,8,3072]{2,1,0:T(8,128)(2,1)S(1)} all-to-all(bf16[64,8,3072]{2,1,0:T(8,128)(2,1)S(1)} %bitcast.96), channel_id=1, replica_groups=mesh['zl'=2,'y'=4,'zh'=2,'x'=4,'core'=2] {'zl','y','zh','x'}, dimensions={0} | all-to-all | bytes 6291456 | tf_op jit(solution)/shard_map/cond/branch_0_fun/all_to_all | solution.py:241
  113.9 7.1 %fusion.3 = f32[512,1536]{1,0:T(8,128)S(1)} fusion(f32[512,1536]{1,0:T(8,128)} %fusion.7, bf16[4096,1536]{1,0:T(8,128)(2,1)S(1)} %copy-done.6, bf16[64,8,3072]{2,1,0:T(8,128)(2,1)S(1)} %all_to_all.30), kind=kOutput, calls=%fused_computation.5 | convolution fusion | flops 4832624640 | bytes 18874368 | tf_op jit(solution)/shard_map/cond/branch_0_fun/dot_general | solution.py:95
  121.0 3.7 %fusion.2 = bf16[64,8,4096]{2,1,0:T(8,128)(2,1)S(1)} fusion(bf16[768,4096]{1,0:T(8,128)(2,1)S(1)} %bitcast.116, f32[512,1536]{1,0:T(8,128)S(1)} %fusion.3), kind=kOutput, calls=%fused_computation.3 | convolution fusion | flops 3225681920 | bytes 13631488 | tf_op jit(solution)/shard_map/cond/branch_0_fun/dot_general | solution.py:101
  124.7 36.9 %all_to_all.31 = bf16[64,8,4096]{2,1,0:T(8,128)(2,1)S(1)} all-to-all(bf16[64,8,4096]{2,1,0:T(8,128)(2,1)S(1)} %fusion.2), channel_id=1, replica_groups=mesh['zl'=2,'y'=4,'zh'=2,'x'=4,'core'=2] {'zl','y','zh','x'}, dimensions={0} | all-to-all | bytes 8388608 | tf_op jit(solution)/shard_map/cond/branch_0_fun/all_to_all | solution.py:241
  161.7 1.6 branch_0_fun.1
  163.6 1.3 collective-permute-done.6
  (69 shorter events, 6.7 us)
Async XLA Ops:
  0.0 19.2 %copy-start = (bf16[256,4096]{1,0:T(8,128)(2,1)S(1)}, bf16[256,4096]{1,0:T(8,128)(2,1)}, u32[]{:S(2)}) copy-start(bf16[256,4096]{1,0:T(8,128)(2,1)} %proj_ref) | copy-start | bytes 6291460
  1.8 17.3 %collective-permute-start.2 = (bf16[256,4096]{1,0:T(8,128)(2,1)}, bf16[256,4096]{1,0:T(8,128)(2,1)}, u32[]{:S(2)}, u32[]{:S(2)}) collective-permute-start(bf16[256,4096]{1,0:T(8,128)(2,1)} %proj_ref), channel_id=1, source_target_pairs={{0,1},{1,0},{2,3},{3,2},{4,5},{5,4},{6,7},{7,6},{8,9},{9,8},{10,11... | collective-permute-start | bytes 6291464 | tf_op jit(solution)/shard_map/ppermute | solution.py:21
  3.3 15.9 %all-to-all-start.5 = ((bf16[8,2,128,128]{3,2,1,0:T(8,128)(2,1)}), bf16[8,2,128,128]{3,2,1,0:T(8,128)(2,1)S(1)}, u32[]{:S(2)}, u32[]{:S(2)}) async-start(bf16[8,2,128,128]{3,2,1,0:T(8,128)(2,1)} %broadcast_in_dim.59), calls=%async_computation.5 | async-start | bytes 1048576 | tf_op jit(solution)/shard_map/all_to_all | solution.py:162
  8.9 2.9 %collective-permute-start.4 = (s32[2,8,8]{2,1,0:T(8,128)}, s32[2,8,8]{2,1,0:T(8,128)S(1)}, u32[]{:S(2)}, u32[]{:S(2)}) collective-permute-start(s32[2,8,8]{2,1,0:T(8,128)} %param.20), channel_id=1, source_target_pairs={{0,1},{1,0},{2,3},{3,2},{4,5},{5,4},{6,7},{7,6},{8,9},{9,8},{10,11... | collective-permute-start | bytes 1544 | tf_op jit(solution)/shard_map/ppermute | solution.py:21
  9.2 4.3 %collective-permute-start.5 = (f32[2,8,8]{2,1,0:T(8,128)}, f32[2,8,8]{2,1,0:T(8,128)S(1)}, u32[]{:S(2)}, u32[]{:S(2)}) collective-permute-start(f32[2,8,8]{2,1,0:T(8,128)} %param.21), channel_id=1, source_target_pairs={{0,1},{1,0},{2,3},{3,2},{4,5},{5,4},{6,7},{7,6},{8,9},{9,8},{10,11... | collective-permute-start | bytes 1544 | tf_op jit(solution)/shard_map/ppermute | solution.py:21
  9.4 22.1 %collective-permute-start = (bf16[2,8,4096]{2,1,0:T(8,128)(2,1)}, bf16[2,8,4096]{2,1,0:T(8,128)(2,1)S(1)}, u32[]{:S(2)}, u32[]{:S(2)}) collective-permute-start(bf16[2,8,4096]{2,1,0:T(8,128)(2,1)} %param.16), channel_id=1, source_target_pairs={{0,1},{1,0},{2,3},{3,2},{4,5},{5,4},{6,7},{7,6},{8,9},{9,8},{10,11... | collective-permute-start | bytes 393224 | tf_op jit(solution)/shard_map/ppermute | solution.py:21
  9.7 5.2 %collective-permute-start.1 = (bf16[2,128,256]{2,1,0:T(8,128)(2,1)}, bf16[2,128,256]{2,1,0:T(8,128)(2,1)S(1)}, u32[]{:S(2)}, u32[]{:S(2)}) collective-permute-start(bf16[2,128,256]{2,1,0:T(8,128)(2,1)} %param.12), channel_id=1, source_target_pairs={{0,1},{1,0},{2,3},{3,2},{4,5},{5,4},{6,7},{7,6},{8,9},{9,8},{10,11... | collective-permute-start | bytes 393224 | tf_op jit(solution)/shard_map/ppermute | solution.py:21
  23.5 24.7 %copy-start.5 = (f32[4096]{0:T(1024)S(1)}, f32[4096]{0:T(1024)}, u32[]{:S(2)}) copy-start(f32[4096]{0:T(1024)} %param.17) | copy-start | bytes 49156
  23.5 24.4 %all-to-all-start.6 = ((bf16[8,16,4096]{2,1,0:T(8,128)(2,1)}), bf16[8,16,4096]{2,1,0:T(8,128)(2,1)S(1)}, u32[]{:S(2)}, u32[]{:S(2)}) async-start(bf16[8,16,4096]{2,1,0:T(8,128)(2,1)} %bitcast.14), calls=%async_computation.6 | async-start | bytes 2097152 | tf_op jit(solution)/shard_map/all_to_all | solution.py:182
  48.4 1.9 %collective-permute-start.3 = (bf16[16,4096]{1,0:T(8,128)(2,1)S(1)}, bf16[16,4096]{1,0:T(8,128)(2,1)S(1)}, u32[]{:S(2)}, u32[]{:S(2)}) collective-permute-start(bf16[16,4096]{1,0:T(8,128)(2,1)S(1)} %multiply_convert_fusion), channel_id=1, source_target_pairs={{0,1},{1,0},{2,3},{3,2},{4,5},{5,4},{6,7},{7,6},{8,9},{9,8},{10,11... | collective-permute-start | bytes 393224 | tf_op jit(solution)/shard_map/ppermute | solution.py:21
  51.8 24.1 %all-to-all-start = ((bf16[64,8,1024]{2,1,0:T(8,128)(2,1)}), bf16[64,8,1024]{2,1,0:T(8,128)(2,1)}, u32[]{:S(2)}, u32[]{:S(2)}) async-start(bf16[64,8,1024]{2,1,0:T(8,128)(2,1)} %fusion.10), calls=%async_computation | async-start | bytes 2097152 | tf_op jit(solution)/shard_map/cond/branch_0_fun/all_to_all | solution.py:241
  75.9 38.0 %copy-start.6 = (bf16[4096,1536]{1,0:T(8,128)(2,1)S(1)}, bf16[4096,1536]{1,0:T(8,128)(2,1)}, u32[]{:S(2)}) copy-start(bf16[4096,1536]{1,0:T(8,128)(2,1)} %get-tuple-element.32) | copy-start | bytes 37748740 | tf_op jit(solution)/shard_map/cond
  81.7 39.3 %slice-start = ((s8[6291456]{0:T(1024)(128)(4,1)}), s8[4194304]{0:T(1024)(128)(4,1)S(1)}, s32[]{:S(2)}) async-start(s8[6291456]{0:T(1024)(128)(4,1)} %bitcast.115), calls=%async_computation.7 | async-start | bytes 8388608 | tf_op jit(solution)/shard_map/cond
  113.9 7.1 %slice-start.1 = ((s8[6291456]{0:T(1024)(128)(4,1)}), s8[2097152]{0:T(1024)(128)(4,1)S(1)}, s32[]{:S(2)}) async-start(s8[6291456]{0:T(1024)(128)(4,1)} %bitcast.115), calls=%async_computation.8 | async-start | bytes 4194304 | tf_op jit(solution)/shard_map/cond
  124.7 37.0 %copy-start.1 = (f32[32,4096]{1,0:T(8,128)S(1)}, f32[32,4096]{1,0:T(8,128)}, u32[]{:S(2)}) copy-start(f32[32,4096]{1,0:T(8,128)} %get-tuple-element.36.base_ref) | copy-start | bytes 1572868 | tf_op jit(solution)/shard_map/cond
  124.7 37.0 %copy-start.3 = (bf16[64,512]{1,0:T(8,128)(2,1)S(1)}, bf16[64,512]{1,0:T(8,128)(2,1)}, u32[]{:S(2)}) copy-start(bf16[64,512]{1,0:T(8,128)(2,1)} %get-tuple-element.29.gates_ref) | copy-start | bytes 196612 | tf_op jit(solution)/shard_map/cond
  163.5 1.4 collective-permute-start.6

commit v6 on v5

--- a/solution.py
+++ b/solution.py
@@ -101,35 +101,38 @@
     return jnp.dot(hidden, w_out, preferred_element_type=jnp.float32).astype(jnp.bfloat16)
 
 
-def combine_kernel(gates_ref, returned_ref, base_ref, kept_ref, sent_ref):
-    token_count = base_ref.shape[0]
+def combine_kernel(core_ref, gates_ref, returned_ref, residual_ref, kept_ref, sent_ref):
+    chip_rows = residual_ref.shape[0]
+    token_rows = chip_rows // 2
+    token_count = gates_ref.shape[0] // 2
     summed = jnp.dot(gates_ref[...], returned_ref[...], preferred_element_type=jnp.float32)
-    total = summed[:token_count] + summed[token_count:] + base_ref[...]
-    kept_ref[...] = total[: token_count // 2]
-    sent_ref[...] = total[token_count // 2 :].astype(sent_ref.dtype)
-
-
-def combine(gates, returned, base):
-    slot_count, model_width = returned.shape
-    token_count = base.shape[0]
-    width = model_width // 4
-    half = (token_count // 2, model_width)
-    columns = lambda rows: pl.BlockSpec((rows, width), lambda step: (0, step))
+    total = summed[:token_count] + summed[token_count:]
+    first, second = residual_ref[:token_rows], residual_ref[token_rows:]
+    on_first = core_ref[0] == 0
+    own = (jnp.where(on_first, first, second), jnp.where(on_first, second, first))
+    for out_ref, rows, part in ((kept_ref, own[0], 0), (sent_ref, own[1], 1)):
+        for batch in range(2):
+            start = part * chip_rows + batch * token_rows
+            mine = on_first if batch == 0 else jnp.logical_not(on_first)
+            out_ref[batch * token_rows : (batch + 1) * token_rows] = (
+                total[start : start + token_rows] + jnp.where(mine, rows, 0.0)
+            ).astype(out_ref.dtype)
+
+
+def combine(core, gates, returned, residual_sum):
+    model_width = returned.shape[1]
+    half = (gates.shape[0] // 4, model_width)
+    whole = pl.BlockSpec(memory_space=pltpu.VMEM)
     return pl.pallas_call(
         combine_kernel,
-        grid=(model_width // width,),
-        in_specs=[
-            pl.BlockSpec(gates.shape, lambda step: (0, 0)),
-            columns(slot_count),
-            columns(token_count),
-        ],
-        out_specs=[columns(token_count // 2), columns(token_count // 2)],
+        in_specs=[pl.BlockSpec(memory_space=pltpu.SMEM), whole, whole, whole],
+        out_specs=[whole, whole],
         out_shape=[
             jax.ShapeDtypeStruct(half, jnp.float32),
             jax.ShapeDtypeStruct(half, jnp.bfloat16),
         ],
-        compiler_params=pltpu.CompilerParams(vmem_limit_bytes=32 * 2**20),
-    )(gates, returned, base)
+        compiler_params=pltpu.CompilerParams(vmem_limit_bytes=24 * 2**20),
+    )(core.astype(jnp.int32).reshape(1), gates, returned, residual_sum)
 
 
 def local(
@@ -229,11 +232,7 @@
     gate_rows = kept_first(both_halves(gate_matrix).T)
     gate_high = gate_rows.astype(jnp.bfloat16)
     gate_low = (gate_rows - gate_high.astype(jnp.float32)).astype(jnp.bfloat16)
-    own_sum = jnp.where(
-        (jnp.arange(batch_count) == core)[:, None, None], residual_sum[None], 0.0
-    ).reshape(tokens, model_width)
     both_gates = jnp.concatenate([gate_high, gate_low])
-    base = kept_first(own_sum)
     first_width = model_width // 4
 
     def exchange(rows):
@@ -247,19 +246,19 @@
             jnp.bfloat16
         )
 
-    def at_once(placing_rows, all_normed, w_in, w_out, both_gates, base):
+    def at_once(placing_rows, all_normed, w_in, w_out, both_gates, residual_sum):
         partial_value = expert_rows(exchange(place(placing_rows, all_normed)), w_in, w_out)
-        return combine(both_gates, exchange(partial_value), base)
-
-    def in_two(placing_rows, all_normed, w_in, w_out, both_gates, base):
+        return combine(core, both_gates, exchange(partial_value), residual_sum)
+
+    def in_two(placing_rows, all_normed, w_in, w_out, both_gates, residual_sum):
         first = exchange(place(placing_rows, all_normed[:, :first_width]))
-        started = jnp.dot(first, w_in[:first_width], preferred_element_type=jnp.float32)
-        outgoing, started = lax.optimization_barrier(
-            (place(placing_rows, all_normed[:, first_width:]), started)
-        )
-        second = exchange(outgoing)
+        started = jnp.dot(
+            first, w_in[:first_width], preferred_element_type=jnp.float32
+        ).astype(jnp.bfloat16)
+        columns, started = lax.optimization_barrier((all_normed[:, first_width:], started))
+        second = exchange(place(placing_rows, columns))
         partial_value = expert_rows(second, w_in, w_out, started)
-        return combine(both_gates, exchange(partial_value), base)
+        return combine(core, both_gates, exchange(partial_value), residual_sum)
 
     kept, sent = lax.cond(
         core == 0,
@@ -270,7 +269,7 @@
         w_in[0],
         w_out[0],
         both_gates,
-        base,
+        residual_sum,
     )
     return (
         (kept + swap_cores(sent).astype(jnp.float32)).astype(jnp.bfloat16).reshape(batch_count, token_rows, model_width)

time: 166 us -> 165 us (level)
  waiting for transfers between devices: 39.6 us -> 42 us
    dot_general x1, matrix products: 5.79 us -> 3.68 us  [in_two(): jnp.dot(first, w_in[:first_width], preferred_element_type=jnp.float32)]
  transfers between devices with their start and end apart: 10 -> 10, of which waited for: 4 -> 5; matrix products, arithmetic and copies ran while one was open for 5% -> 3% of each run, Pallas kernels for 3% -> 3%
where the time goes in v6:
time: 165 us; the launch traced here: 164 us
  blocking collectives  69.9 us (42%)
  waiting for transfers between devices  42 us (25%)
  starting transfers between devices  20.8 us (13%)
  matrix products  17.5 us (11%)
  Pallas kernels  5.1 us (3%)
  local copies, waits for them, and re-layouts  4.66 us (3%)
  other arithmetic  3.63 us (2%)
    all_to_all x2, blocking collectives, exchange(): lax.all_to_all(rows.reshape(chip_count, slots, width), CHIPS, 0, 0)  69.9 us
    all_to_all x1, waiting for transfers between devices, exchange(): lax.all_to_all(rows.reshape(chip_count, slots, width), CHIPS, 0, 0)  18.5 us
    all_to_all x1, waiting for transfers between devices, local(): lax.all_to_all(projected.reshape(column_size, chip_rows, model_width), CO...  16.9 us
    dot_general x1, matrix products, expert_rows(): jnp.dot(rows, w_in[model_width - rows.shape[1]:], preferred_element_type=...  7.77 us
    all_to_all x1, starting transfers between devices, local(): lax.all_to_all(projected.reshape(column_size, chip_rows, model_width), CO...  7.05 us
    all_to_all x1, starting transfers between devices, local(): gathered = lax.all_to_all(spread, CONTEXT, 0, 0)  5.63 us
    all_to_all x1, starting transfers between devices, exchange(): lax.all_to_all(rows.reshape(chip_count, slots, width), CHIPS, 0, 0)  4.65 us
    all_to_all x1, waiting for transfers between devices, local(): gathered = lax.all_to_all(spread, CONTEXT, 0, 0)  4.32 us
  transfers between devices with their start and end apart: 10, of which 5 were waited for; matrix products, arithmetic and copies ran while one was open for 3% of the time, Pallas kernels for 3%

profile of v6, /device:TPU:1, one launch (start us, length us, event | category | flops | bytes accessed | tf_op | source)
XLA Modules:
  0.0 164.0 jit_solution(13190283471683764655)
XLA Ops:
  0.0 0.9 constant_dynamic-slice_fusion.2
  0.9 0.9 broadcast_in_dim.22
  1.8 1.4 collective-permute-start.2
  3.3 5.6 %all-to-all-start.5 = ((bf16[8,2,128,128]{3,2,1,0:T(8,128)(2,1)}), bf16[8,2,128,128]{3,2,1,0:T(8,128)(2,1)S(1)}, u32[]{:S(2)}, u32[]{:S(2)}) async-start(bf16[8,2,128,128]{3,2,1,0:T(8,128)(2,1)} %broadcast_in_dim.22), calls=%async_computation.5 | async-start | bytes 1048576 | tf_op jit(solution)/shard_map/all_to_all | solution.py:165
  9.9 0.8 dynamic-slice_bitcast_fusion.1.own_ref
  10.8 0.8 constant_dynamic-slice_fusion.1
  14.9 4.3 %all-to-all-done.5.kv_ref = bf16[8,2,128,128]{3,2,1,0:T(8,128)(2,1)S(1)} async-done(((bf16[8,2,128,128]{3,2,1,0:T(8,128)(2,1)}), bf16[8,2,128,128]{3,2,1,0:T(8,128)(2,1)S(1)}, u32[]{:S(2)}, u32[]{:S(2)}) %all-to-all-start.5) | async-done | bytes 524320 | tf_op jit(solution)/shard_map/all_to_all | solution.py:165
  19.2 4.3 %shard_map.100 = bf16[128,4096]{1,0:T(8,128)(2,1)} custom-call(s32[1]{0:T(128)} %bitcast.14.index_ref, bf16[128,256]{1,0:T(8,128)(2,1)S(1)} %dynamic-slice_bitcast_fusion.1.own_ref, bf16[128,256]{1,0:T(8,128)(2,1)S(1)} %dynamic-slice_bitcast_fusion.other_ref, bf16[8,2,128,128]{3,2,1,0:T(8,128)(2,1)S(1)} %all-to-all-done.5.kv_ref, ...), custom_call_target="tpu_custom_call" | custom-call | tf_op jit(solution)/shard_map/pallas_call | solution.py:80
  23.5 7.1 %all-to-all-start.6 = ((bf16[8,16,4096]{2,1,0:T(8,128)(2,1)}), bf16[8,16,4096]{2,1,0:T(8,128)(2,1)S(1)}, u32[]{:S(2)}, u32[]{:S(2)}) async-start(bf16[8,16,4096]{2,1,0:T(8,128)(2,1)} %bitcast.17), calls=%async_computation.6 | async-start | bytes 2097152 | tf_op jit(solution)/shard_map/all_to_all | solution.py:185
  30.9 16.9 %all-to-all-done.6 = bf16[8,16,4096]{2,1,0:T(8,128)(2,1)S(1)} async-done(((bf16[8,16,4096]{2,1,0:T(8,128)(2,1)}), bf16[8,16,4096]{2,1,0:T(8,128)(2,1)S(1)}, u32[]{:S(2)}, u32[]{:S(2)}) %all-to-all-start.6) | async-done | bytes 1048608 | tf_op jit(solution)/shard_map/all_to_all | solution.py:185
  48.2 0.9 collective-permute-start.3
  49.3 0.9 collective-permute-done.3
  50.2 111.6 %conditional.1 = ((f32[16,4096]{1,0:T(8,128)S(1)}, bf16[16,4096]{1,0:T(8,128)(2,1)S(1)})) conditional(s32[]{:T(128)} %convert_element_type.98, (s32[]{:T(128)}, bf16[32,4096]{1,0:T(8,128)(2,1)S(1)}, bf16[512,32]{1,0:T(8,128)(2,1)S(1)}, bf16[4096,1536]{1,0:T(8,128)(2,1)}, bf16[768,4096]{1,0:T(8,128)(2,1)}, /*index=5*/bf16[64,512]{1,0:T(8,128)(2,1)S(1)}, ...), branch_computations={%region_6.7_spmd, %region_7.8_spmd} | conditional | flops 9806807040 | bytes 124026968 | solution.py:263
  50.2 1.4 fusion.14
  51.6 4.7 %all-to-all-start = ((bf16[64,8,1024]{2,1,0:T(8,128)(2,1)}), bf16[64,8,1024]{2,1,0:T(8,128)(2,1)S(1)}, u32[]{:S(2)}, u32[]{:S(2)}) async-start(bf16[64,8,1024]{2,1,0:T(8,128)(2,1)} %fusion.14), calls=%async_computation | async-start | bytes 2097152 | tf_op jit(solution)/shard_map/cond/branch_0_fun/all_to_all | solution.py:240
  56.3 18.5 %all-to-all-done = bf16[64,8,1024]{2,1,0:T(8,128)(2,1)S(1)} async-done(((bf16[64,8,1024]{2,1,0:T(8,128)(2,1)}), bf16[64,8,1024]{2,1,0:T(8,128)(2,1)S(1)}, u32[]{:S(2)}, u32[]{:S(2)}) %all-to-all-start) | async-done | bytes 1048608 | tf_op jit(solution)/shard_map/cond/branch_0_fun/all_to_all | solution.py:240
  74.8 3.7 %fusion.10 = bf16[512,1536]{1,0:T(8,128)(2,1)S(1)} fusion(bf16[4096,1536]{1,0:T(8,128)(2,1)} %get-tuple-element.37, bf16[64,8,1024]{2,1,0:T(8,128)(2,1)S(1)} %all-to-all-done), kind=kOutput, calls=%fused_computation.10 | convolution fusion | flops 1611399168 | bytes 5767168 | tf_op jit(solution)/shard_map/cond/branch_0_fun/dot_general | solution.py:255
  78.5 1.0 fusion.3
  79.5 30.3 %all_to_all.30 = bf16[64,8,3072]{2,1,0:T(8,128)(2,1)S(1)} all-to-all(bf16[64,8,3072]{2,1,0:T(8,128)(2,1)S(1)} %fusion.3), channel_id=1, replica_groups=mesh['zl'=2,'y'=4,'zh'=2,'x'=4,'core'=2] {'zl','y','zh','x'}, dimensions={0} | all-to-all | bytes 6291456 | tf_op jit(solution)/shard_map/cond/branch_0_fun/all_to_all | solution.py:240
  109.8 7.8 %fusion.4 = f32[512,1536]{1,0:T(8,128)S(1)} fusion(bf16[4096,1536]{1,0:T(8,128)(2,1)} %get-tuple-element.37, bf16[64,8,3072]{2,1,0:T(8,128)(2,1)S(1)} %all_to_all.30, bf16[512,1536]{1,0:T(8,128)(2,1)S(1)} %fusion.10), kind=kOutput, calls=%fused_computation.6 | convolution fusion | flops 4833411072 | bytes 17301504 | tf_op jit(solution)/shard_map/cond/branch_0_fun/dot_general | solution.py:95
  117.6 3.7 %fusion.2 = bf16[64,8,4096]{2,1,0:T(8,128)(2,1)S(1)} fusion(bf16[768,4096]{1,0:T(8,128)(2,1)S(1)} %bitcast.109, f32[512,1536]{1,0:T(8,128)S(1)} %fusion.4), kind=kOutput, calls=%fused_computation.3 | convolution fusion | flops 3225681920 | bytes 13631488 | tf_op jit(solution)/shard_map/cond/branch_0_fun/dot_general | solution.py:101
  121.3 39.6 %all_to_all.31 = bf16[64,8,4096]{2,1,0:T(8,128)(2,1)S(1)} all-to-all(bf16[64,8,4096]{2,1,0:T(8,128)(2,1)S(1)} %fusion.2), channel_id=1, replica_groups=mesh['zl'=2,'y'=4,'zh'=2,'x'=4,'core'=2] {'zl','y','zh','x'}, dimensions={0} | all-to-all | bytes 8388608 | tf_op jit(solution)/shard_map/cond/branch_0_fun/all_to_all | solution.py:240
  160.9 0.8 branch_0_fun.1
  162.0 1.3 collective-permute-done.6
  (59 shorter events, 5.9 us)
Async XLA Ops:
  0.0 19.2 %copy-start = (bf16[256,4096]{1,0:T(8,128)(2,1)S(1)}, bf16[256,4096]{1,0:T(8,128)(2,1)}, u32[]{:S(2)}) copy-start(bf16[256,4096]{1,0:T(8,128)(2,1)} %proj_ref) | copy-start | bytes 6291460
  1.8 17.3 %collective-permute-start.2 = (bf16[256,4096]{1,0:T(8,128)(2,1)}, bf16[256,4096]{1,0:T(8,128)(2,1)}, u32[]{:S(2)}, u32[]{:S(2)}) collective-permute-start(bf16[256,4096]{1,0:T(8,128)(2,1)} %proj_ref), channel_id=1, source_target_pairs={{0,1},{1,0},{2,3},{3,2},{4,5},{5,4},{6,7},{7,6},{8,9},{9,8},{10,11... | collective-permute-start | bytes 6291464 | tf_op jit(solution)/shard_map/ppermute | solution.py:21
  3.3 15.9 %all-to-all-start.5 = ((bf16[8,2,128,128]{3,2,1,0:T(8,128)(2,1)}), bf16[8,2,128,128]{3,2,1,0:T(8,128)(2,1)S(1)}, u32[]{:S(2)}, u32[]{:S(2)}) async-start(bf16[8,2,128,128]{3,2,1,0:T(8,128)(2,1)} %broadcast_in_dim.22), calls=%async_computation.5 | async-start | bytes 1048576 | tf_op jit(solution)/shard_map/all_to_all | solution.py:165
  8.9 2.9 %collective-permute-start.4 = (s32[2,8,8]{2,1,0:T(8,128)}, s32[2,8,8]{2,1,0:T(8,128)S(1)}, u32[]{:S(2)}, u32[]{:S(2)}) collective-permute-start(s32[2,8,8]{2,1,0:T(8,128)} %param.20), channel_id=1, source_target_pairs={{0,1},{1,0},{2,3},{3,2},{4,5},{5,4},{6,7},{7,6},{8,9},{9,8},{10,11... | collective-permute-start | bytes 1544 | tf_op jit(solution)/shard_map/ppermute | solution.py:21
  9.2 4.3 %collective-permute-start.5 = (f32[2,8,8]{2,1,0:T(8,128)}, f32[2,8,8]{2,1,0:T(8,128)S(1)}, u32[]{:S(2)}, u32[]{:S(2)}) collective-permute-start(f32[2,8,8]{2,1,0:T(8,128)} %param.21), channel_id=1, source_target_pairs={{0,1},{1,0},{2,3},{3,2},{4,5},{5,4},{6,7},{7,6},{8,9},{9,8},{10,11... | collective-permute-start | bytes 1544 | tf_op jit(solution)/shard_map/ppermute | solution.py:21
  9.4 21.4 %collective-permute-start = (bf16[2,8,4096]{2,1,0:T(8,128)(2,1)}, bf16[2,8,4096]{2,1,0:T(8,128)(2,1)S(1)}, u32[]{:S(2)}, u32[]{:S(2)}) collective-permute-start(bf16[2,8,4096]{2,1,0:T(8,128)(2,1)} %param.16), channel_id=1, source_target_pairs={{0,1},{1,0},{2,3},{3,2},{4,5},{5,4},{6,7},{7,6},{8,9},{9,8},{10,11... | collective-permute-start | bytes 393224 | tf_op jit(solution)/shard_map/ppermute | solution.py:21
  9.7 5.1 %collective-permute-start.1 = (bf16[2,128,256]{2,1,0:T(8,128)(2,1)}, bf16[2,128,256]{2,1,0:T(8,128)(2,1)S(1)}, u32[]{:S(2)}, u32[]{:S(2)}) collective-permute-start(bf16[2,128,256]{2,1,0:T(8,128)(2,1)} %param.12), channel_id=1, source_target_pairs={{0,1},{1,0},{2,3},{3,2},{4,5},{5,4},{6,7},{7,6},{8,9},{9,8},{10,11... | collective-permute-start | bytes 393224 | tf_op jit(solution)/shard_map/ppermute | solution.py:21
  23.5 24.7 %copy-start.1 = (f32[4096]{0:T(1024)S(1)}, f32[4096]{0:T(1024)}, u32[]{:S(2)}) copy-start(f32[4096]{0:T(1024)} %param.17) | copy-start | bytes 49156
  23.5 24.4 %all-to-all-start.6 = ((bf16[8,16,4096]{2,1,0:T(8,128)(2,1)}), bf16[8,16,4096]{2,1,0:T(8,128)(2,1)S(1)}, u32[]{:S(2)}, u32[]{:S(2)}) async-start(bf16[8,16,4096]{2,1,0:T(8,128)(2,1)} %bitcast.17), calls=%async_computation.6 | async-start | bytes 2097152 | tf_op jit(solution)/shard_map/all_to_all | solution.py:185
  48.2 1.9 %collective-permute-start.3 = (bf16[16,4096]{1,0:T(8,128)(2,1)S(1)}, bf16[16,4096]{1,0:T(8,128)(2,1)S(1)}, u32[]{:S(2)}, u32[]{:S(2)}) collective-permute-start(bf16[16,4096]{1,0:T(8,128)(2,1)S(1)} %multiply_convert_fusion), channel_id=1, source_target_pairs={{0,1},{1,0},{2,3},{3,2},{4,5},{5,4},{6,7},{7,6},{8,9},{9,8},{10,11... | collective-permute-start | bytes 393224 | tf_op jit(solution)/shard_map/ppermute | solution.py:21
  51.6 23.2 %all-to-all-start = ((bf16[64,8,1024]{2,1,0:T(8,128)(2,1)}), bf16[64,8,1024]{2,1,0:T(8,128)(2,1)S(1)}, u32[]{:S(2)}, u32[]{:S(2)}) async-start(bf16[64,8,1024]{2,1,0:T(8,128)(2,1)} %fusion.14), calls=%async_computation | async-start | bytes 2097152 | tf_op jit(solution)/shard_map/cond/branch_0_fun/all_to_all | solution.py:240
  79.5 38.1 %slice-start = ((s8[6291456]{0:T(1024)(128)(4,1)}), s8[4194304]{0:T(1024)(128)(4,1)S(1)}, s32[]{:S(2)}) async-start(s8[6291456]{0:T(1024)(128)(4,1)} %bitcast.108), calls=%async_computation.7 | async-start | bytes 8388608 | tf_op jit(solution)/shard_map/cond
  109.8 7.8 %slice-start.1 = ((s8[6291456]{0:T(1024)(128)(4,1)}), s8[2097152]{0:T(1024)(128)(4,1)S(1)}, s32[]{:S(2)}) async-start(s8[6291456]{0:T(1024)(128)(4,1)} %bitcast.108), calls=%async_computation.8 | async-start | bytes 4194304 | tf_op jit(solution)/shard_map/cond
  161.9 1.4 collective-permute-start.6

commit v7 on v6

--- a/solution.py
+++ b/solution.py
@@ -110,13 +110,11 @@
     first, second = residual_ref[:token_rows], residual_ref[token_rows:]
     on_first = core_ref[0] == 0
     own = (jnp.where(on_first, first, second), jnp.where(on_first, second, first))
-    for out_ref, rows, part in ((kept_ref, own[0], 0), (sent_ref, own[1], 1)):
-        for batch in range(2):
-            start = part * chip_rows + batch * token_rows
-            mine = on_first if batch == 0 else jnp.logical_not(on_first)
-            out_ref[batch * token_rows : (batch + 1) * token_rows] = (
-                total[start : start + token_rows] + jnp.where(mine, rows, 0.0)
-            ).astype(out_ref.dtype)
+    for out_ref, rows, start in ((kept_ref, own[0], 0), (sent_ref, own[1], chip_rows)):
+        added = jnp.concatenate(
+            [jnp.where(on_first, rows, 0.0), jnp.where(on_first, 0.0, rows)], axis=0
+        )
+        out_ref[...] = (total[start : start + chip_rows] + added).astype(out_ref.dtype)
 
 
 def combine(core, gates, returned, residual_sum):

time: 165 us -> 165 us (level)
  no operation moved by 1% of the time
where the time goes in v7:
time: 165 us; the launch traced here: 164 us
  blocking collectives  69.9 us (42%)
  waiting for transfers between devices  42 us (25%)
  starting transfers between devices  20.8 us (13%)
  matrix products  17.5 us (11%)
  Pallas kernels  5.1 us (3%)
  local copies, waits for them, and re-layouts  4.66 us (3%)
  other arithmetic  3.63 us (2%)
    all_to_all x2, blocking collectives, exchange(): lax.all_to_all(rows.reshape(chip_count, slots, width), CHIPS, 0, 0)  69.9 us
    all_to_all x1, waiting for transfers between devices, exchange(): lax.all_to_all(rows.reshape(chip_count, slots, width), CHIPS, 0, 0)  18.5 us
    all_to_all x1, waiting for transfers between devices, local(): lax.all_to_all(projected.reshape(column_size, chip_rows, model_width), CO...  16.9 us
    dot_general x1, matrix products, expert_rows(): jnp.dot(rows, w_in[model_width - rows.shape[1]:], preferred_element_type=...  7.77 us
    all_to_all x1, starting transfers between devices, local(): lax.all_to_all(projected.reshape(column_size, chip_rows, model_width), CO...  7.05 us
    all_to_all x1, starting transfers between devices, local(): gathered = lax.all_to_all(spread, CONTEXT, 0, 0)  5.63 us
    all_to_all x1, starting transfers between devices, exchange(): lax.all_to_all(rows.reshape(chip_count, slots, width), CHIPS, 0, 0)  4.65 us
    all_to_all x1, waiting for transfers between devices, local(): gathered = lax.all_to_all(spread, CONTEXT, 0, 0)  4.32 us
  transfers between devices with their start and end apart: 10, of which 5 were waited for; matrix products, arithmetic and copies ran while one was open for 3% of the time, Pallas kernels for 3%

profile of v7, /device:TPU:1, one launch (start us, length us, event | category | flops | bytes accessed | tf_op | source)
XLA Modules:
  0.0 164.0 jit_solution(13190283471683764655)
XLA Ops:
  0.0 0.9 constant_dynamic-slice_fusion.2
  0.9 0.9 broadcast_in_dim.22
  1.8 1.4 collective-permute-start.2
  3.3 5.6 %all-to-all-start.5 = ((bf16[8,2,128,128]{3,2,1,0:T(8,128)(2,1)}), bf16[8,2,128,128]{3,2,1,0:T(8,128)(2,1)S(1)}, u32[]{:S(2)}, u32[]{:S(2)}) async-start(bf16[8,2,128,128]{3,2,1,0:T(8,128)(2,1)} %broadcast_in_dim.22), calls=%async_computation.5 | async-start | bytes 1048576 | tf_op jit(solution)/shard_map/all_to_all | solution.py:163
  9.9 0.8 dynamic-slice_bitcast_fusion.1.own_ref
  10.8 0.8 constant_dynamic-slice_fusion.1
  14.9 4.3 %all-to-all-done.5.kv_ref = bf16[8,2,128,128]{3,2,1,0:T(8,128)(2,1)S(1)} async-done(((bf16[8,2,128,128]{3,2,1,0:T(8,128)(2,1)}), bf16[8,2,128,128]{3,2,1,0:T(8,128)(2,1)S(1)}, u32[]{:S(2)}, u32[]{:S(2)}) %all-to-all-start.5) | async-done | bytes 524320 | tf_op jit(solution)/shard_map/all_to_all | solution.py:163
  19.2 4.3 %shard_map.100 = bf16[128,4096]{1,0:T(8,128)(2,1)} custom-call(s32[1]{0:T(128)} %bitcast.14.index_ref, bf16[128,256]{1,0:T(8,128)(2,1)S(1)} %dynamic-slice_bitcast_fusion.1.own_ref, bf16[128,256]{1,0:T(8,128)(2,1)S(1)} %dynamic-slice_bitcast_fusion.other_ref, bf16[8,2,128,128]{3,2,1,0:T(8,128)(2,1)S(1)} %all-to-all-done.5.kv_ref, ...), custom_call_target="tpu_custom_call" | custom-call | tf_op jit(solution)/shard_map/pallas_call | solution.py:80
  23.5 7.1 %all-to-all-start.6 = ((bf16[8,16,4096]{2,1,0:T(8,128)(2,1)}), bf16[8,16,4096]{2,1,0:T(8,128)(2,1)S(1)}, u32[]{:S(2)}, u32[]{:S(2)}) async-start(bf16[8,16,4096]{2,1,0:T(8,128)(2,1)} %bitcast.17), calls=%async_computation.6 | async-start | bytes 2097152 | tf_op jit(solution)/shard_map/all_to_all | solution.py:183
  30.9 16.9 %all-to-all-done.6 = bf16[8,16,4096]{2,1,0:T(8,128)(2,1)S(1)} async-done(((bf16[8,16,4096]{2,1,0:T(8,128)(2,1)}), bf16[8,16,4096]{2,1,0:T(8,128)(2,1)S(1)}, u32[]{:S(2)}, u32[]{:S(2)}) %all-to-all-start.6) | async-done | bytes 1048608 | tf_op jit(solution)/shard_map/all_to_all | solution.py:183
  48.2 0.9 collective-permute-start.3
  49.3 0.9 collective-permute-done.3
  50.2 111.6 %conditional.1 = ((f32[16,4096]{1,0:T(8,128)S(1)}, bf16[16,4096]{1,0:T(8,128)(2,1)S(1)})) conditional(s32[]{:T(128)} %convert_element_type.98, (s32[]{:T(128)}, bf16[32,4096]{1,0:T(8,128)(2,1)S(1)}, bf16[512,32]{1,0:T(8,128)(2,1)S(1)}, bf16[4096,1536]{1,0:T(8,128)(2,1)}, bf16[768,4096]{1,0:T(8,128)(2,1)}, /*index=5*/bf16[64,512]{1,0:T(8,128)(2,1)S(1)}, ...), branch_computations={%region_6.7_spmd, %region_7.8_spmd} | conditional | flops 9806807040 | bytes 124026968 | solution.py:261
  50.2 1.4 fusion.14
  51.6 4.7 %all-to-all-start = ((bf16[64,8,1024]{2,1,0:T(8,128)(2,1)}), bf16[64,8,1024]{2,1,0:T(8,128)(2,1)S(1)}, u32[]{:S(2)}, u32[]{:S(2)}) async-start(bf16[64,8,1024]{2,1,0:T(8,128)(2,1)} %fusion.14), calls=%async_computation | async-start | bytes 2097152 | tf_op jit(solution)/shard_map/cond/branch_0_fun/all_to_all | solution.py:238
  56.3 18.5 %all-to-all-done = bf16[64,8,1024]{2,1,0:T(8,128)(2,1)S(1)} async-done(((bf16[64,8,1024]{2,1,0:T(8,128)(2,1)}), bf16[64,8,1024]{2,1,0:T(8,128)(2,1)S(1)}, u32[]{:S(2)}, u32[]{:S(2)}) %all-to-all-start) | async-done | bytes 1048608 | tf_op jit(solution)/shard_map/cond/branch_0_fun/all_to_all | solution.py:238
  74.8 3.7 %fusion.10 = bf16[512,1536]{1,0:T(8,128)(2,1)S(1)} fusion(bf16[4096,1536]{1,0:T(8,128)(2,1)} %get-tuple-element.37, bf16[64,8,1024]{2,1,0:T(8,128)(2,1)S(1)} %all-to-all-done), kind=kOutput, calls=%fused_computation.10 | convolution fusion | flops 1611399168 | bytes 5767168 | tf_op jit(solution)/shard_map/cond/branch_0_fun/dot_general | solution.py:253
  78.5 1.0 fusion.3
  79.5 30.3 %all_to_all.30 = bf16[64,8,3072]{2,1,0:T(8,128)(2,1)S(1)} all-to-all(bf16[64,8,3072]{2,1,0:T(8,128)(2,1)S(1)} %fusion.3), channel_id=1, replica_groups=mesh['zl'=2,'y'=4,'zh'=2,'x'=4,'core'=2] {'zl','y','zh','x'}, dimensions={0} | all-to-all | bytes 6291456 | tf_op jit(solution)/shard_map/cond/branch_0_fun/all_to_all | solution.py:238
  109.8 7.8 %fusion.4 = f32[512,1536]{1,0:T(8,128)S(1)} fusion(bf16[4096,1536]{1,0:T(8,128)(2,1)} %get-tuple-element.37, bf16[64,8,3072]{2,1,0:T(8,128)(2,1)S(1)} %all_to_all.30, bf16[512,1536]{1,0:T(8,128)(2,1)S(1)} %fusion.10), kind=kOutput, calls=%fused_computation.6 | convolution fusion | flops 4833411072 | bytes 17301504 | tf_op jit(solution)/shard_map/cond/branch_0_fun/dot_general | solution.py:95
  117.6 3.7 %fusion.2 = bf16[64,8,4096]{2,1,0:T(8,128)(2,1)S(1)} fusion(bf16[768,4096]{1,0:T(8,128)(2,1)S(1)} %bitcast.109, f32[512,1536]{1,0:T(8,128)S(1)} %fusion.4), kind=kOutput, calls=%fused_computation.3 | convolution fusion | flops 3225681920 | bytes 13631488 | tf_op jit(solution)/shard_map/cond/branch_0_fun/dot_general | solution.py:101
  121.3 39.6 %all_to_all.31 = bf16[64,8,4096]{2,1,0:T(8,128)(2,1)S(1)} all-to-all(bf16[64,8,4096]{2,1,0:T(8,128)(2,1)S(1)} %fusion.2), channel_id=1, replica_groups=mesh['zl'=2,'y'=4,'zh'=2,'x'=4,'core'=2] {'zl','y','zh','x'}, dimensions={0} | all-to-all | bytes 8388608 | tf_op jit(solution)/shard_map/cond/branch_0_fun/all_to_all | solution.py:238
  160.9 0.8 branch_0_fun.1
  162.0 1.3 collective-permute-done.6
  (59 shorter events, 5.9 us)
Async XLA Ops:
  0.0 19.2 %copy-start = (bf16[256,4096]{1,0:T(8,128)(2,1)S(1)}, bf16[256,4096]{1,0:T(8,128)(2,1)}, u32[]{:S(2)}) copy-start(bf16[256,4096]{1,0:T(8,128)(2,1)} %proj_ref) | copy-start | bytes 6291460
  1.8 17.3 %collective-permute-start.2 = (bf16[256,4096]{1,0:T(8,128)(2,1)}, bf16[256,4096]{1,0:T(8,128)(2,1)}, u32[]{:S(2)}, u32[]{:S(2)}) collective-permute-start(bf16[256,4096]{1,0:T(8,128)(2,1)} %proj_ref), channel_id=1, source_target_pairs={{0,1},{1,0},{2,3},{3,2},{4,5},{5,4},{6,7},{7,6},{8,9},{9,8},{10,11... | collective-permute-start | bytes 6291464 | tf_op jit(solution)/shard_map/ppermute | solution.py:21
  3.3 15.9 %all-to-all-start.5 = ((bf16[8,2,128,128]{3,2,1,0:T(8,128)(2,1)}), bf16[8,2,128,128]{3,2,1,0:T(8,128)(2,1)S(1)}, u32[]{:S(2)}, u32[]{:S(2)}) async-start(bf16[8,2,128,128]{3,2,1,0:T(8,128)(2,1)} %broadcast_in_dim.22), calls=%async_computation.5 | async-start | bytes 1048576 | tf_op jit(solution)/shard_map/all_to_all | solution.py:163
  8.9 2.9 %collective-permute-start.4 = (s32[2,8,8]{2,1,0:T(8,128)}, s32[2,8,8]{2,1,0:T(8,128)S(1)}, u32[]{:S(2)}, u32[]{:S(2)}) collective-permute-start(s32[2,8,8]{2,1,0:T(8,128)} %param.20), channel_id=1, source_target_pairs={{0,1},{1,0},{2,3},{3,2},{4,5},{5,4},{6,7},{7,6},{8,9},{9,8},{10,11... | collective-permute-start | bytes 1544 | tf_op jit(solution)/shard_map/ppermute | solution.py:21
  9.2 4.3 %collective-permute-start.5 = (f32[2,8,8]{2,1,0:T(8,128)}, f32[2,8,8]{2,1,0:T(8,128)S(1)}, u32[]{:S(2)}, u32[]{:S(2)}) collective-permute-start(f32[2,8,8]{2,1,0:T(8,128)} %param.21), channel_id=1, source_target_pairs={{0,1},{1,0},{2,3},{3,2},{4,5},{5,4},{6,7},{7,6},{8,9},{9,8},{10,11... | collective-permute-start | bytes 1544 | tf_op jit(solution)/shard_map/ppermute | solution.py:21
  9.4 21.4 %collective-permute-start = (bf16[2,8,4096]{2,1,0:T(8,128)(2,1)}, bf16[2,8,4096]{2,1,0:T(8,128)(2,1)S(1)}, u32[]{:S(2)}, u32[]{:S(2)}) collective-permute-start(bf16[2,8,4096]{2,1,0:T(8,128)(2,1)} %param.16), channel_id=1, source_target_pairs={{0,1},{1,0},{2,3},{3,2},{4,5},{5,4},{6,7},{7,6},{8,9},{9,8},{10,11... | collective-permute-start | bytes 393224 | tf_op jit(solution)/shard_map/ppermute | solution.py:21
  9.7 5.1 %collective-permute-start.1 = (bf16[2,128,256]{2,1,0:T(8,128)(2,1)}, bf16[2,128,256]{2,1,0:T(8,128)(2,1)S(1)}, u32[]{:S(2)}, u32[]{:S(2)}) collective-permute-start(bf16[2,128,256]{2,1,0:T(8,128)(2,1)} %param.12), channel_id=1, source_target_pairs={{0,1},{1,0},{2,3},{3,2},{4,5},{5,4},{6,7},{7,6},{8,9},{9,8},{10,11... | collective-permute-start | bytes 393224 | tf_op jit(solution)/shard_map/ppermute | solution.py:21
  23.5 24.7 %copy-start.1 = (f32[4096]{0:T(1024)S(1)}, f32[4096]{0:T(1024)}, u32[]{:S(2)}) copy-start(f32[4096]{0:T(1024)} %param.17) | copy-start | bytes 49156
  23.5 24.4 %all-to-all-start.6 = ((bf16[8,16,4096]{2,1,0:T(8,128)(2,1)}), bf16[8,16,4096]{2,1,0:T(8,128)(2,1)S(1)}, u32[]{:S(2)}, u32[]{:S(2)}) async-start(bf16[8,16,4096]{2,1,0:T(8,128)(2,1)} %bitcast.17), calls=%async_computation.6 | async-start | bytes 2097152 | tf_op jit(solution)/shard_map/all_to_all | solution.py:183
  48.2 1.9 %collective-permute-start.3 = (bf16[16,4096]{1,0:T(8,128)(2,1)S(1)}, bf16[16,4096]{1,0:T(8,128)(2,1)S(1)}, u32[]{:S(2)}, u32[]{:S(2)}) collective-permute-start(bf16[16,4096]{1,0:T(8,128)(2,1)S(1)} %multiply_convert_fusion), channel_id=1, source_target_pairs={{0,1},{1,0},{2,3},{3,2},{4,5},{5,4},{6,7},{7,6},{8,9},{9,8},{10,11... | collective-permute-start | bytes 393224 | tf_op jit(solution)/shard_map/ppermute | solution.py:21
  51.6 23.2 %all-to-all-start = ((bf16[64,8,1024]{2,1,0:T(8,128)(2,1)}), bf16[64,8,1024]{2,1,0:T(8,128)(2,1)S(1)}, u32[]{:S(2)}, u32[]{:S(2)}) async-start(bf16[64,8,1024]{2,1,0:T(8,128)(2,1)} %fusion.14), calls=%async_computation | async-start | bytes 2097152 | tf_op jit(solution)/shard_map/cond/branch_0_fun/all_to_all | solution.py:238
  79.5 38.1 %slice-start = ((s8[6291456]{0:T(1024)(128)(4,1)}), s8[4194304]{0:T(1024)(128)(4,1)S(1)}, s32[]{:S(2)}) async-start(s8[6291456]{0:T(1024)(128)(4,1)} %bitcast.108), calls=%async_computation.7 | async-start | bytes 8388608 | tf_op jit(solution)/shard_map/cond
  109.8 7.8 %slice-start.1 = ((s8[6291456]{0:T(1024)(128)(4,1)}), s8[2097152]{0:T(1024)(128)(4,1)S(1)}, s32[]{:S(2)}) async-start(s8[6291456]{0:T(1024)(128)(4,1)} %bitcast.108), calls=%async_computation.8 | async-start | bytes 4194304 | tf_op jit(solution)/shard_map/cond
  161.9 1.4 collective-permute-start.6

commit v8 on v7

--- a/solution.py
+++ b/solution.py
@@ -45,8 +45,8 @@
     allowed = folded(key_rows % row_count, key_rows // row_count, context_size) <= folded(
         query_rows, index_ref[0], context_size
     )
-    heads = []
-    for source in (own_ref, other_ref):
+    projected = 0.0
+    for part, source in enumerate((own_ref, other_ref)):
         head_count = feature_count // HD
         query = jnp.concatenate(
             [source[:, head * HD : (head + 1) * HD] for head in range(head_count)], axis=0
@@ -63,13 +63,16 @@
             weights.astype(jnp.bfloat16), values, preferred_element_type=jnp.float32
         )
         rows = (weighted / total).astype(jnp.bfloat16)
-        heads += [rows[head * row_count : (head + 1) * row_count] for head in range(head_count)]
-    attended = jnp.concatenate(heads, axis=1)
-    for copy in copies:
-        copy.wait()
-    out_ref[...] = jnp.dot(attended, proj[...], preferred_element_type=jnp.float32).astype(
-        jnp.bfloat16
-    )
+        attended = jnp.concatenate(
+            [rows[head * row_count : (head + 1) * row_count] for head in range(head_count)], axis=1
+        )
+        copies[part].wait()
+        projected += jnp.dot(
+            attended,
+            proj[part * feature_count : (part + 1) * feature_count],
+            preferred_element_type=jnp.float32,
+        )
+    out_ref[...] = projected.astype(jnp.bfloat16)
 
 
 def attend(context_index, own, other, gathered, out_proj, other_proj):

time: 165 us -> 164 us (level)
  transfers between devices with their start and end apart: 10 -> 10, of which waited for: 5 -> 5; matrix products, arithmetic and copies ran while one was open for 3% -> 3% of each run, Pallas kernels for 3% -> 2%
where the time goes in v8:
time: 164 us
  blocking collectives  69.8 us (43%)
  waiting for transfers between devices  42 us (26%)
  starting transfers between devices  20.8 us (13%)
  matrix products  17.5 us (11%)
  Pallas kernels  4.67 us (3%)
  local copies, waits for them, and re-layouts  4.66 us (3%)
  other arithmetic  3.63 us (2%)
    all_to_all x2, blocking collectives, exchange(): lax.all_to_all(rows.reshape(chip_count, slots, width), CHIPS, 0, 0)  69.8 us
    all_to_all x1, waiting for transfers between devices, exchange(): lax.all_to_all(rows.reshape(chip_count, slots, width), CHIPS, 0, 0)  18.5 us
    all_to_all x1, waiting for transfers between devices, local(): lax.all_to_all(projected.reshape(column_size, chip_rows, model_width), CO...  16.9 us
    dot_general x1, matrix products, expert_rows(): jnp.dot(rows, w_in[model_width - rows.shape[1]:], preferred_element_type=...  7.77 us
    all_to_all x1, starting transfers between devices, local(): lax.all_to_all(projected.reshape(column_size, chip_rows, model_width), CO...  7.05 us
    all_to_all x1, starting transfers between devices, local(): gathered = lax.all_to_all(spread, CONTEXT, 0, 0)  5.63 us
    all_to_all x1, starting transfers between devices, exchange(): lax.all_to_all(rows.reshape(chip_count, slots, width), CHIPS, 0, 0)  4.65 us
    all_to_all x1, waiting for transfers between devices, local(): gathered = lax.all_to_all(spread, CONTEXT, 0, 0)  4.32 us
  transfers between devices with their start and end apart: 10, of which 5 were waited for; matrix products, arithmetic and copies ran while one was open for 3% of the time, Pallas kernels for 2%

profile of v8, /device:TPU:1, one launch (start us, length us, event | category | flops | bytes accessed | tf_op | source)
XLA Modules:
  0.0 163.6 jit_solution(5915231244777541922)
XLA Ops:
  0.0 0.9 constant_dynamic-slice_fusion.2
  0.9 0.9 broadcast_in_dim.22
  1.8 1.4 collective-permute-start.2
  3.3 5.6 %all-to-all-start.5 = ((bf16[8,2,128,128]{3,2,1,0:T(8,128)(2,1)}), bf16[8,2,128,128]{3,2,1,0:T(8,128)(2,1)S(1)}, u32[]{:S(2)}, u32[]{:S(2)}) async-start(bf16[8,2,128,128]{3,2,1,0:T(8,128)(2,1)} %broadcast_in_dim.22), calls=%async_computation.5 | async-start | bytes 1048576 | tf_op jit(solution)/shard_map/all_to_all | solution.py:166
  9.9 0.8 dynamic-slice_bitcast_fusion.1.own_ref
  10.8 0.8 constant_dynamic-slice_fusion.1
  14.9 4.3 %all-to-all-done.5.kv_ref = bf16[8,2,128,128]{3,2,1,0:T(8,128)(2,1)S(1)} async-done(((bf16[8,2,128,128]{3,2,1,0:T(8,128)(2,1)}), bf16[8,2,128,128]{3,2,1,0:T(8,128)(2,1)S(1)}, u32[]{:S(2)}, u32[]{:S(2)}) %all-to-all-start.5) | async-done | bytes 524320 | tf_op jit(solution)/shard_map/all_to_all | solution.py:166
  19.2 3.8 %shard_map.100 = bf16[128,4096]{1,0:T(8,128)(2,1)} custom-call(s32[1]{0:T(128)} %bitcast.14.index_ref, bf16[128,256]{1,0:T(8,128)(2,1)S(1)} %dynamic-slice_bitcast_fusion.1.own_ref, bf16[128,256]{1,0:T(8,128)(2,1)S(1)} %dynamic-slice_bitcast_fusion.other_ref, bf16[8,2,128,128]{3,2,1,0:T(8,128)(2,1)S(1)} %all-to-all-done.5.kv_ref, ...), custom_call_target="tpu_custom_call" | custom-call | tf_op jit(solution)/shard_map/pallas_call | solution.py:83
  23.0 7.1 %all-to-all-start.6 = ((bf16[8,16,4096]{2,1,0:T(8,128)(2,1)}), bf16[8,16,4096]{2,1,0:T(8,128)(2,1)S(1)}, u32[]{:S(2)}, u32[]{:S(2)}) async-start(bf16[8,16,4096]{2,1,0:T(8,128)(2,1)} %bitcast.17), calls=%async_computation.6 | async-start | bytes 2097152 | tf_op jit(solution)/shard_map/all_to_all | solution.py:186
  30.5 16.9 %all-to-all-done.6 = bf16[8,16,4096]{2,1,0:T(8,128)(2,1)S(1)} async-done(((bf16[8,16,4096]{2,1,0:T(8,128)(2,1)}), bf16[8,16,4096]{2,1,0:T(8,128)(2,1)S(1)}, u32[]{:S(2)}, u32[]{:S(2)}) %all-to-all-start.6) | async-done | bytes 1048608 | tf_op jit(solution)/shard_map/all_to_all | solution.py:186
  47.8 0.9 collective-permute-start.3
  48.9 0.9 collective-permute-done.3
  49.8 111.7 %conditional.1 = ((f32[16,4096]{1,0:T(8,128)S(1)}, bf16[16,4096]{1,0:T(8,128)(2,1)S(1)})) conditional(s32[]{:T(128)} %convert_element_type.98, (s32[]{:T(128)}, bf16[32,4096]{1,0:T(8,128)(2,1)S(1)}, bf16[512,32]{1,0:T(8,128)(2,1)S(1)}, bf16[4096,1536]{1,0:T(8,128)(2,1)}, bf16[768,4096]{1,0:T(8,128)(2,1)}, /*index=5*/bf16[64,512]{1,0:T(8,128)(2,1)S(1)}, ...), branch_computations={%region_6.7_spmd, %region_7.8_spmd} | conditional | flops 9806807040 | bytes 124026968 | solution.py:264
  49.8 1.4 fusion.14
  51.2 4.7 %all-to-all-start = ((bf16[64,8,1024]{2,1,0:T(8,128)(2,1)}), bf16[64,8,1024]{2,1,0:T(8,128)(2,1)S(1)}, u32[]{:S(2)}, u32[]{:S(2)}) async-start(bf16[64,8,1024]{2,1,0:T(8,128)(2,1)} %fusion.14), calls=%async_computation | async-start | bytes 2097152 | tf_op jit(solution)/shard_map/cond/branch_0_fun/all_to_all | solution.py:241
  55.9 18.5 %all-to-all-done = bf16[64,8,1024]{2,1,0:T(8,128)(2,1)S(1)} async-done(((bf16[64,8,1024]{2,1,0:T(8,128)(2,1)}), bf16[64,8,1024]{2,1,0:T(8,128)(2,1)S(1)}, u32[]{:S(2)}, u32[]{:S(2)}) %all-to-all-start) | async-done | bytes 1048608 | tf_op jit(solution)/shard_map/cond/branch_0_fun/all_to_all | solution.py:241
  74.4 3.7 %fusion.10 = bf16[512,1536]{1,0:T(8,128)(2,1)S(1)} fusion(bf16[4096,1536]{1,0:T(8,128)(2,1)} %get-tuple-element.37, bf16[64,8,1024]{2,1,0:T(8,128)(2,1)S(1)} %all-to-all-done), kind=kOutput, calls=%fused_computation.10 | convolution fusion | flops 1611399168 | bytes 5767168 | tf_op jit(solution)/shard_map/cond/branch_0_fun/dot_general | solution.py:256
  78.1 1.0 fusion.3
  79.1 30.3 %all_to_all.30 = bf16[64,8,3072]{2,1,0:T(8,128)(2,1)S(1)} all-to-all(bf16[64,8,3072]{2,1,0:T(8,128)(2,1)S(1)} %fusion.3), channel_id=1, replica_groups=mesh['zl'=2,'y'=4,'zh'=2,'x'=4,'core'=2] {'zl','y','zh','x'}, dimensions={0} | all-to-all | bytes 6291456 | tf_op jit(solution)/shard_map/cond/branch_0_fun/all_to_all | solution.py:241
  109.4 7.8 %fusion.4 = f32[512,1536]{1,0:T(8,128)S(1)} fusion(bf16[4096,1536]{1,0:T(8,128)(2,1)} %get-tuple-element.37, bf16[64,8,3072]{2,1,0:T(8,128)(2,1)S(1)} %all_to_all.30, bf16[512,1536]{1,0:T(8,128)(2,1)S(1)} %fusion.10), kind=kOutput, calls=%fused_computation.6 | convolution fusion | flops 4833411072 | bytes 17301504 | tf_op jit(solution)/shard_map/cond/branch_0_fun/dot_general | solution.py:98
  117.2 3.7 %fusion.2 = bf16[64,8,4096]{2,1,0:T(8,128)(2,1)S(1)} fusion(bf16[768,4096]{1,0:T(8,128)(2,1)S(1)} %bitcast.109, f32[512,1536]{1,0:T(8,128)S(1)} %fusion.4), kind=kOutput, calls=%fused_computation.3 | convolution fusion | flops 3225681920 | bytes 13631488 | tf_op jit(solution)/shard_map/cond/branch_0_fun/dot_general | solution.py:104
  120.9 39.6 %all_to_all.31 = bf16[64,8,4096]{2,1,0:T(8,128)(2,1)S(1)} all-to-all(bf16[64,8,4096]{2,1,0:T(8,128)(2,1)S(1)} %fusion.2), channel_id=1, replica_groups=mesh['zl'=2,'y'=4,'zh'=2,'x'=4,'core'=2] {'zl','y','zh','x'}, dimensions={0} | all-to-all | bytes 8388608 | tf_op jit(solution)/shard_map/cond/branch_0_fun/all_to_all | solution.py:241
  160.5 0.8 branch_0_fun.1
  161.6 1.3 collective-permute-done.6
  (59 shorter events, 5.9 us)
Async XLA Ops:
  0.0 19.2 %copy-start = (bf16[256,4096]{1,0:T(8,128)(2,1)S(1)}, bf16[256,4096]{1,0:T(8,128)(2,1)}, u32[]{:S(2)}) copy-start(bf16[256,4096]{1,0:T(8,128)(2,1)} %proj_ref) | copy-start | bytes 6291460
  1.8 17.3 %collective-permute-start.2 = (bf16[256,4096]{1,0:T(8,128)(2,1)}, bf16[256,4096]{1,0:T(8,128)(2,1)}, u32[]{:S(2)}, u32[]{:S(2)}) collective-permute-start(bf16[256,4096]{1,0:T(8,128)(2,1)} %proj_ref), channel_id=1, source_target_pairs={{0,1},{1,0},{2,3},{3,2},{4,5},{5,4},{6,7},{7,6},{8,9},{9,8},{10,11... | collective-permute-start | bytes 6291464 | tf_op jit(solution)/shard_map/ppermute | solution.py:21
  3.3 15.9 %all-to-all-start.5 = ((bf16[8,2,128,128]{3,2,1,0:T(8,128)(2,1)}), bf16[8,2,128,128]{3,2,1,0:T(8,128)(2,1)S(1)}, u32[]{:S(2)}, u32[]{:S(2)}) async-start(bf16[8,2,128,128]{3,2,1,0:T(8,128)(2,1)} %broadcast_in_dim.22), calls=%async_computation.5 | async-start | bytes 1048576 | tf_op jit(solution)/shard_map/all_to_all | solution.py:166
  8.9 2.9 %collective-permute-start.4 = (s32[2,8,8]{2,1,0:T(8,128)}, s32[2,8,8]{2,1,0:T(8,128)S(1)}, u32[]{:S(2)}, u32[]{:S(2)}) collective-permute-start(s32[2,8,8]{2,1,0:T(8,128)} %param.20), channel_id=1, source_target_pairs={{0,1},{1,0},{2,3},{3,2},{4,5},{5,4},{6,7},{7,6},{8,9},{9,8},{10,11... | collective-permute-start | bytes 1544 | tf_op jit(solution)/shard_map/ppermute | solution.py:21
  9.2 4.3 %collective-permute-start.5 = (f32[2,8,8]{2,1,0:T(8,128)}, f32[2,8,8]{2,1,0:T(8,128)S(1)}, u32[]{:S(2)}, u32[]{:S(2)}) collective-permute-start(f32[2,8,8]{2,1,0:T(8,128)} %param.21), channel_id=1, source_target_pairs={{0,1},{1,0},{2,3},{3,2},{4,5},{5,4},{6,7},{7,6},{8,9},{9,8},{10,11... | collective-permute-start | bytes 1544 | tf_op jit(solution)/shard_map/ppermute | solution.py:21
  9.4 21.0 %collective-permute-start = (bf16[2,8,4096]{2,1,0:T(8,128)(2,1)}, bf16[2,8,4096]{2,1,0:T(8,128)(2,1)S(1)}, u32[]{:S(2)}, u32[]{:S(2)}) collective-permute-start(bf16[2,8,4096]{2,1,0:T(8,128)(2,1)} %param.16), channel_id=1, source_target_pairs={{0,1},{1,0},{2,3},{3,2},{4,5},{5,4},{6,7},{7,6},{8,9},{9,8},{10,11... | collective-permute-start | bytes 393224 | tf_op jit(solution)/shard_map/ppermute | solution.py:21
  9.7 5.1 %collective-permute-start.1 = (bf16[2,128,256]{2,1,0:T(8,128)(2,1)}, bf16[2,128,256]{2,1,0:T(8,128)(2,1)S(1)}, u32[]{:S(2)}, u32[]{:S(2)}) collective-permute-start(bf16[2,128,256]{2,1,0:T(8,128)(2,1)} %param.12), channel_id=1, source_target_pairs={{0,1},{1,0},{2,3},{3,2},{4,5},{5,4},{6,7},{7,6},{8,9},{9,8},{10,11... | collective-permute-start | bytes 393224 | tf_op jit(solution)/shard_map/ppermute | solution.py:21
  23.0 24.7 %copy-start.1 = (f32[4096]{0:T(1024)S(1)}, f32[4096]{0:T(1024)}, u32[]{:S(2)}) copy-start(f32[4096]{0:T(1024)} %param.17) | copy-start | bytes 49156
  23.0 24.4 %all-to-all-start.6 = ((bf16[8,16,4096]{2,1,0:T(8,128)(2,1)}), bf16[8,16,4096]{2,1,0:T(8,128)(2,1)S(1)}, u32[]{:S(2)}, u32[]{:S(2)}) async-start(bf16[8,16,4096]{2,1,0:T(8,128)(2,1)} %bitcast.17), calls=%async_computation.6 | async-start | bytes 2097152 | tf_op jit(solution)/shard_map/all_to_all | solution.py:186
  47.8 1.9 %collective-permute-start.3 = (bf16[16,4096]{1,0:T(8,128)(2,1)S(1)}, bf16[16,4096]{1,0:T(8,128)(2,1)S(1)}, u32[]{:S(2)}, u32[]{:S(2)}) collective-permute-start(bf16[16,4096]{1,0:T(8,128)(2,1)S(1)} %multiply_convert_fusion), channel_id=1, source_target_pairs={{0,1},{1,0},{2,3},{3,2},{4,5},{5,4},{6,7},{7,6},{8,9},{9,8},{10,11... | collective-permute-start | bytes 393224 | tf_op jit(solution)/shard_map/ppermute | solution.py:21
  51.2 23.2 %all-to-all-start = ((bf16[64,8,1024]{2,1,0:T(8,128)(2,1)}), bf16[64,8,1024]{2,1,0:T(8,128)(2,1)S(1)}, u32[]{:S(2)}, u32[]{:S(2)}) async-start(bf16[64,8,1024]{2,1,0:T(8,128)(2,1)} %fusion.14), calls=%async_computation | async-start | bytes 2097152 | tf_op jit(solution)/shard_map/cond/branch_0_fun/all_to_all | solution.py:241
  79.1 38.1 %slice-start = ((s8[6291456]{0:T(1024)(128)(4,1)}), s8[4194304]{0:T(1024)(128)(4,1)S(1)}, s32[]{:S(2)}) async-start(s8[6291456]{0:T(1024)(128)(4,1)} %bitcast.108), calls=%async_computation.7 | async-start | bytes 8388608 | tf_op jit(solution)/shard_map/cond
  109.4 7.8 %slice-start.1 = ((s8[6291456]{0:T(1024)(128)(4,1)}), s8[2097152]{0:T(1024)(128)(4,1)S(1)}, s32[]{:S(2)}) async-start(s8[6291456]{0:T(1024)(128)(4,1)} %bitcast.108), calls=%async_computation.8 | async-start | bytes 4194304 | tf_op jit(solution)/shard_map/cond
  161.5 1.4 collective-permute-start.6
